TPU v7x, 128 devices: a whole 4x4x4 slice. The times are simulated.
128 devices in a mesh: section: 2 (over core), dp: 64 (over y, z, x).
Axes of the slice: x: 4, y: 4, z: 4, core: 2. Of those that a mesh axis runs over, the one named last changes fastest.
Arguments:
- inputs: bfloat16 [2, 8192, 512], P(None, 'dp'), may hold values from -6 to 6
- groups: int32 [2, 8192], P(None, 'dp'), may hold values from 0 to 3, as said below
- cotangent: bfloat16 [2, 8192, 512], P(None, 'dp'), may hold values from -6 to 6
- w_query: bfloat16 [512, 512], replicated, may hold values from -0.25 to 0.25
- w_key: bfloat16 [512, 512], replicated, may hold values from -0.25 to 0.25
- w_value: bfloat16 [512, 512], replicated, may hold values from -0.25 to 0.25
- w_out: bfloat16 [512, 512], replicated, may hold values from -1 to 1
- w_up: bfloat16 [512, 2048], replicated, may hold values from -0.25 to 0.25
- w_down: bfloat16 [2048, 512], replicated, may hold values from -0.125 to 0.125
- gain_one: float32 [512], replicated, may hold values from 0.5 to 1.5
- shift_one: float32 [512], replicated, may hold values from -3 to 3
- gain_two: float32 [512], replicated, may hold values from 0.5 to 1.5
- shift_two: float32 [512], replicated, may hold values from -3 to 3
Outputs:
- output: bfloat16 [2, 8192, 512], P('section', 'dp')
- input_grad: bfloat16 [2, 8192, 512], P('section', 'dp')
- w_query_grad: float32 [512, 512], replicated
- w_key_grad: float32 [512, 512], replicated
- w_value_grad: float32 [512, 512], replicated
- w_out_grad: float32 [512, 512], replicated
- w_up_grad: float32 [512, 2048], replicated
- w_down_grad: float32 [2048, 512], replicated
- gain_one_grad: float32 [512], replicated
- shift_one_grad: float32 [512], replicated
- gain_two_grad: float32 [512], replicated
- shift_two_grad: float32 [512], replicated
Inputs may be any that keep to these rules, and one draw needn't show every extreme that they name: Group ids come in runs of consecutive tokens; every one of the 4 groups occurs in every stream, and the first and the last token of a stream belong to the same group.
All inputs are finite; a program needn't handle non-finite values.
Results may differ from a plain program's by a relative error of at most 0.035.
Values may be sent and summed in bfloat16 or wider, within the bound.
A program may use at most 256 MiB of HBM per device.

v0:
```python
from functools import partial

import jax
import jax.numpy as jnp
from jax import lax
from jax.sharding import PartitionSpec as P

HEADS = 8
HEAD = 64


NEG_FILL = -1e30


def passed_along(value, axis, steps):
    count = lax.axis_size(axis)
    leading, last = (max(0, -steps), min(count, count - steps))
    return lax.ppermute(value, axis, [(source, source + steps) for source in range(leading, last)])


def partner(value, axis, bit):
    return lax.ppermute(value, axis, [(i, i ^ 1 << bit) for i in range(lax.axis_size(axis))])


def dot_plain(left, right):
    return jnp.dot(left, right, preferred_element_type=jnp.float32)


def dot_left(left, right):
    return lax.dot_general(
        left, right, (((0,), (0,)), ((), ())), preferred_element_type=jnp.float32
    )


def dot_right(left, right):
    return lax.dot_general(
        left, right, (((1,), (1,)), ((), ())), preferred_element_type=jnp.float32
    )


def gelu_tanh(values_in):
    return jax.nn.gelu(values_in, approximate=True)


def select_by(flag, early_val, later_val):
    return jnp.where(flag, early_val, later_val)


def layer_norm(values_in, gain_vec, shift_vec):
    centred = values_in - jnp.mean(values_in, axis=-1, keepdims=True)
    factor = lax.rsqrt(jnp.mean(centred * centred, axis=-1, keepdims=True) + 1e-05)
    normed = centred * factor
    return (normed * gain_vec + shift_vec, (normed, factor))


def norm_back(upstream, stored, gain_vec):
    normed, factor = stored
    scaled = upstream * gain_vec
    centred_grad = (
        scaled
        - jnp.mean(scaled, axis=-1, keepdims=True)
        - normed * jnp.mean(scaled * normed, axis=-1, keepdims=True)
    )
    return (centred_grad * factor, jnp.sum(upstream * normed, axis=0), jnp.sum(upstream, axis=0))


def mask_for(query_pos, query_grp, key_pos, key_grp):
    return (key_pos[None, :] <= query_pos[:, None]) & (key_grp[None, :] == query_grp[:, None])


def score_grads(
    query_blk,
    grad_blk,
    total_blk,
    delta_blk,
    query_pos,
    query_grp,
    key_blk,
    value_blk,
    key_pos,
    key_grp,
):
    factor = HEAD ** (-0.5)
    allowed = mask_for(query_pos, query_grp, key_pos, key_grp)[None]
    scores = (
        jnp.einsum("thd,shd->hts", query_blk, key_blk, preferred_element_type=jnp.float32) * factor
    )
    scores = jnp.where(allowed, scores, NEG_FILL)
    probs = jnp.where(allowed, jnp.exp(scores - total_blk[..., None]), 0.0)
    grad_probs = jnp.einsum("thd,shd->hts", grad_blk, value_blk, preferred_element_type=jnp.float32)
    grad_scores = (factor * probs * (grad_probs - delta_blk[..., None])).astype(jnp.bfloat16)
    return (probs.astype(jnp.bfloat16), grad_scores)


def forward_visit(hidden, local_grp, whole_grp, params):
    w_query, w_key, w_value, w_out, w_up, w_down, gain_one, shift_one, gain_two, shift_two = params
    row_count = hidden.shape[0]
    factor = HEAD ** (-0.5)
    queries = dot_plain(hidden, w_query).astype(jnp.bfloat16).reshape(row_count, HEADS, HEAD)
    keys_loc = dot_plain(hidden, w_key).astype(jnp.bfloat16).reshape(row_count, HEADS, HEAD)
    values_loc = dot_plain(hidden, w_value).astype(jnp.bfloat16).reshape(row_count, HEADS, HEAD)
    query_pos = lax.axis_index("dp") * row_count + jnp.arange(row_count, dtype=jnp.int32)
    run_max = jnp.full((HEADS, row_count), NEG_FILL, jnp.float32)
    run_acc = jnp.zeros((row_count, HEADS, HEAD), jnp.float32)
    key_piece = lax.all_gather(keys_loc, "dp", axis=0, tiled=True)
    value_piece = lax.all_gather(values_loc, "dp", axis=0, tiled=True)
    piece_rows = key_piece.shape[0]
    key_pos = jnp.arange(piece_rows, dtype=jnp.int32)
    allowed = mask_for(query_pos, local_grp, key_pos, whole_grp)[None]
    scores = (
        jnp.einsum("thd,shd->hts", queries, key_piece, preferred_element_type=jnp.float32) * factor
    )
    scores = jnp.where(allowed, scores, NEG_FILL)
    new_max = jnp.maximum(run_max, jnp.max(scores, axis=-1))
    rescale = jnp.exp(run_max - new_max)
    weights = jnp.where(allowed, jnp.exp(scores - new_max[..., None]), 0.0)
    new_sum = jnp.sum(weights, axis=-1)
    new_acc = run_acc * rescale.T[:, :, None] + jnp.einsum(
        "hts,shd->thd",
        weights.astype(jnp.bfloat16),
        value_piece,
        preferred_element_type=jnp.float32,
    )
    attended = new_acc / new_sum.T[:, :, None]
    log_total = new_max + jnp.log(new_sum)
    attended_low = attended.reshape(row_count, HEADS * HEAD).astype(jnp.bfloat16)
    first, norm_one = layer_norm(
        hidden.astype(jnp.float32) + dot_plain(attended_low, w_out), gain_one, shift_one
    )
    first_low = first.astype(jnp.bfloat16)
    pre_act = dot_plain(first_low, w_up)
    act_low = gelu_tanh(pre_act).astype(jnp.bfloat16)
    result, norm_two = layer_norm(first + dot_plain(act_low, w_down), gain_two, shift_two)
    stored = (
        hidden,
        queries,
        keys_loc,
        values_loc,
        attended,
        attended_low,
        log_total,
        norm_one,
        first_low,
        pre_act,
        act_low,
        norm_two,
    )
    return (result, stored)


def attention_back(
    queries, keys_loc, values_loc, attended, log_total, grad_att, local_grp, whole_grp
):
    row_count = queries.shape[0]
    total_rows = whole_grp.shape[0]
    span = min(512, total_rows)
    block_count = total_rows // span
    my_pos = lax.axis_index("dp") * row_count + jnp.arange(row_count, dtype=jnp.int32)
    delta = jnp.einsum("thd,thd->ht", grad_att.astype(jnp.float32), attended)
    keys_all, values_all = (
        lax.all_gather(keys_loc, "dp", axis=0, tiled=True),
        lax.all_gather(values_loc, "dp", axis=0, tiled=True),
    )
    zero_query = jnp.zeros((row_count, HEADS, HEAD), jnp.float32)

    def query_only(grad_query, block_index):
        begin = block_index * span
        key_blk = lax.dynamic_slice_in_dim(keys_all, begin, span, 0)
        value_blk = lax.dynamic_slice_in_dim(values_all, begin, span, 0)
        key_grp = lax.dynamic_slice_in_dim(whole_grp, begin, span, 0)
        key_pos = begin + jnp.arange(span, dtype=jnp.int32)
        probs_low, grad_scores = score_grads(
            queries,
            grad_att,
            log_total,
            delta,
            my_pos,
            local_grp,
            key_blk,
            value_blk,
            key_pos,
            key_grp,
        )
        return (
            grad_query
            + jnp.einsum("hts,shd->thd", grad_scores, key_blk, preferred_element_type=jnp.float32),
            None,
        )

    grad_query, unused_out = lax.scan(
        query_only, zero_query, jnp.arange(block_count, dtype=jnp.int32)
    )
    queries_all, grads_all = (
        lax.all_gather(queries, "dp", axis=0, tiled=True),
        lax.all_gather(grad_att, "dp", axis=0, tiled=True),
    )
    totals_all, deltas_all = (
        lax.all_gather(log_total, "dp", axis=1, tiled=True),
        lax.all_gather(delta, "dp", axis=1, tiled=True),
    )

    def over_queries(running, block_index):
        grad_key_acc, grad_value_acc = running
        begin = block_index * span
        query_blk = lax.dynamic_slice_in_dim(queries_all, begin, span, 0)
        grad_blk = lax.dynamic_slice_in_dim(grads_all, begin, span, 0)
        total_blk = lax.dynamic_slice_in_dim(totals_all, begin, span, 1)
        delta_blk = lax.dynamic_slice_in_dim(deltas_all, begin, span, 1)
        query_grp = lax.dynamic_slice_in_dim(whole_grp, begin, span, 0)
        query_pos = begin + jnp.arange(span, dtype=jnp.int32)
        probs_low, grad_scores = score_grads(
            query_blk,
            grad_blk,
            total_blk,
            delta_blk,
            query_pos,
            query_grp,
            keys_loc,
            values_loc,
            my_pos,
            local_grp,
        )
        grad_key_acc = grad_key_acc + jnp.einsum(
            "hts,thd->shd", grad_scores, query_blk, preferred_element_type=jnp.float32
        )
        grad_value_acc = grad_value_acc + jnp.einsum(
            "hts,thd->shd", probs_low, grad_blk, preferred_element_type=jnp.float32
        )
        return ((grad_key_acc, grad_value_acc), None)

    key_value_acc, unused_tail = lax.scan(
        over_queries, (zero_query, zero_query), jnp.arange(block_count, dtype=jnp.int32)
    )
    grad_key, grad_value = key_value_acc
    width = HEADS * HEAD
    return (
        grad_query.astype(jnp.bfloat16).reshape(row_count, width),
        grad_key.astype(jnp.bfloat16).reshape(row_count, width),
        grad_value.astype(jnp.bfloat16).reshape(row_count, width),
    )


def backward_visit(upstream, stored, local_grp, whole_grp, params):
    w_query, w_key, w_value, w_out, w_up, w_down, gain_one, shift_one, gain_two, shift_two = params
    (
        hidden,
        queries,
        keys_loc,
        values_loc,
        attended,
        attended_low,
        log_total,
        norm_one,
        first_low,
        pre_act,
        act_low,
        norm_two,
    ) = stored
    row_count = hidden.shape[0]
    grad_two, gain_two_grad, shift_two_grad = norm_back(upstream, norm_two, gain_two)
    down_low = grad_two.astype(jnp.bfloat16)
    w_down_grad = dot_left(act_low, down_low)
    unused_act, gelu_pull = jax.vjp(gelu_tanh, pre_act)
    up_low = gelu_pull(dot_right(down_low, w_down))[0].astype(jnp.bfloat16)
    w_up_grad = dot_left(first_low, up_low)
    grad_one, gain_one_grad, shift_one_grad = norm_back(
        grad_two + dot_right(up_low, w_up), norm_one, gain_one
    )
    out_low = grad_one.astype(jnp.bfloat16)
    w_out_grad = dot_left(attended_low, out_low)
    grad_att = dot_right(out_low, w_out).astype(jnp.bfloat16).reshape(row_count, HEADS, HEAD)
    grad_query, grad_key, grad_value = attention_back(
        queries, keys_loc, values_loc, attended, log_total, grad_att, local_grp, whole_grp
    )
    grad_hidden = (
        grad_one
        + dot_right(grad_query, w_query)
        + dot_right(grad_key, w_key)
        + dot_right(grad_value, w_value)
    )
    grads = (
        dot_left(hidden, grad_query),
        dot_left(hidden, grad_key),
        dot_left(hidden, grad_value),
        w_out_grad,
        w_up_grad,
        w_down_grad,
        gain_one_grad,
        shift_one_grad,
        gain_two_grad,
        shift_two_grad,
    )
    return (grad_hidden, grads)


def on_device(
    inputs,
    groups,
    cotangent,
    w_query,
    w_key,
    w_value,
    w_out,
    w_up,
    w_down,
    gain_one,
    shift_one,
    gain_two,
    shift_two,
):
    params = (
        w_query,
        w_key,
        w_value,
        w_out,
        w_up,
        w_down,
        gain_one,
        shift_one,
        gain_two,
        shift_two,
    )
    micro = inputs.shape[0]
    leading = lax.axis_index("section") == 0
    whole_groups = lax.all_gather(groups, "dp", axis=1, tiled=True)
    received = jnp.zeros(inputs.shape[1:], jnp.bfloat16)
    saved = []
    outputs_seen = []
    for step in range(micro + 1):
        ahead = min(step, micro - 1)
        behind = max(step - 1, 0)
        hidden = jnp.where(leading, inputs[ahead], received)
        local_grp = jnp.where(leading, groups[ahead], groups[behind])
        whole_grp = jnp.where(leading, whole_groups[ahead], whole_groups[behind])
        result, stored = forward_visit(hidden, local_grp, whole_grp, params)
        saved.append((stored, local_grp, whole_grp))
        outputs_seen.append(result)
        if step < micro:
            received = passed_along(result.astype(jnp.bfloat16), "section", 1)
    incoming = jnp.zeros(inputs.shape[1:], jnp.bfloat16)
    grad_sums = None
    input_grads = []
    for step in range(micro + 1):
        chosen = jax.tree.map(
            partial(select_by, leading), saved[max(step - 1, 0)], saved[min(step + 1, micro)]
        )
        stored, local_grp, whole_grp = chosen
        live = jnp.where(leading, step >= 1, step < micro)
        upstream = jnp.where(
            leading,
            incoming.astype(jnp.float32),
            cotangent[min(step, micro - 1)].astype(jnp.float32),
        )
        upstream = jnp.where(live, upstream, 0.0)
        grad_hidden, grads = backward_visit(upstream, stored, local_grp, whole_grp, params)
        if grad_sums is None:
            grad_sums = grads
        else:
            grad_sums = jax.tree.map(jnp.add, grad_sums, grads)
        input_grads.append(grad_hidden)
        if step < micro:
            incoming = passed_along(grad_hidden.astype(jnp.bfloat16), "section", -1)
    (
        sum_query,
        sum_key,
        sum_value,
        sum_out,
        sum_up,
        sum_down,
        sum_gain_one,
        sum_shift_one,
        sum_gain_two,
        sum_shift_two,
    ) = grad_sums
    totals = lax.psum(
        (
            sum_query,
            sum_key,
            sum_value,
            sum_out,
            sum_up,
            sum_down,
            sum_gain_one,
            sum_shift_one,
            sum_gain_two,
            sum_shift_two,
        ),
        ("section", "dp"),
    )
    half_count = micro // 2
    produced = jnp.stack(outputs_seen[1:]).astype(jnp.bfloat16)
    input_grad = jnp.stack(input_grads[1:]).astype(jnp.bfloat16)
    outgoing = jnp.where(leading, input_grad[half_count:], produced[:half_count])
    arrived = partner(outgoing, "section", 0)
    output_part = jnp.where(leading, arrived, produced[half_count:])
    grad_part = jnp.where(leading, input_grad[:half_count], arrived)
    return (
        output_part,
        grad_part,
        totals[0],
        totals[1],
        totals[2],
        totals[3],
        totals[4],
        totals[5],
        totals[6],
        totals[7],
        totals[8],
        totals[9],
    )


def solution(mesh):
    placed = (
        P(None, "dp", None),
        P(None, "dp"),
        P(None, "dp", None),
        P(),
        P(),
        P(),
        P(),
        P(),
        P(),
        P(),
        P(),
        P(),
        P(),
    )
    return jax.shard_map(
        on_device,
        mesh=mesh,
        in_specs=placed,
        out_specs=(
            P("section", "dp", None),
            P("section", "dp", None),
            P(),
            P(),
            P(),
            P(),
            P(),
            P(),
            P(),
            P(),
            P(),
            P(),
        ),
        check_vma=False,
    )
```

profile of v0, /device:TPU:1, one launch (start us, length us, event | category | flops | bytes accessed | tf_op | source)
XLA Modules:
  0.0 3297.7 jit_solution(11274999025486118190)
XLA Ops:
  13.2 151.5 %all_gather.75 = s32[2,8192]{1,0:T(2,128)S(1)} all-gather(s32[2,128]{1,0:T(2,128)} %param.26), channel_id=1, replica_groups=mesh['section'=2,'dp'=64] {'dp'}, dimensions={1}, use_global_device_ids=true | all-gather | bytes 66560 | tf_op jit(solution)/shard_map/all_gather | solution.py:325
  171.0 16.2 fusion.156
  187.2 16.3 fusion.159
  203.5 9.7 all-gather.21.cloned.1.call-done
  213.2 17.9 fusion.353
  236.7 19.1 collective-permute-done
  265.5 84.3 %all-gather.23.cloned.1.call-done = bf16[8192,8,64]{0,2,1:T(8,128)(2,1)} async-done(((bf16[128,8,64]{0,2,1:T(8,128)(2,1)}), bf16[8192,8,64]{0,2,1:T(8,128)(2,1)}) %all-gather.23.cloned.1.call-update) | async-done | bytes 8388624 | tf_op jit(solution)/shard_map/all_gather | solution.py:105
  349.9 16.4 fusion.157
  368.0 16.6 fusion.161
  384.6 65.5 %all-gather.25.cloned.1.call-done = bf16[8192,8,64]{0,2,1:T(8,128)(2,1)} async-done(((bf16[128,8,64]{0,2,1:T(8,128)(2,1)}), bf16[8192,8,64]{0,2,1:T(8,128)(2,1)}) %all-gather.25.cloned.1.call-update) | async-done | bytes 8388624 | tf_op jit(solution)/shard_map/all_gather | solution.py:106
  450.1 18.0 fusion.356
  498.9 78.0 %all-gather.35.cloned.1.call-done = bf16[8192,8,64]{0,2,1:T(8,128)(2,1)} async-done(((bf16[128,8,64]{0,2,1:T(8,128)(2,1)}), bf16[8192,8,64]{0,2,1:T(8,128)(2,1)}) %all-gather.35.cloned.1.call-update) | async-done | bytes 8388624 | tf_op jit(solution)/shard_map/all_gather | solution.py:105
  576.9 16.4 fusion.158
  593.3 16.0 fusion.163
  610.5 66.7 %all-gather.37.cloned.1.call-done = bf16[8192,8,64]{0,2,1:T(8,128)(2,1)} async-done(((bf16[128,8,64]{0,2,1:T(8,128)(2,1)}), bf16[8192,8,64]{0,2,1:T(8,128)(2,1)}) %all-gather.37.cloned.1.call-update) | async-done | bytes 8388624 | tf_op jit(solution)/shard_map/all_gather | solution.py:106
  677.3 18.2 fusion.358
  710.7 158.8 %all_gather.83 = f32[8,8192]{1,0:T(8,128)} all-gather(f32[8,128]{1,0:T(8,128)S(1)} %copy-done.122), channel_id=1, replica_groups=mesh['section'=2,'dp'=64] {'dp'}, dimensions={1}, use_global_device_ids=true | all-gather | bytes 266240 | tf_op jit(solution)/shard_map/all_gather | solution.py:198
  870.6 154.5 %all_gather.85 = f32[8,8192]{1,0:T(8,128)} all-gather(f32[8,128]{1,0:T(8,128)S(1)} %fusion.268), channel_id=1, replica_groups=mesh['section'=2,'dp'=64] {'dp'}, dimensions={1}, use_global_device_ids=true | all-gather | bytes 266240 | tf_op jit(solution)/shard_map/all_gather | solution.py:199
  1025.7 173.1 %while.72 = (s32[]{:T(128)}, f32[128,8,64]{0,2,1:T(8,128)}, s32[16]{0:T(128)}, bf16[8192,8,64]{0,2,1:T(8,128)(2,1)}, s32[8192]{0:T(1024)}, /*index=5*/s32[128]{0...) while((s32[]{:T(128)}, f32[128,8,64]{0,2,1:T(8,128)}, ...), condition=%wide.region_17.18_spmd.clone, body=%wide.region_16.17_spmd.clone.sunk | while | flops 205849216 | bytes 6968560 | solution.py:190
  1043.3 3.9 fusion.520
  1054.2 4.0 fusion.520
  1140.7 4.1 fusion.520
  1173.2 3.9 fusion.520
  1206.8 228.3 %while.73 = (s32[]{:T(128)}, f32[128,8,64]{0,2,1:T(8,128)}, f32[128,8,64]{0,2,1:T(8,128)}, s32[16]{0:T(128)}, bf16[8192,8,64]{0,2,1:T(8,128)(2,1)}, /*index=5*/s...) while((s32[]{:T(128)}, f32[128,8,64]{0,2,1:T(8,128)}, ...), condition=%wide.region_19.20_spmd.clone, body=%wide.region_18.19_spmd.clone.sunk | while | flops 273613440 | bytes 10073345 | solution.py:231
  1242.9 4.0 fusion.528
  1257.3 4.0 fusion.528
  1271.6 3.9 fusion.528
  1314.3 4.0 fusion.528
  1342.9 4.0 fusion.528
  1357.3 4.0 fusion.528
  1371.6 4.0 fusion.528
  1440.2 59.0 %collective-permute-start.1 = (bf16[128,512]{1,0:T(8,128)(2,1)S(1)}, bf16[128,512]{1,0:T(8,128)(2,1)S(1)}, u32[]{:S(2)}, u32[]{:S(2)}) collective-permute-start(bf16[128,512]{1,0:T(8,128)(2,1)S(1)} %fusion.198), channel_id=1, source_target_pairs={{64,0},{65,1},{66,2},{67,3},{68,4},{69,5},{70,6},{71,7},{72,8},{73... | collective-permute-start | bytes 393224 | tf_op jit(solution)/shard_map/ppermute | solution.py:18
  1514.4 4.2 fusion.293
  1532.9 156.1 %all_gather.91 = f32[8,8192]{1,0:T(8,128)} all-gather(f32[8,128]{1,0:T(8,128)} %get-tuple-element.1669), channel_id=1, replica_groups=mesh['section'=2,'dp'=64] {'dp'}, dimensions={1}, use_global_device_ids=true | all-gather | bytes 266240 | tf_op jit(solution)/shard_map/all_gather | solution.py:198
  1689.0 155.2 %all_gather.97 = f32[8,8192]{1,0:T(8,128)} all-gather(f32[8,128]{1,0:T(8,128)} %get-tuple-element.1768), channel_id=1, replica_groups=mesh['section'=2,'dp'=64] {'dp'}, dimensions={1}, use_global_device_ids=true | all-gather | bytes 266240 | tf_op jit(solution)/shard_map/all_gather | solution.py:198
  1848.3 4.1 fusion.291
  1855.5 154.3 %all_gather.93 = f32[8,8192]{1,0:T(8,128)} all-gather(f32[8,128]{1,0:T(8,128)S(1)} %fusion.267), channel_id=1, replica_groups=mesh['section'=2,'dp'=64] {'dp'}, dimensions={1}, use_global_device_ids=true | all-gather | bytes 266240 | tf_op jit(solution)/shard_map/all_gather | solution.py:199
  2009.9 161.8 %while.74 = (s32[]{:T(128)}, f32[128,8,64]{0,2,1:T(8,128)}, s32[16]{0:T(128)S(1)}, bf16[8192,8,64]{0,2,1:T(8,128)(2,1)}, s32[8192]{0:T(1024)}, /*index=5*/s32[12...) while((s32[]{:T(128)}, f32[128,8,64]{0,2,1:T(8,128)}, ...), condition=%wide.region_31.32_spmd.clone, body=%wide.region_30.31_spmd.clone.sunk | while | flops 205849216 | bytes 6837488 | solution.py:190
  2179.2 227.0 %while.75 = (s32[]{:T(128)}, f32[128,8,64]{0,2,1:T(8,128)}, f32[128,8,64]{0,2,1:T(8,128)}, s32[16]{0:T(128)}, bf16[8192,8,64]{0,2,1:T(8,128)(2,1)}, /*index=5*/s...) while((s32[]{:T(128)}, f32[128,8,64]{0,2,1:T(8,128)}, ...), condition=%wide.region_33.34_spmd.clone, body=%wide.region_32.33_spmd.clone.sunk | while | flops 273613440 | bytes 9942273 | solution.py:231
  2411.4 84.4 %collective-permute-start.3 = (bf16[128,512]{1,0:T(8,128)(2,1)S(1)}, bf16[128,512]{1,0:T(8,128)(2,1)S(1)}, u32[]{:S(2)}, u32[]{:S(2)}) collective-permute-start(bf16[128,512]{1,0:T(8,128)(2,1)S(1)} %fusion.199), channel_id=1, source_target_pairs={{64,0},{65,1},{66,2},{67,3},{68,4},{69,5},{70,6},{71,7},{72,8},{73... | collective-permute-start | bytes 393224 | tf_op jit(solution)/shard_map/ppermute | solution.py:18
  2508.0 173.6 %while.76 = (s32[]{:T(128)}, f32[128,8,64]{0,2,1:T(8,128)}, s32[16]{0:T(128)}, bf16[8192,8,64]{0,2,1:T(8,128)(2,1)}, s32[8192]{0:T(1024)}, /*index=5*/s32[128]{0...) while((s32[]{:T(128)}, f32[128,8,64]{0,2,1:T(8,128)}, ...), condition=%wide.region_39.40_spmd.clone, body=%wide.region_38.39_spmd.clone.sunk | while | flops 205849216 | bytes 6968560 | solution.py:190
  2558.3 4.1 fusion.552
  2682.7 152.8 %all_gather.99 = f32[8,8192]{1,0:T(8,128)} all-gather(f32[8,128]{1,0:T(8,128)S(1)} %get-tuple-element.1977), channel_id=1, replica_groups=mesh['section'=2,'dp'=64] {'dp'}, dimensions={1}, use_global_device_ids=true | all-gather | bytes 266240 | tf_op jit(solution)/shard_map/all_gather | solution.py:199
  2841.2 5.5 add_add_fusion.1
  2851.9 225.9 %while.77 = (s32[]{:T(128)}, f32[128,8,64]{0,2,1:T(8,128)}, f32[128,8,64]{0,2,1:T(8,128)}, s32[16]{0:T(128)}, bf16[8192,8,64]{0,2,1:T(8,128)(2,1)}, /*index=5*/s...) while((s32[]{:T(128)}, f32[128,8,64]{0,2,1:T(8,128)}, ...), condition=%wide.region_41.42_spmd.clone, body=%wide.region_40.41_spmd.clone.sunk | while | flops 273613440 | bytes 9942273 | solution.py:231
  3092.3 27.3 collective-permute-start.4
  3120.2 63.7 %all-reduce = (f32[512]{0:T(512)}, f32[512]{0:T(512)}, f32[512]{0:T(512)}, f32[512]{0:T(512)}) all-reduce(f32[512]{0:T(512)} %add_add_fusion.5, f32[512]{0:T(512)S(1)} %add_add_fusion.4, f32[512]{0:T(512)S(1)} %add_add_fusion.3, f32[512]{0:T(512)S(1)} %add_add_fusion.2), channel_id=1, replica_groups=mesh['section'=2,'dp'=64] {'section','dp'}, use_global_device_ids=true, to_apply=%region_51.52 | all-reduce | flops 2048 | bytes 16384 | tf_op jit(solution)/shard_map/psum | solution.py:375
  3185.6 92.6 %all-reduce.4.cloned.1.call-done = (f32[512,512]{1,0:T(8,128)}, f32[512,512]{1,0:T(8,128)}, f32[512,512]{1,0:T(8,128)}, f32[512,512]{1,0:T(8,128)}, f32[512,2048]{1,0:T(8,128)}, /*index=5*/f32[2048,512]{1,0:T(8,128)}) async-done(((f32[512,512]{1,0:T(8,128)}, f32[512,512]{1,0:T(8,128)}, f32[512,512]{1,0:T(8,128)}, f32[512,512]{1,0:T(8,128)}, f32[512,2048]{1,0:T(8,128)}, /*index=5*/f32[2048,512]{1,0:T(8,128)}), ...) | async-done | bytes 12582928 | tf_op jit(solution)/shard_map/psum | solution.py:375
  (1331 shorter events, 1270.5 us)
Async XLA Ops:
  7.2 224.6 %copy-start = (bf16[512,2048]{1,0:T(8,128)(2,1)S(1)}, bf16[512,2048]{1,0:T(8,128)(2,1)}, u32[]{:S(2)}) copy-start(bf16[512,2048]{1,0:T(8,128)(2,1)} %param.32) | copy-start | bytes 6291460
  7.2 163.8 %all-gather.19.cloned.1.call-start = ((), (), s32[]{:S(2)}) async-start(), calls=%async_computation | async-start | bytes 8519680 | tf_op jit(solution)/shard_map/all_gather | solution.py:105
  9.5 203.7 %all-gather.21.cloned.1.call-start = ((), (), s32[]{:S(2)}) async-start(), calls=%async_computation.1 | async-start | bytes 8519680 | tf_op jit(solution)/shard_map/all_gather | solution.py:106
  11.7 338.2 %all-gather.23.cloned.1.call-start = ((), (), s32[]{:S(2)}) async-start(), calls=%async_computation.2 | async-start | bytes 8519680 | tf_op jit(solution)/shard_map/all_gather | solution.py:105
  13.2 174.0 %copy-start.73 = (bf16[128,512]{0,1:T(8,128)(2,1)}, bf16[128,512]{0,1:T(8,128)(2,1)S(1)}, u32[]{:S(2)}) copy-start(bf16[128,512]{0,1:T(8,128)(2,1)S(1)} %copy.58) | copy-start | bytes 393220
  235.4 20.4 collective-permute-start
  259.0 191.1 %all-gather.25.cloned.1.call-start = ((), (), s32[]{:S(2)}) async-start(), calls=%async_computation.3 | async-start | bytes 8519680 | tf_op jit(solution)/shard_map/all_gather | solution.py:106
  262.9 313.9 %all-gather.35.cloned.1.call-start = ((), (), s32[]{:S(2)}) async-start(), calls=%async_computation.8 | async-start | bytes 8519680 | tf_op jit(solution)/shard_map/all_gather | solution.py:105
  472.8 3.6 collective-permute-start.2
  480.4 196.8 %all-gather.37.cloned.1.call-start = ((), (), s32[]{:S(2)}) async-start(), calls=%async_computation.9 | async-start | bytes 8519680 | tf_op jit(solution)/shard_map/all_gather | solution.py:106
  484.1 541.0 %all-gather.27.cloned.1.call-start = ((), (), s32[]{:S(2)}) async-start(), calls=%async_computation.4 | async-start | bytes 8519680 | tf_op jit(solution)/shard_map/all_gather | solution.py:161
  486.0 539.1 %all-gather.29.cloned.1.call-start = ((), (), s32[]{:S(2)}) async-start(), calls=%async_computation.5 | async-start | bytes 8519680 | tf_op jit(solution)/shard_map/all_gather | solution.py:162
  487.9 718.4 %all-gather.31.cloned.1.call-start = ((), (), s32[]{:S(2)}) async-start(), calls=%async_computation.6 | async-start | bytes 8519680 | tf_op jit(solution)/shard_map/all_gather | solution.py:194
  493.3 713.0 %all-gather.33.cloned.1.call-start = ((), (), s32[]{:S(2)}) async-start(), calls=%async_computation.7 | async-start | bytes 8519680 | tf_op jit(solution)/shard_map/all_gather | solution.py:195
  702.5 1307.3 %all-gather.39.cloned.1.call-start = ((), (), s32[]{:S(2)}) async-start(), calls=%async_computation.10 | async-start | bytes 8519680 | tf_op jit(solution)/shard_map/all_gather | solution.py:161
  703.2 1306.6 %all-gather.41.cloned.1.call-start = ((), (), s32[]{:S(2)}) async-start(), calls=%async_computation.11 | async-start | bytes 8519680 | tf_op jit(solution)/shard_map/all_gather | solution.py:162
  703.8 1474.9 %all-gather.43.cloned.1.call-start = ((), (), s32[]{:S(2)}) async-start(), calls=%async_computation.12 | async-start | bytes 8519680 | tf_op jit(solution)/shard_map/all_gather | solution.py:194
  708.9 1469.8 %all-gather.45.cloned.1.call-start = ((), (), s32[]{:S(2)}) async-start(), calls=%async_computation.13 | async-start | bytes 8519680 | tf_op jit(solution)/shard_map/all_gather | solution.py:195
  1440.2 60.2 %collective-permute-start.1 = (bf16[128,512]{1,0:T(8,128)(2,1)S(1)}, bf16[128,512]{1,0:T(8,128)(2,1)S(1)}, u32[]{:S(2)}, u32[]{:S(2)}) collective-permute-start(bf16[128,512]{1,0:T(8,128)(2,1)S(1)} %fusion.198), channel_id=1, source_target_pairs={{64,0},{65,1},{66,2},{67,3},{68,4},{69,5},{70,6},{71,7},{72,8},{73... | collective-permute-start | bytes 393224 | tf_op jit(solution)/shard_map/ppermute | solution.py:18
  1509.7 997.7 %all-gather.47.cloned.1.call-start = ((), (), s32[]{:S(2)}) async-start(), calls=%async_computation.14 | async-start | bytes 8519680 | tf_op jit(solution)/shard_map/all_gather | solution.py:161
  1510.3 997.1 %all-gather.49.cloned.1.call-start = ((), (), s32[]{:S(2)}) async-start(), calls=%async_computation.15 | async-start | bytes 8519680 | tf_op jit(solution)/shard_map/all_gather | solution.py:162
  1510.9 1340.5 %all-gather.51.cloned.1.call-start = ((), (), s32[]{:S(2)}) async-start(), calls=%async_computation.16 | async-start | bytes 8519680 | tf_op jit(solution)/shard_map/all_gather | solution.py:194
  1518.6 329.7 %copy-start.115 = (f32[128]{0:T(128)S(1)}, f32[128]{0:T(128)}, u32[]{:S(2)}) copy-start(f32[128]{0:T(128)} %copy-done.112) | copy-start | bytes 1540
  1522.4 325.9 %copy-start.132 = (f32[128]{0:T(128)S(1)}, f32[128]{0:T(128)}, u32[]{:S(2)}) copy-start(f32[128]{0:T(128)} %copy-done.129) | copy-start | bytes 1540
  1531.2 1320.2 %all-gather.53.cloned.1.call-start = ((), (), s32[]{:S(2)}) async-start(), calls=%async_computation.17 | async-start | bytes 8519680 | tf_op jit(solution)/shard_map/all_gather | solution.py:195
  1852.5 157.4 %copy-start.22 = (bf16[128,8,64]{2,1,0:T(8,128)(2,1)S(1)}, bf16[128,8,64]{2,1,0:T(8,128)(2,1)}, u32[]{:S(2)}) copy-start(bf16[128,8,64]{2,1,0:T(8,128)(2,1)} %copy.73) | copy-start | bytes 393220
  1852.5 157.4 %copy-start.119 = (f32[8,128]{1,0:T(8,128)S(1)}, f32[8,128]{1,0:T(8,128)}, u32[]{:S(2)}) copy-start(f32[8,128]{1,0:T(8,128)} %get-tuple-element.1669) | copy-start | bytes 12292
  2009.9 164.9 %copy-start.68 = (bf16[128,512]{1,0:T(8,128)(2,1)S(1)}, bf16[128,512]{1,0:T(8,128)(2,1)}, u32[]{:S(2)}) copy-start(bf16[128,512]{1,0:T(8,128)(2,1)} %get-tuple-element.1007) | copy-start | bytes 393220
  2406.2 92.3 %copy-start.146 = (f32[128]{0:T(128)S(1)}, f32[128]{0:T(128)}, u32[]{:S(2)}) copy-start(f32[128]{0:T(128)} %copy-done.145) | copy-start | bytes 1540
  2406.2 92.3 %copy-start.148 = (f32[128]{0:T(128)S(1)}, f32[128]{0:T(128)}, u32[]{:S(2)}) copy-start(f32[128]{0:T(128)} %copy-done.147) | copy-start | bytes 1540
  2406.3 92.3 %copy-start.150 = (f32[128]{0:T(128)S(1)}, f32[128]{0:T(128)}, u32[]{:S(2)}) copy-start(f32[128]{0:T(128)} %copy-done.149) | copy-start | bytes 1540
  2406.3 93.1 %copy-start.163 = (f32[128]{0:T(128)S(1)}, f32[128]{0:T(128)}, u32[]{:S(2)}) copy-start(f32[128]{0:T(128)} %get-tuple-element.1062) | copy-start | bytes 1540
  2406.3 93.3 %copy-start.18 = (f32[128,2048]{1,0:T(8,128)S(1)}, f32[128,2048]{1,0:T(8,128)}, u32[]{:S(2)}) copy-start(f32[128,2048]{1,0:T(8,128)} %copy-done.16) | copy-start | bytes 3145732
  2406.3 93.3 %copy-start.30 = (f32[128,2048]{1,0:T(8,128)S(1)}, f32[128,2048]{1,0:T(8,128)}, u32[]{:S(2)}) copy-start(f32[128,2048]{1,0:T(8,128)} %copy-done.27) | copy-start | bytes 3145732
  2406.3 93.2 %copy-start.174 = (bf16[2048,512]{1,0:T(8,128)(2,1)S(1)}, bf16[2048,512]{1,0:T(8,128)(2,1)}, u32[]{:S(2)}) copy-start(bf16[2048,512]{1,0:T(8,128)(2,1)} %param.33) | copy-start | bytes 6291460
  2411.4 87.1 %collective-permute-start.3 = (bf16[128,512]{1,0:T(8,128)(2,1)S(1)}, bf16[128,512]{1,0:T(8,128)(2,1)S(1)}, u32[]{:S(2)}, u32[]{:S(2)}) collective-permute-start(bf16[128,512]{1,0:T(8,128)(2,1)S(1)} %fusion.199), channel_id=1, source_target_pairs={{64,0},{65,1},{66,2},{67,3},{68,4},{69,5},{70,6},{71,7},{72,8},{73... | collective-permute-start | bytes 393224 | tf_op jit(solution)/shard_map/ppermute | solution.py:18
  2507.1 771.2 %all-reduce.4.cloned.1.call-start = ((), (), s32[]{:S(2)}) async-start(), calls=%async_computation.18 | async-start | bytes 25165824 | tf_op jit(solution)/shard_map/psum | solution.py:375
  2507.9 327.5 %copy-start.69 = (bf16[128,512]{1,0:T(8,128)(2,1)S(1)}, bf16[128,512]{1,0:T(8,128)(2,1)}, u32[]{:S(2)}) copy-start(bf16[128,512]{1,0:T(8,128)(2,1)} %broadcast_select_fusion) | copy-start | bytes 393220
  2681.6 159.6 %copy-start.8 = (f32[512,2048]{1,0:T(8,128)S(1)}, f32[512,2048]{1,0:T(8,128)}, u32[]{:S(2)}) copy-start(f32[512,2048]{1,0:T(8,128)} %fusion.291) | copy-start | bytes 12582916
  2681.6 159.6 %copy-start.63 = (bf16[128,512]{1,0:T(8,128)(2,1)S(1)}, bf16[128,512]{1,0:T(8,128)(2,1)}, u32[]{:S(2)}) copy-start(bf16[128,512]{1,0:T(8,128)(2,1)} %get-tuple-element.1051) | copy-start | bytes 393220
  2681.6 159.6 %copy-start.66 = (bf16[128,2048]{1,0:T(8,128)(2,1)S(1)}, bf16[128,2048]{1,0:T(8,128)(2,1)}, u32[]{:S(2)}) copy-start(bf16[128,2048]{1,0:T(8,128)(2,1)} %copy-done.65) | copy-start | bytes 1572868
  2681.6 159.6 %copy-start.102 = (f32[512]{0:T(512)S(1)}, f32[512]{0:T(512)}, u32[]{:S(2)}) copy-start(f32[512]{0:T(512)} %param.35) | copy-start | bytes 6148
  2681.6 159.6 %copy-start.128 = (f32[128]{0:T(128)S(1)}, f32[128]{0:T(128)}, u32[]{:S(2)}) copy-start(f32[128]{0:T(128)} %copy-done.125) | copy-start | bytes 1540
  2682.7 152.8 %copy-start.74 = (bf16[128,8,64]{0,2,1:T(8,128)(2,1)}, bf16[128,8,64]{0,2,1:T(8,128)(2,1)S(1)}, u32[]{:S(2)}) copy-start(bf16[128,8,64]{0,2,1:T(8,128)(2,1)S(1)} %convert_element_type.266) | copy-start | bytes 393220
  3084.6 99.3 %copy-start.40 = (f32[128,512]{1,0:T(8,128)S(1)}, f32[128,512]{1,0:T(8,128)}, u32[]{:S(2)}) copy-start(f32[128,512]{1,0:T(8,128)} %copy-done.38) | copy-start | bytes 786436
  3084.6 99.3 %copy-start.99 = (f32[512]{0:T(512)S(1)}, f32[512]{0:T(512)}, u32[]{:S(2)}) copy-start(f32[512]{0:T(512)} %param.36) | copy-start | bytes 6148
  3084.6 99.3 %copy-start.107 = (f32[512]{0:T(512)S(1)}, f32[512]{0:T(512)}, u32[]{:S(2)}) copy-start(f32[512]{0:T(512)} %param.37) | copy-start | bytes 6148
  3092.3 91.6 %collective-permute-start.4 = (bf16[1,128,512]{2,1,0:T(8,128)(2,1)S(1)}, bf16[1,128,512]{2,1,0:T(8,128)(2,1)S(1)}, u32[]{:S(2)}, u32[]{:S(2)}) collective-permute-start(bf16[1,128,512]{2,1,0:T(8,128)(2,1)S(1)} %fusion.202), channel_id=1, source_target_pairs={{0,64},{64,0},{1,65},{65,1},{2,66},{66,2},{3,67},{67,3},{4,68},{68... | collective-permute-start | bytes 393224 | tf_op jit(solution)/shard_map/ppermute | solution.py:22
  (151 other events, 1822.5 us)
Sparse Core Ops, SparseCore 0:
  11.3 100.8 all-gather.18
  115.5 97.7 all-gather.20
  259.2 90.6 all-gather.22
  352.4 97.6 all-gather.24
  480.5 96.3 all-gather.34
  579.4 97.6 all-gather.36
  679.8 98.0 all-gather.26
  780.6 98.4 all-gather.28
  881.7 98.0 all-gather.30
  982.4 98.1 all-gather.32
  1083.2 97.5 all-gather.38
  1183.3 97.6 all-gather.40
  1283.7 97.6 all-gather.42
  1509.8 92.6 all-gather.44
  1605.1 98.2 all-gather.46
  1705.9 98.2 all-gather.48
  1806.7 97.9 all-gather.50
  2507.2 90.6 all-gather.52
  3084.8 193.4 all-reduce.3
where the time goes:
time: 3320 us; the launch traced here: 3300 us
  blocking collectives  1150 us (35%)
  matrix products  993 us (30%)
  waiting for transfers between devices  421 us (13%)
  local copies, waits for them, and re-layouts  279 us (8%)
  other arithmetic  203 us (6%)
  starting transfers between devices  175 us (5%)
  loops' own time  63.8 us (2%)
    all_gather x3, blocking collectives, attention_back(): lax.all_gather(log_total, 'dp', axis=1, tiled=True)  470 us
    all_gather x3, blocking collectives, attention_back(): lax.all_gather(delta, 'dp', axis=1, tiled=True)  462 us
    dot_general x96, matrix products, score_grads(): jnp.einsum('thd,shd->hts', query_blk, key_blk, preferred_element_type=jnp...  299 us
    dot_general x48, matrix products, query_only(): jnp.einsum('hts,shd->thd', grad_scores, key_blk, preferred_element_type=j...  187 us
    dot_general x48, matrix products, over_queries(): jnp.einsum('hts,thd->shd', grad_scores, query_blk, preferred_element_type...  182 us
    all_gather x3, waiting for transfers between devices, forward_visit(): key_piece = lax.all_gather(keys_loc, 'dp', axis=0, tiled=True)  162 us
    all_gather x1, blocking collectives, on_device(): whole_groups = lax.all_gather(groups, 'dp', axis=1, tiled=True)  151 us
    ppermute x4, starting transfers between devices, passed_along(): lax.ppermute(value, axis, [(source, source + steps) for source in range(l...  146 us
  transfers between devices with their start and end apart: 24, of which 8 were waited for; matrix products, arithmetic and copies ran while one was open for 36% of the time, Pallas kernels for 0%

commit v1 on v0

v1 whole, which is shorter than its diff:
```python
from types import SimpleNamespace

import jax
import jax.numpy as jnp
from jax import lax
from jax.experimental import pallas as pl
from jax.experimental.pallas import tpu as pltpu
from jax.sharding import PartitionSpec as P

F32, BF = jnp.float32, jnp.bfloat16
BIG = 1e30
ROWS, D, FF, HEADS = 128, 512, 2048, 8
MESH = pl.DeviceIdType.MESH
FWD_C, BWD_C = 8, 4


def nt(a, b):
    return lax.dot_general(a, b, (((1,), (1,)), ((), ())), preferred_element_type=F32)


def nn(a, b):
    return lax.dot_general(a, b, (((1,), (0,)), ((), ())), preferred_element_type=F32)


def tn(a, b):
    return lax.dot_general(a, b, (((0,), (0,)), ((), ())), preferred_element_type=F32)


def lanes(shape):
    return lax.broadcasted_iota(jnp.int32, shape, len(shape) - 1)


def subs(shape):
    return lax.broadcasted_iota(jnp.int32, shape, len(shape) - 2)


def ds(start, size):
    if isinstance(start, int):
        return pl.ds(start, size)
    return pl.ds(pl.multiple_of(start, size), size)


def split3(x):
    a = x.astype(BF).astype(F32)
    b = (x - a).astype(BF).astype(F32)
    return a, b, (x - a - b).astype(BF).astype(F32)


def tile_of(r, t):
    return 8 * (r // 2) + jnp.where(r % 2 == 0, t, 7 - t)


def mean(x):
    return jnp.mean(x, axis=-1, keepdims=True)


def norm(x):
    centred = x - mean(x)
    factor = lax.rsqrt(mean(centred * centred) + 1e-05)
    return centred * factor, factor


def norm_back(dy, n, factor, gain):
    u = dy * gain
    return factor * (u - mean(u) - n * mean(u * n))


GELU_C = 0.7978845608028654


def gelu(x):
    return 0.5 * x * (1.0 + jnp.tanh(GELU_C * (x + 0.044715 * x * x * x)))


def gelu_slope(x):
    sq = x * x
    th = jnp.tanh(GELU_C * x * (1.0 + 0.044715 * sq))
    return 0.5 * (1.0 + th) + 0.5 * x * (1.0 - th * th) * (GELU_C * (1.0 + 3 * 0.044715 * sq))


class Place:
    def __init__(self):
        self.me = lax.axis_index("dp")
        self.s = lax.axis_index("section")
        me = self.me
        self.t = me % 4
        self.head = (me // 4) % 8
        self.micro = me // 32
        w = (me // 2) % 8
        low = w < 4
        self.own_t = jnp.where(low, w, 7 - w)
        self.own_slot = 4 * (me // 16) + jnp.where(low, 0, 2) + me % 2
        mine = self.micro == self.s
        self.self_kv = mine & (me % 2 == self.s)
        self.self_q = mine & (self.own_t == self.t)

    def chip(self, h, t):
        return (self.s * 8 + h) * 4 + t

    def send(self, src, dst, send_sem, recv_sem, section, dp):
        to_self = (section == self.s) & (dp == self.me)

        @pl.when(jnp.logical_not(to_self))
        def _():
            pltpu.make_async_remote_copy(
                src_ref=src,
                dst_ref=dst,
                send_sem=send_sem,
                recv_sem=recv_sem,
                device_id=(section, dp),
                device_id_type=MESH,
            ).start()

        @pl.when(to_self)
        def _():
            pltpu.make_async_copy(src, dst, recv_sem).start()


def wait_all(ref, sem):
    pltpu.make_async_copy(ref, ref, sem).wait()


def wait_sent(ref, sem, to_self, count):
    @pl.when(to_self)
    def _():
        wait_all(ref.at[pl.ds(0, count - 1)], sem)

    @pl.when(jnp.logical_not(to_self))
    def _():
        wait_all(ref.at[pl.ds(0, count)], sem)


def barrier(place):
    sem = pltpu.get_barrier_semaphore()

    @pl.loop(1, 128)
    def _(k):
        other = (place.s * 64 + place.me + k) % 128
        pl.semaphore_signal(sem, inc=1, device_id=(other // 64, other % 64), device_id_type=MESH)

    pl.semaphore_wait(sem, 127)


def project(v, r):
    hid = r.hid[v]
    q = nn(hid, r.w_query[...]).astype(BF).astype(F32) * 0.125
    k = nn(hid, r.w_key[...]).astype(BF).astype(F32)
    w = nn(hid, r.w_value[...]).astype(BF).astype(F32)
    ln = lanes((ROWS, 128))
    low = ln < 64
    aug = r.own_aug[...]
    for h in range(HEADS):
        cols = slice(128 * (h // 2), 128 * (h // 2) + 128)
        qt, kt, vt = q[:, cols], k[:, cols], w[:, cols]
        if h % 2 == 0:
            vt = pltpu.roll(vt, 64, 1)
        else:
            qt, kt = pltpu.roll(qt, 64, 1), pltpu.roll(kt, 64, 1)
        r.q_out[v, h] = jnp.where(low, qt, aug).astype(BF)
        r.kv_out[v, h] = jnp.where(low, kt, vt).astype(BF)


def send_qkv(v, r, place):
    @pl.loop(0, HEADS)
    def _(h):
        for t in range(4):
            place.send(
                r.kv_out.at[v, h],
                r.kv_in.at[v, place.me // 2],
                r.sems.at[0, v],
                r.sems.at[1, v],
                place.me % 2,
                place.chip(h, t),
            )
        for core in range(2):
            place.send(
                r.q_out.at[v, h],
                r.q_in.at[v, place.own_slot],
                r.sems.at[2, v],
                r.sems.at[3, v],
                core,
                place.chip(h, place.own_t),
            )


def send_groups(r, place):
    r.grp_out[0] = jnp.broadcast_to(r.groups[pl.ds(place.s, 1), :], (8, 128))

    @pl.loop(0, HEADS)
    def _(h):
        for t in range(4):
            place.send(
                r.grp_out.at[0],
                r.grp_in.at[place.me // 2],
                r.gsems.at[0],
                r.gsems.at[1],
                place.me % 2,
                place.chip(h, t),
            )


def column_of(row):
    return jnp.transpose(jnp.broadcast_to(row.astype(F32), (128, 128)))


def make_own_aug(r, place):
    ln = lanes((ROWS, 128))
    g = column_of(r.groups[pl.ds(place.s, 1), :]).astype(jnp.int32)
    r.own_aug[...] = jnp.where(ln - 64 == g, 1.0, 0.0)


def make_key_aug(r):
    ln = lanes((ROWS, 128))

    @pl.loop(0, 32)
    def _(n):
        g = column_of(r.grp_in[n][0:1, :]).astype(jnp.int32)
        inside = (ln >= 64) & (ln < 68)
        aug = jnp.where(inside, jnp.where(ln - 64 == g, 0.0, -BIG), 0.0)
        r.key_aug[n] = jnp.where((ln >= 68) & (ln < 71), 1.0, aug).astype(BF)


def make_kv(v, r):
    ln = lanes((ROWS, 128))
    low = ln < 64
    ones = jnp.where(ln < 3, 1.0, 0.0)

    @pl.loop(0, 32)
    def _(n):
        rows = ds(n * 128, 128)
        kv = r.kv_in[v, n].astype(F32)
        r.ka[v, rows, :] = jnp.where(low, kv, r.key_aug[n].astype(F32)).astype(BF)
        r.va[v, rows, :] = jnp.where(low, ones, kv).astype(BF)


def fwd_tile(v, i, r, place):
    width = FWD_C * 128
    u = tile_of(i, place.t)
    q = jnp.concatenate([r.q_in[v, 2 * i], r.q_in[v, 2 * i + 1]], axis=0)

    def step(c, carry, masked):
        top, acc = carry
        rows = ds(c * width, width)
        sc = nt(q, r.ka[v, rows, :])
        if masked:
            col, row = lanes((256, width)), subs((256, width))
            at = 256 * (col // 128) + col % 128 + (256 * FWD_C * c + 128 * place.s - 256 * u)
            sc = jnp.where(at <= row, sc, -BIG)
        new = jnp.maximum(top, jnp.max(sc, axis=1, keepdims=True))
        p = jnp.exp(sc - new).astype(BF)
        return new, acc * jnp.exp(top - new) + nn(p, r.va[v, rows, :])

    start = (jnp.full((256, 1), -2 * BIG, F32), jnp.zeros((256, 128), F32))
    full = u // FWD_C
    carry = lax.fori_loop(0, full, lambda c, x: step(c, x, False), start)
    top, acc = step(full, carry, True)
    total = acc[:, 0:1]
    a, b, c = split3(top + jnp.log(total))
    ln = lanes((256, 128))
    aux = jnp.where(ln == 0, a, jnp.where(ln == 1, b, jnp.where(ln == 2, c, 0.0)))
    out = jnp.where(ln >= 64, acc / total, aux).astype(BF)
    r.o_out[v, 2 * i] = out[:128]
    r.o_out[v, 2 * i + 1] = out[128:]
    for half in range(2):
        place.send(
            r.o_out.at[v, 2 * i + half],
            r.o_in.at[v, 2 * place.head + place.s],
            r.sems.at[4, v],
            r.sems.at[5, v],
            place.micro,
            2 * u + half,
        )


def after_attention(v, r):
    ln = lanes((ROWS, 128))
    low = ln < 64
    att = []
    for h in range(HEADS):
        parts = [r.o_in[v, 2 * h + core].astype(F32) for core in range(2)]
        logs = [x[:, 0:1] + x[:, 1:2] + x[:, 2:3] for x in parts]
        top = jnp.maximum(logs[0], logs[1])
        weights = [jnp.exp(x - top) for x in logs]
        total = weights[0] + weights[1]
        whole = (parts[0] * weights[0] + parts[1] * weights[1]) / total
        log_total = top + jnp.log(total)
        r.att[v, h] = jnp.where(low, jnp.where(ln == 0, log_total, 0.0), whole)
        att.append(whole)
    for i in range(HEADS // 2):
        pair = jnp.where(low, pltpu.roll(att[2 * i], 64, 1), att[2 * i + 1])
        r.att_low[v, :, 128 * i : 128 * i + 128] = pair.astype(BF)
    mixed = r.hid[v].astype(F32) + nn(r.att_low[v], r.w_out[...])
    n_one, f_one = norm(mixed)
    first = n_one * r.gain_one[...] + r.shift_one[...]
    first_low = first.astype(BF)
    r.n_one[v] = n_one
    r.f_one[v] = jnp.broadcast_to(f_one, (ROWS, 128))
    r.first_low[v] = first_low
    r.work[...] = first

    @pl.loop(0, 4)
    def _(j):
        cols = ds(j * 512, 512)
        pre = nn(r.first_low[v], r.w_up[:, cols])
        r.pre[v, :, cols] = pre
        act = gelu(pre).astype(BF)
        r.act[v, :, cols] = act
        r.work[...] += nn(act, r.w_down[cols, :])

    n_two, f_two = norm(r.work[...])
    r.n_two[v] = n_two
    r.f_two[v] = jnp.broadcast_to(f_two, (ROWS, 128))
    r.hid[v + 1] = (n_two * r.gain_two[...] + r.shift_two[...]).astype(BF)


def before_attention_back(v, r):
    dy = r.dy[...]
    n_two = r.n_two[v]
    r.vec[2:3, :] += jnp.sum(dy * n_two, axis=0, keepdims=True)
    r.vec[3:4, :] += jnp.sum(dy, axis=0, keepdims=True)
    grad_two = norm_back(dy, n_two, r.f_two[v][:, 0:1], r.gain_two[...])
    r.down_low[v] = grad_two.astype(BF)
    r.work[...] = grad_two

    @pl.loop(0, 4)
    def _(j):
        cols = ds(j * 512, 512)
        grad = nt(r.down_low[v], r.w_down[cols, :])
        up = (grad * gelu_slope(r.pre[v, :, cols])).astype(BF)
        r.up_low[v, :, cols] = up
        r.work[...] += nt(up, r.w_up[:, cols])

    dz = r.work[...]
    n_one = r.n_one[v]
    r.vec[0:1, :] += jnp.sum(dz * n_one, axis=0, keepdims=True)
    r.vec[1:2, :] += jnp.sum(dz, axis=0, keepdims=True)
    grad_one = norm_back(dz, n_one, r.f_one[v][:, 0:1], r.gain_one[...])
    out_low = grad_one.astype(BF)
    r.out_low[v] = out_low
    r.work[...] = grad_one
    grad_att = nt(out_low, r.w_out[...]).astype(BF).astype(F32)
    ln = lanes((ROWS, 128))
    low = ln < 64
    for h in range(HEADS):
        tile = grad_att[:, 128 * (h // 2) : 128 * (h // 2) + 128]
        if h % 2 == 0:
            tile = pltpu.roll(tile, 64, 1)
        att = r.att[v, h]
        delta = jnp.sum(jnp.where(low, 0.0, tile * att), axis=1, keepdims=True)
        parts = split3(-delta) + split3(-att[:, 0:1])
        aux = jnp.zeros((ROWS, 128), F32)
        for i, part in enumerate(parts):
            aux = jnp.where(ln == i, part, aux)
        r.do_out[v, h] = jnp.where(low, aux, tile).astype(BF)


def send_do(v, r, place):
    @pl.loop(0, HEADS)
    def _(h):
        for core in range(2):
            place.send(
                r.do_out.at[v, h],
                r.do_in.at[v, place.own_slot],
                r.sems.at[6, v],
                r.sems.at[7, v],
                core,
                place.chip(h, place.own_t),
            )


def bwd_tile(v, i, r, place):
    width = BWD_C * 128
    u = tile_of(i, place.t)
    q = jnp.concatenate([r.q_in[v, 2 * i], r.q_in[v, 2 * i + 1]], axis=0).astype(F32)
    do = jnp.concatenate([r.do_in[v, 2 * i], r.do_in[v, 2 * i + 1]], axis=0).astype(F32)
    ln = lanes((256, 128))
    lq = jnp.where((ln >= 68) & (ln < 71), pltpu.roll(do, 65, 1), q).astype(BF)
    ld = jnp.where((ln >= 3) & (ln < 64), 0.0, do).astype(BF)
    qz = jnp.where(ln < 64, q, 0.0).astype(BF)
    dz = jnp.where(ln >= 64, do, 0.0).astype(BF)

    def step(c, dqt, masked):
        rows = ds(c * width, width)
        x = nt(r.ka[v, rows, :], lq)
        if masked:
            row, col = subs((width, 256)), lanes((width, 256))
            at = 256 * (row // 128) + row % 128 + (256 * BWD_C * c + 128 * place.s - 256 * u)
            x = jnp.where(at <= col, x, -BIG)
        p = jnp.exp(x)
        dp = nt(r.va[v, rows, :], ld)
        dsc = (p * dp).astype(BF)
        r.dkv_acc[rows, :] += nn(dsc, qz) + nn(p.astype(BF), dz)
        return dqt + nn(r.kat[:, rows], dsc)

    full = u // BWD_C
    dqt = lax.fori_loop(0, full, lambda c, x: step(c, x, False), jnp.zeros((64, 256), F32))
    dqt = step(full, dqt, True)
    dq = jnp.transpose(jnp.concatenate([dqt, jnp.zeros((64, 256), F32)], axis=0)).astype(BF)
    r.dq_out[v, 2 * i] = dq[:128]
    r.dq_out[v, 2 * i + 1] = dq[128:]
    for half in range(2):
        place.send(
            r.dq_out.at[v, 2 * i + half],
            r.dq_in.at[v, 2 * place.head + place.s],
            r.sems.at[8, v],
            r.sems.at[9, v],
            place.micro,
            2 * u + half,
        )


def attention_back(v, r, place):
    r.dkv_acc[...] = jnp.zeros_like(r.dkv_acc)

    @pl.loop(0, 8)
    def _(i):
        rows = ds(i * 512, 512)
        r.kat[:, rows] = jnp.transpose(r.ka[v, rows, :].astype(F32))[:64].astype(BF)

    @pl.loop(0, 8)
    def _(i):
        bwd_tile(v, i, r, place)

    @pl.loop(0, 32)
    def _(n):
        r.dkv_out[v, n] = r.dkv_acc[ds(n * 128, 128), :].astype(BF)
        place.send(
            r.dkv_out.at[v, n],
            r.dkv_in.at[v, 4 * place.head + place.t],
            r.sems.at[10, v],
            r.sems.at[11, v],
            place.micro,
            2 * n + place.s,
        )


def after_attention_back(v, r):
    ln = lanes((ROWS, 128))
    low = ln < 64
    for i in range(HEADS // 2):
        cols = slice(128 * i, 128 * i + 128)
        dq, dkv = [], []
        for h in (2 * i, 2 * i + 1):
            both = r.dq_in[v, 2 * h].astype(F32) + r.dq_in[v, 2 * h + 1].astype(F32)
            dq.append(both * 0.125)
            four = [r.dkv_in[v, 4 * h + t].astype(F32) for t in range(4)]
            dkv.append((four[0] + four[1]) + (four[2] + four[3]))
        r.dq[v, :, cols] = jnp.where(low, dq[0], pltpu.roll(dq[1], 64, 1)).astype(BF)
        r.dk[v, :, cols] = jnp.where(low, dkv[0], pltpu.roll(dkv[1], 64, 1)).astype(BF)
        r.dv[v, :, cols] = jnp.where(low, pltpu.roll(dkv[0], 64, 1), dkv[1]).astype(BF)
    r.work[...] += (
        nt(r.dq[v], r.w_query[...]) + nt(r.dk[v], r.w_key[...]) + nt(r.dv[v], r.w_value[...])
    )


def both(ref):
    return jnp.concatenate([ref[0], ref[1]], axis=0)


def weight_grads(r):
    hid = jnp.concatenate([r.hid[0], r.hid[1]], axis=0)
    r.g_query[...] = tn(hid, both(r.dq))
    r.g_key[...] = tn(hid, both(r.dk))
    r.g_value[...] = tn(hid, both(r.dv))
    r.g_out[...] = tn(both(r.att_low), both(r.out_low))

    @pl.loop(0, 4)
    def _(j):
        cols = ds(j * 512, 512)
        up = jnp.concatenate([r.up_low[0, :, cols], r.up_low[1, :, cols]], axis=0)
        r.g_up[:, cols] = tn(both(r.first_low), up)
        act = jnp.concatenate([r.act[0, :, cols], r.act[1, :, cols]], axis=0)
        r.g_down[cols, :] = tn(act, both(r.down_low))


INPUTS = ["inputs", "groups", "cotangent", "w_query", "w_key", "w_value", "w_out", "w_up", "w_down"]
INPUTS += ["gain_one", "shift_one", "gain_two", "shift_two"]
OUTPUTS = {
    "output": ((1, ROWS, D), BF),
    "input_grad": ((1, ROWS, D), BF),
    "g_query": ((D, D), F32),
    "g_key": ((D, D), F32),
    "g_value": ((D, D), F32),
    "g_out": ((D, D), F32),
    "g_up": ((D, FF), F32),
    "g_down": ((FF, D), F32),
    "vec": ((8, D), F32),
}
SCRATCH = {
    "hid": ((3, ROWS, D), BF),
    "own_aug": ((ROWS, 128), F32),
    "q_out": ((2, 8, ROWS, 128), BF),
    "kv_out": ((2, 8, ROWS, 128), BF),
    "q_in": ((2, 16, ROWS, 128), BF),
    "kv_in": ((2, 32, ROWS, 128), BF),
    "grp_out": ((1, 8, 128), jnp.int32),
    "grp_in": ((32, 8, 128), jnp.int32),
    "key_aug": ((32, ROWS, 128), BF),
    "ka": ((2, 4096, 128), BF),
    "va": ((2, 4096, 128), BF),
    "kat": ((64, 4096), BF),
    "o_out": ((2, 16, ROWS, 128), BF),
    "o_in": ((2, 16, ROWS, 128), BF),
    "att": ((2, 8, ROWS, 128), F32),
    "att_low": ((2, ROWS, D), BF),
    "n_one": ((2, ROWS, D), F32),
    "f_one": ((2, ROWS, 128), F32),
    "first_low": ((2, ROWS, D), BF),
    "pre": ((2, ROWS, FF), F32),
    "act": ((2, ROWS, FF), BF),
    "n_two": ((2, ROWS, D), F32),
    "f_two": ((2, ROWS, 128), F32),
    "work": ((ROWS, D), F32),
    "dy": ((ROWS, D), F32),
    "down_low": ((2, ROWS, D), BF),
    "up_low": ((2, ROWS, FF), BF),
    "out_low": ((2, ROWS, D), BF),
    "do_out": ((2, 8, ROWS, 128), BF),
    "do_in": ((2, 16, ROWS, 128), BF),
    "dq_out": ((2, 16, ROWS, 128), BF),
    "dq_in": ((2, 16, ROWS, 128), BF),
    "dkv_acc": ((4096, 128), F32),
    "dkv_out": ((2, 32, ROWS, 128), BF),
    "dkv_in": ((2, 32, ROWS, 128), BF),
    "dq": ((2, ROWS, D), BF),
    "dk": ((2, ROWS, D), BF),
    "dv": ((2, ROWS, D), BF),
}


def kernel(*refs):
    names = INPUTS + list(OUTPUTS) + list(SCRATCH) + ["sems", "gsems"]
    r = SimpleNamespace(**dict(zip(names, refs)))
    place = Place()
    barrier(place)
    send_groups(r, place)
    make_own_aug(r, place)
    r.vec[...] = jnp.zeros_like(r.vec)
    r.hid[0] = r.inputs[place.s]

    @pl.loop(0, 2)
    def _(v):
        project(v, r)
        send_qkv(v, r, place)

        @pl.when(v == 0)
        def _():
            wait_all(r.grp_in, r.gsems.at[1])
            make_key_aug(r)

        wait_all(r.kv_in.at[v], r.sems.at[1, v])
        make_kv(v, r)
        wait_all(r.q_in.at[v], r.sems.at[3, v])

        @pl.loop(0, 8)
        def _(i):
            fwd_tile(v, i, r, place)

        wait_all(r.o_in.at[v], r.sems.at[5, v])
        after_attention(v, r)

    r.output[0] = r.hid[2]
    r.dy[...] = r.cotangent[place.s].astype(F32)

    @pl.loop(0, 2)
    def _(step):
        v = 1 - step
        before_attention_back(v, r)
        send_do(v, r, place)
        wait_all(r.do_in.at[v], r.sems.at[7, v])
        attention_back(v, r, place)
        wait_all(r.dq_in.at[v], r.sems.at[9, v])
        wait_all(r.dkv_in.at[v], r.sems.at[11, v])
        after_attention_back(v, r)
        r.dy[...] = r.work[...].astype(BF).astype(F32)

    r.input_grad[0] = r.dy[...].astype(BF)
    weight_grads(r)

    wait_sent(r.grp_in, r.gsems.at[0], place.self_kv, 32)

    @pl.loop(0, 2)
    def _(v):
        wait_sent(r.kv_in.at[v], r.sems.at[0, v], place.self_kv, 32)
        wait_sent(r.q_in.at[v], r.sems.at[2, v], place.self_q, 16)
        wait_sent(r.o_in.at[v], r.sems.at[4, v], place.self_q, 16)
        wait_sent(r.do_in.at[v], r.sems.at[6, v], place.self_q, 16)
        wait_sent(r.dq_in.at[v], r.sems.at[8, v], place.self_q, 16)
        wait_sent(r.dkv_in.at[v], r.sems.at[10, v], place.self_kv, 32)


def on_device(inputs, groups, cotangent, *params):
    vectors = [x.reshape(1, D) for x in params[6:]]
    vmem = pl.BlockSpec(memory_space=pltpu.VMEM)
    out = pl.pallas_call(
        kernel,
        out_shape=[jax.ShapeDtypeStruct(shape, kind) for shape, kind in OUTPUTS.values()],
        in_specs=[vmem] * len(INPUTS),
        out_specs=[vmem] * len(OUTPUTS),
        scratch_shapes=[pltpu.VMEM(shape, kind) for shape, kind in SCRATCH.values()]
        + [pltpu.SemaphoreType.DMA((12, 2)), pltpu.SemaphoreType.DMA((2,))],
        compiler_params=pltpu.CompilerParams(
            collective_id=0, has_side_effects=True, vmem_limit_bytes=60 * 2**20
        ),
        name="visits",
    )(inputs, groups, cotangent, *params[:6], *vectors)
    sums = lax.psum(tuple(out[2:]), ("section", "dp"))
    vec = sums[6]
    return (*out[:2], *sums[:6], vec[0], vec[1], vec[2], vec[3])


def solution(mesh):
    rows = P(None, "dp", None)
    return jax.shard_map(
        on_device,
        mesh=mesh,
        in_specs=(rows, P(None, "dp"), rows) + (P(),) * 10,
        out_specs=(P("section", "dp", None),) * 2 + (P(),) * 10,
        check_vma=False,
    )
```

time: 3320 us -> 478 us (0.14)
  blocking collectives: 1150 us -> 77.3 us
  matrix products: 993 us -> 0 us
  waiting for transfers between devices: 421 us -> 106 us
  Pallas kernels: 0 us -> 266 us
  local copies, waits for them, and re-layouts: 279 us -> 14.9 us
  other arithmetic: 203 us -> 0 us
  starting transfers between devices: 175 us -> 0.04 us
  loops' own time: 63.8 us -> 0 us
    all_gather x7 -> x0, blocking collectives: 1080 us -> none  [the longest x3 470 us: attention_back(): lax.all_gather(log_total, 'dp', axis=1, tiled=True)]
    dot_general x300 -> x0, matrix products: 993 us -> none  [the longest x96 299 us: score_grads(): jnp.einsum('thd,shd->hts', query_blk, key_blk, preferred_element_type=jnp...]
    all_gather x18 -> x0, waiting for transfers between devices: 304 us -> none  [the longest x3 162 us: forward_visit(): key_piece = lax.all_gather(keys_loc, 'dp', axis=0, tiled=True)]
    pallas_call x0 -> x1, Pallas kernels: none -> 266 us  [on_device(): pl.pallas_call(kernel, out_shape=[jax.ShapeDtypeStruct(shape, kind) for s...]
    dynamic_slice x240 -> x0, local copies, waits for them, and re-layouts: 215 us -> none  [the longest x96 107 us: attention_back(): lax.scan(query_only, zero_query, jnp.arange(block_count, dtype=jnp.int32))]
    ppermute x5 -> x0, starting transfers between devices: 173 us -> none  [the longest x4 146 us: passed_along(): lax.ppermute(value, axis, [(source, source + steps) for source in range(l...]
    and x97 -> x0, other arithmetic: 112 us -> none  [mask_for(): (key_pos[None, :] <= query_pos[:, None]) & (key_grp[None, :] == query_grp...]
    another operation x6 -> x0, loops' own time: 63.8 us -> none  [the longest x3 32.1 us: attention_back(): lax.scan(over_queries, (zero_query, zero_query), jnp.arange(block_count,...]
  transfers between devices with their start and end apart: 24 -> 1, of which waited for: 8 -> 1; matrix products, arithmetic and copies ran while one was open for 36% -> 0% of each run, Pallas kernels for 0% -> 0%
where the time goes in v1:
time: 478 us
  Pallas kernels  266 us (56%)
  waiting for transfers between devices  106 us (22%)
  blocking collectives  77.3 us (16%)
  local copies, waits for them, and re-layouts  14.9 us (3%)
  between operations  14.1 us (3%)
    pallas_call x1, Pallas kernels, on_device(): pl.pallas_call(kernel, out_shape=[jax.ShapeDtypeStruct(shape, kind) for s...  266 us
    psum x1, waiting for transfers between devices, on_device(): sums = lax.psum(tuple(out[2:]), ('section', 'dp'))  106 us
    psum x1, blocking collectives, on_device(): sums = lax.psum(tuple(out[2:]), ('section', 'dp'))  77.3 us
    unnamed x22, local copies, waits for them, and re-layouts  14.3 us
  transfers between devices with their start and end apart: 1, of which 1 were waited for; matrix products, arithmetic and copies ran while one was open for 0% of the time, Pallas kernels for 0%

profile of v1, /device:TPU:1, one launch (start us, length us, event | category | flops | bytes accessed | tf_op | source)
XLA Modules:
  0.0 477.6 jit_solution(10045706108552098041)
XLA Ops:
  7.2 0.0 all-reduce.3.cloned.1.call-start
  7.2 265.6 %visits.1 = (bf16[1,128,512]{2,1,0:T(8,128)(2,1)}, bf16[1,128,512]{2,1,0:T(8,128)(2,1)}, f32[512,512]{1,0:T(8,128)}, f32[512,512]{1,0:T(8,128)}, f32[512,512]{1,...) custom-call(bf16[2,128,512]{2,1,0:T(8,128)(2,1)} %refs_0_.1, ...), custom_call_target="tpu_custom_call" | custom-call | tf_op jit(solution)/shard_map/visits/pallas_call | solution.py:595
  272.8 0.0 copy-start.6
  272.8 0.0 copy-start.5
  272.8 0.0 copy-start.4
  272.8 0.0 all-reduce.3.cloned.1.call-update
  272.9 0.7 copy-done.6
  273.5 77.3 %psum.55 = f32[8,512]{1,0:T(8,128)S(1)} all-reduce(f32[8,512]{1,0:T(8,128)S(1)} %copy-done.6), channel_id=1, replica_groups=mesh['section'=2,'dp'=64] {'section','dp'}, use_global_device_ids=true, to_apply=%region_6.0 | all-reduce | flops 4096 | bytes 32768 | tf_op jit(solution)/shard_map/psum | solution.py:607
  350.8 0.6 fusion
  351.4 105.8 %all-reduce.3.cloned.1.call-done = (f32[512,512]{1,0:T(8,128)}, f32[512,512]{1,0:T(8,128)}, f32[512,512]{1,0:T(8,128)}, f32[512,512]{1,0:T(8,128)}, f32[512,2048]{1,0:T(8,128)}, /*index=5*/f32[2048,512]{1,0:T(8,128)}) async-done(((f32[512,512]{1,0:T(8,128)}, f32[512,512]{1,0:T(8,128)}, f32[512,512]{1,0:T(8,128)}, f32[512,512]{1,0:T(8,128)}, f32[512,2048]{1,0:T(8,128)}, /*index=5*/f32[2048,512]{1,0:T(8,128)}), ...) | async-done | bytes 12582928 | tf_op jit(solution)/shard_map/psum | solution.py:607
  457.1 0.0 copy-start.3
  457.1 0.0 copy-start.2
  457.1 0.0 copy-done.5
  457.1 0.7 copy.39
  457.8 0.0 copy-done.4
  457.8 0.7 copy.40
  458.4 0.0 copy-start.1
  458.4 2.4 copy.41
  460.9 2.3 copy.42
  463.1 0.0 copy-done.3
  463.1 1.0 copy.43
  464.1 0.0 copy-done.2
  464.1 1.0 copy.44
  465.1 0.0 copy-done.1
  465.1 0.0 copy-start
  465.1 2.1 copy.45
  467.2 1.6 copy-done
  468.8 2.0 copy.46
Async XLA Ops:
  7.2 449.9 %all-reduce.3.cloned.1.call-start = ((), (), s32[]{:S(2)}) async-start(), calls=%async_computation | async-start | bytes 25165824 | tf_op jit(solution)/shard_map/psum | solution.py:607
  272.8 0.7 copy-start.6
  272.8 184.3 %copy-start.5 = (bf16[1,128,512]{2,1,0:T(8,128)(2,1)S(1)}, bf16[1,128,512]{2,1,0:T(8,128)(2,1)}, u32[]{:S(2)}) copy-start(bf16[1,128,512]{2,1,0:T(8,128)(2,1)} %get-tuple-element.52) | copy-start | bytes 393220
  272.8 185.0 %copy-start.4 = (bf16[1,128,512]{2,1,0:T(8,128)(2,1)S(1)}, bf16[1,128,512]{2,1,0:T(8,128)(2,1)}, u32[]{:S(2)}) copy-start(bf16[1,128,512]{2,1,0:T(8,128)(2,1)} %get-tuple-element.53) | copy-start | bytes 393220
  457.1 6.0 %copy-start.3 = (f32[512,512]{1,0:T(8,128)S(1)}, f32[512,512]{1,0:T(8,128)}, u32[]{:S(2)}) copy-start(f32[512,512]{1,0:T(8,128)} %get-tuple-element.56) | copy-start | bytes 3145732
  457.1 7.0 %copy-start.2 = (f32[512,512]{1,0:T(8,128)S(1)}, f32[512,512]{1,0:T(8,128)}, u32[]{:S(2)}) copy-start(f32[512,512]{1,0:T(8,128)} %get-tuple-element.57) | copy-start | bytes 3145732
  458.4 6.6 %copy-start.1 = (f32[512,2048]{1,0:T(8,128)S(1)}, f32[512,2048]{1,0:T(8,128)}, u32[]{:S(2)}) copy-start(f32[512,2048]{1,0:T(8,128)} %get-tuple-element.58) | copy-start | bytes 12582916
  465.1 3.7 copy-start
Sparse Core Ops, SparseCore 0:
  273.0 184.0 all-reduce.2

commit v2 on v1

--- a/solution.py
+++ b/solution.py
@@ -83,6 +83,7 @@
         self.me = lax.axis_index("dp")
         self.s = lax.axis_index("section")
         me = self.me
+        self.coords = (me % 4, me // 16, (me // 4) % 4)
         self.t = me % 4
         self.head = (me // 4) % 8
         self.micro = me // 32
@@ -93,6 +94,10 @@
         mine = self.micro == self.s
         self.self_kv = mine & (me % 2 == self.s)
         self.self_q = mine & (self.own_t == self.t)
+
+    def along(self, axis, d):
+        c = self.coords[axis]
+        return self.me + ((c + d) % 4 - c) * (1, 16, 4)[axis]
 
     def chip(self, h, t):
         return (self.s * 8 + h) * 4 + t
@@ -162,23 +167,25 @@
 
 def send_qkv(v, r, place):
     @pl.loop(0, HEADS)
-    def _(h):
-        for t in range(4):
+    def _(a):
+        h = (place.me // 8 + a) % 8
+        for b in range(4):
             place.send(
                 r.kv_out.at[v, h],
                 r.kv_in.at[v, place.me // 2],
                 r.sems.at[0, v],
                 r.sems.at[1, v],
                 place.me % 2,
-                place.chip(h, t),
+                place.chip(h, (place.me // 2 + b) % 4),
             )
-        for core in range(2):
+        h = (place.own_slot // 2 + a) % 8
+        for b in range(2):
             place.send(
                 r.q_out.at[v, h],
                 r.q_in.at[v, place.own_slot],
                 r.sems.at[2, v],
                 r.sems.at[3, v],
-                core,
+                (place.me + b) % 2,
                 place.chip(h, place.own_t),
             )
 
@@ -187,15 +194,16 @@
     r.grp_out[0] = jnp.broadcast_to(r.groups[pl.ds(place.s, 1), :], (8, 128))
 
     @pl.loop(0, HEADS)
-    def _(h):
-        for t in range(4):
+    def _(a):
+        h = (place.me // 8 + a) % 8
+        for b in range(4):
             place.send(
                 r.grp_out.at[0],
                 r.grp_in.at[place.me // 2],
                 r.gsems.at[0],
                 r.gsems.at[1],
                 place.me % 2,
-                place.chip(h, t),
+                place.chip(h, (place.me // 2 + b) % 4),
             )
 
 
@@ -261,7 +269,8 @@
     out = jnp.where(ln >= 64, acc / total, aux).astype(BF)
     r.o_out[v, 2 * i] = out[:128]
     r.o_out[v, 2 * i + 1] = out[128:]
-    for half in range(2):
+    for turn in range(2):
+        half = (turn + place.s) % 2
         place.send(
             r.o_out.at[v, 2 * i + half],
             r.o_in.at[v, 2 * place.head + place.s],
@@ -316,8 +325,8 @@
 def before_attention_back(v, r):
     dy = r.dy[...]
     n_two = r.n_two[v]
-    r.vec[2:3, :] += jnp.sum(dy * n_two, axis=0, keepdims=True)
-    r.vec[3:4, :] += jnp.sum(dy, axis=0, keepdims=True)
+    r.vec_own[2:3, :] += jnp.sum(dy * n_two, axis=0, keepdims=True)
+    r.vec_own[3:4, :] += jnp.sum(dy, axis=0, keepdims=True)
     grad_two = norm_back(dy, n_two, r.f_two[v][:, 0:1], r.gain_two[...])
     r.down_low[v] = grad_two.astype(BF)
     r.work[...] = grad_two
@@ -332,8 +341,8 @@
 
     dz = r.work[...]
     n_one = r.n_one[v]
-    r.vec[0:1, :] += jnp.sum(dz * n_one, axis=0, keepdims=True)
-    r.vec[1:2, :] += jnp.sum(dz, axis=0, keepdims=True)
+    r.vec_own[0:1, :] += jnp.sum(dz * n_one, axis=0, keepdims=True)
+    r.vec_own[1:2, :] += jnp.sum(dz, axis=0, keepdims=True)
     grad_one = norm_back(dz, n_one, r.f_one[v][:, 0:1], r.gain_one[...])
     out_low = grad_one.astype(BF)
     r.out_low[v] = out_low
@@ -356,14 +365,15 @@
 
 def send_do(v, r, place):
     @pl.loop(0, HEADS)
-    def _(h):
-        for core in range(2):
+    def _(a):
+        h = (place.own_slot // 2 + a) % 8
+        for b in range(2):
             place.send(
                 r.do_out.at[v, h],
                 r.do_in.at[v, place.own_slot],
                 r.sems.at[6, v],
                 r.sems.at[7, v],
-                core,
+                (place.me + b) % 2,
                 place.chip(h, place.own_t),
             )
 
@@ -398,7 +408,8 @@
     dq = jnp.transpose(jnp.concatenate([dqt, jnp.zeros((64, 256), F32)], axis=0)).astype(BF)
     r.dq_out[v, 2 * i] = dq[:128]
     r.dq_out[v, 2 * i + 1] = dq[128:]
-    for half in range(2):
+    for turn in range(2):
+        half = (turn + place.s) % 2
         place.send(
             r.dq_out.at[v, 2 * i + half],
             r.dq_in.at[v, 2 * place.head + place.s],
@@ -419,10 +430,16 @@
 
     @pl.loop(0, 8)
     def _(i):
-        bwd_tile(v, i, r, place)
+        bwd_tile(v, (i + place.head) % 8, r, place)
+        for after, step in SUM_DURING_BACK:
+
+            @pl.when((v == 0) & (i == after))
+            def _():
+                SUM_STEPS[step](0, r, place)
 
     @pl.loop(0, 32)
-    def _(n):
+    def _(k):
+        n = (k + 4 * place.head + place.t) % 32
         r.dkv_out[v, n] = r.dkv_acc[ds(n * 128, 128), :].astype(BF)
         place.send(
             r.dkv_out.at[v, n],
@@ -457,20 +474,261 @@
     return jnp.concatenate([ref[0], ref[1]], axis=0)
 
 
-def weight_grads(r):
-    hid = jnp.concatenate([r.hid[0], r.hid[1]], axis=0)
-    r.g_query[...] = tn(hid, both(r.dq))
-    r.g_key[...] = tn(hid, both(r.dk))
-    r.g_value[...] = tn(hid, both(r.dv))
-    r.g_out[...] = tn(both(r.att_low), both(r.out_low))
-
+def put(ref, unit, tile):
+    ref[ds(unit * 512, 512), :] = tile.astype(BF)
+
+
+def weight_grads_early(r):
     @pl.loop(0, 4)
     def _(j):
         cols = ds(j * 512, 512)
         up = jnp.concatenate([r.up_low[0, :, cols], r.up_low[1, :, cols]], axis=0)
-        r.g_up[:, cols] = tn(both(r.first_low), up)
+        grad = tn(both(r.first_low), up)
+        for k in range(4):
+            put(r.sum_in0, 4 * j + k, grad[:, 128 * k : 128 * k + 128])
         act = jnp.concatenate([r.act[0, :, cols], r.act[1, :, cols]], axis=0)
-        r.g_down[cols, :] = tn(act, both(r.down_low))
+        grad = tn(act, both(r.down_low))
+        for k in range(4):
+            put(r.sum_in0, 16 + 4 * k + j, grad[:, 128 * k : 128 * k + 128])
+
+    grad = tn(both(r.att_low), both(r.out_low))
+    for k in range(4):
+        put(r.sum_in0, 32 + k, grad[:, 128 * k : 128 * k + 128])
+
+
+def weight_grads_late(r):
+    hid = jnp.concatenate([r.hid[0], r.hid[1]], axis=0)
+    for i, ref in enumerate((r.dq, r.dk, r.dv)):
+        grad = tn(hid, both(ref))
+        for k in range(4):
+            put(r.sum_in1, 4 * i + k, grad[:, 128 * k : 128 * k + 128])
+
+
+SUM_ROWS = (3072, 1024)
+ORDERS = ((0, 1, 2), (1, 2, 0), (2, 0, 1))
+
+
+def sum_refs(g, r):
+    names = ("in", "x", "r0", "r1", "r2", "s0", "s1", "t", "sems")
+    return SimpleNamespace(**{n: getattr(r, "sum_" + n + str(g)) for n in names})
+
+
+def remote(src, dst, send_sem, recv_sem, section, dp):
+    pltpu.make_async_remote_copy(
+        src_ref=src,
+        dst_ref=dst,
+        send_sem=send_sem,
+        recv_sem=recv_sem,
+        device_id=(section, dp),
+        device_id_type=MESH,
+    ).start()
+
+
+def offsets(p, rows, place):
+    out, at = [], 0
+    for k in range(3):
+        at = at + place.coords[ORDERS[p][k]] * (rows // 4 ** (k + 1))
+        out.append(at)
+    return out
+
+
+def exchange_start(g, r, place):
+    q, rows = sum_refs(g, r), SUM_ROWS[g]
+    for p in range(3):
+        remote(
+            q.__dict__["in"].at[ds((1 - place.s) * 3 * rows + p * rows, rows)],
+            q.x.at[pl.ds(p * rows, rows)],
+            q.sems.at[0, 0, p],
+            q.sems.at[1, 0, p],
+            1 - place.s,
+            place.me,
+        )
+
+
+def scatter_send(g, p, k, src, base, q, place):
+    size = SUM_ROWS[g] // 4 ** (k + 1)
+    dst = (q.r0, q.r1, q.r2)[k]
+    axis = ORDERS[p][k]
+    for d in (2, 1, 3):
+        c = (place.coords[axis] + d) % 4
+        remote(
+            src.at[ds(base + c * size, size)],
+            dst.at[p, d - 1],
+            q.sems.at[0, 1 + k, p],
+            q.sems.at[1, 1 + k, p],
+            place.s,
+            place.along(axis, d),
+        )
+
+
+def exchange_done(g, r, place):
+    q, rows = sum_refs(g, r), SUM_ROWS[g]
+    src = q.__dict__["in"]
+    for p in range(3):
+        base = place.s * 3 * rows + p * rows
+        wait_all(q.x.at[pl.ds(p * rows, rows)], q.sems.at[1, 0, p])
+
+        @pl.loop(0, rows // 512)
+        def _(k):
+            at = ds(base + k * 512, 512)
+            other = q.x[ds(p * rows + k * 512, 512), :]
+            src[at, :] = (src[at, :].astype(F32) + other.astype(F32)).astype(BF)
+
+        scatter_send(g, p, 0, src, base, q, place)
+
+
+def scatter_done(k, g, r, place):
+    q, rows = sum_refs(g, r), SUM_ROWS[g]
+    size = rows // 4 ** (k + 1)
+    got = (q.r0, q.r1, q.r2)[k]
+    for p in range(3):
+        wait_all(got.at[p], q.sems.at[1, 1 + k, p])
+        c = place.coords[ORDERS[p][k]]
+        if k == 0:
+            own = q.__dict__["in"][ds(place.s * 3 * rows + p * rows + c * size, size), :]
+        else:
+            own = (q.s0, q.s1)[k - 1][p, ds(c * size, size), :]
+        total = own.astype(F32)
+        for d in range(3):
+            total = total + got[p, d].astype(F32)
+        if k < 2:
+            dst = (q.s0, q.s1)[k]
+            dst[p] = total.astype(BF)
+            scatter_send(g, p, k + 1, dst.at[p], 0, q, place)
+        else:
+            q.t[place.s, p, ds(offsets(p, rows, place)[2], size), :] = total.astype(BF)
+            gather_send(g, p, 2, q, place)
+
+
+def gather_send(g, p, k, q, place):
+    rows = SUM_ROWS[g]
+    size = rows // 4 ** (k + 1)
+    block = q.t.at[place.s, p, ds(offsets(p, rows, place)[k], size)]
+    axis = ORDERS[p][k]
+    for d in (2, 1, 3):
+        sem = 4 + k if k else 6 + d
+        remote(
+            block, block, q.sems.at[0, sem, p], q.sems.at[1, sem, p], place.s, place.along(axis, d)
+        )
+
+
+def cross_send(p, start, size, q, place):
+    block = q.t.at[place.s, p, ds(start, size)]
+    remote(block, block, q.sems.at[0, 4, p], q.sems.at[1, 4, p], 1 - place.s, place.me)
+
+
+def gather_done(k, g, r, place):
+    q, rows = sum_refs(g, r), SUM_ROWS[g]
+    for p in range(3):
+        wait_all(
+            q.t.at[0, p, pl.ds(0, 3 * rows // 4 ** (k + 1))],
+            q.sems.at[1, 4 + k, p],
+        )
+        gather_send(g, p, k - 1, q, place)
+        if k == 1:
+            cross_send(p, offsets(p, rows, place)[0], rows // 4, q, place)
+
+
+def gather_last(g, r, place):
+    q, rows = sum_refs(g, r), SUM_ROWS[g]
+    size = rows // 4
+    for d in (1, 3, 2):
+        for p in range(3):
+            wait_all(q.t.at[0, p, pl.ds(0, size)], q.sems.at[1, 6 + d, p])
+            c = (place.coords[ORDERS[p][0]] - d + 4) % 4
+            cross_send(p, c * size, size, q, place)
+
+
+def sum_out(g, r, place):
+    q = sum_refs(g, r)
+    for p in range(3):
+        wait_all(q.t.at[0, p], q.sems.at[1, 4, p])
+    pltpu.make_async_copy(q.t, (r.sums0, r.sums1)[g], r.vsems.at[2, g]).start()
+
+
+def sum_drain(g, r, place):
+    q, rows = sum_refs(g, r), SUM_ROWS[g]
+    for p in range(3):
+        wait_all(q.x.at[pl.ds(0, rows)], q.sems.at[0, 0, p])
+        for k in range(3):
+            wait_all(q.t.at[0, p, pl.ds(0, 3 * rows // 4 ** (k + 1))], q.sems.at[0, 1 + k, p])
+        for k in (1, 2):
+            wait_all(q.t.at[0, p, pl.ds(0, 3 * rows // 4 ** (k + 1))], q.sems.at[0, 4 + k, p])
+        for d in range(1, 4):
+            wait_all(q.t.at[0, p, pl.ds(0, rows // 4)], q.sems.at[0, 6 + d, p])
+        wait_all(q.t.at[0, p], q.sems.at[0, 4, p])
+    pltpu.make_async_copy(q.t, (r.sums0, r.sums1)[g], r.vsems.at[2, g]).wait()
+
+
+def vec_exchange(r, place):
+    remote(r.vec_own, r.vec_x, r.vsems.at[0, 0], r.vsems.at[1, 0], 1 - place.s, place.me)
+
+
+def vec_send(axis, r, place):
+    c = place.coords[axis]
+    for d in (1, 2, 3):
+        remote(
+            r.vec_in.at[axis, c],
+            r.vec_in.at[axis, c],
+            r.vsems.at[0, 1 + axis],
+            r.vsems.at[1, 1 + axis],
+            place.s,
+            place.along(axis, d),
+        )
+
+
+def vec_step(axis, r, place):
+    if axis == 0:
+        wait_all(r.vec_x, r.vsems.at[1, 0])
+        total = r.vec_own[...] + r.vec_x[...]
+    else:
+        wait_all(r.vec_in.at[axis - 1, pl.ds(0, 3)], r.vsems.at[1, axis])
+        total = (r.vec_in[axis - 1, 0] + r.vec_in[axis - 1, 1]) + (
+            r.vec_in[axis - 1, 2] + r.vec_in[axis - 1, 3]
+        )
+    if axis < 3:
+        r.vec_in[axis, place.coords[axis]] = total
+        vec_send(axis, r, place)
+    else:
+        r.vec[...] = total
+
+
+def vec_drain(r):
+    wait_all(r.vec_x, r.vsems.at[0, 0])
+    for axis in range(3):
+        wait_all(r.vec_in.at[axis, pl.ds(0, 3)], r.vsems.at[0, 1 + axis])
+
+
+def step_exchange(g, r, place):
+    exchange_start(g, r, place)
+    if g == 0:
+        vec_exchange(r, place)
+
+
+def step_scatter(g, r, place):
+    exchange_done(g, r, place)
+    if g == 0:
+        vec_step(0, r, place)
+
+
+def step_between(k, g, r, place):
+    scatter_done(k, g, r, place)
+    if g == 0:
+        vec_step(k + 1, r, place)
+
+
+SUM_STEPS = (
+    step_exchange,
+    step_scatter,
+    lambda *a: step_between(0, *a),
+    lambda *a: step_between(1, *a),
+    lambda *a: step_between(2, *a),
+    lambda *a: gather_done(2, *a),
+    lambda *a: gather_done(1, *a),
+    gather_last,
+    sum_out,
+)
+SUM_DURING_BACK = ((1, 1), (4, 2), (5, 3), (6, 4), (7, 5))
 
 
 INPUTS = ["inputs", "groups", "cotangent", "w_query", "w_key", "w_value", "w_out", "w_up", "w_down"]
@@ -478,12 +736,8 @@
 OUTPUTS = {
     "output": ((1, ROWS, D), BF),
     "input_grad": ((1, ROWS, D), BF),
-    "g_query": ((D, D), F32),
-    "g_key": ((D, D), F32),
-    "g_value": ((D, D), F32),
-    "g_out": ((D, D), F32),
-    "g_up": ((D, FF), F32),
-    "g_down": ((FF, D), F32),
+    "sums0": ((2, 3, 3072, 128), BF),
+    "sums1": ((2, 3, 1024, 128), BF),
     "vec": ((8, D), F32),
 }
 SCRATCH = {
@@ -525,17 +779,32 @@
     "dq": ((2, ROWS, D), BF),
     "dk": ((2, ROWS, D), BF),
     "dv": ((2, ROWS, D), BF),
+    "vec_own": ((8, D), F32),
+    "vec_x": ((8, D), F32),
+    "vec_in": ((3, 4, 8, D), F32),
 }
+for g, rows in enumerate(SUM_ROWS):
+    SCRATCH |= {
+        f"sum_in{g}": ((6 * rows, 128), BF),
+        f"sum_x{g}": ((3 * rows, 128), BF),
+        f"sum_r0{g}": ((3, 3, rows // 4, 128), BF),
+        f"sum_r1{g}": ((3, 3, rows // 16, 128), BF),
+        f"sum_r2{g}": ((3, 3, rows // 64, 128), BF),
+        f"sum_s0{g}": ((3, rows // 4, 128), BF),
+        f"sum_s1{g}": ((3, rows // 16, 128), BF),
+        f"sum_t{g}": ((2, 3, rows, 128), BF),
+    }
+SEMS = {"sems": (12, 2), "gsems": (2,), "sum_sems0": (2, 10, 3), "sum_sems1": (2, 10, 3), "vsems": (3, 4)}
 
 
 def kernel(*refs):
-    names = INPUTS + list(OUTPUTS) + list(SCRATCH) + ["sems", "gsems"]
+    names = INPUTS + list(OUTPUTS) + list(SCRATCH) + list(SEMS)
     r = SimpleNamespace(**dict(zip(names, refs)))
     place = Place()
     barrier(place)
     send_groups(r, place)
     make_own_aug(r, place)
-    r.vec[...] = jnp.zeros_like(r.vec)
+    r.vec_own[...] = jnp.zeros_like(r.vec_own)
     r.hid[0] = r.inputs[place.s]
 
     @pl.loop(0, 2)
@@ -554,7 +823,7 @@
 
         @pl.loop(0, 8)
         def _(i):
-            fwd_tile(v, i, r, place)
+            fwd_tile(v, (i + place.head) % 8, r, place)
 
         wait_all(r.o_in.at[v], r.sems.at[5, v])
         after_attention(v, r)
@@ -567,16 +836,37 @@
         v = 1 - step
         before_attention_back(v, r)
         send_do(v, r, place)
+
+        @pl.when(v == 0)
+        def _():
+            weight_grads_early(r)
+            SUM_STEPS[0](0, r, place)
+
         wait_all(r.do_in.at[v], r.sems.at[7, v])
         attention_back(v, r, place)
+
+        @pl.when(v == 0)
+        def _():
+            SUM_STEPS[6](0, r, place)
+
         wait_all(r.dq_in.at[v], r.sems.at[9, v])
         wait_all(r.dkv_in.at[v], r.sems.at[11, v])
         after_attention_back(v, r)
         r.dy[...] = r.work[...].astype(BF).astype(F32)
 
     r.input_grad[0] = r.dy[...].astype(BF)
-    weight_grads(r)
-
+    weight_grads_late(r)
+    SUM_STEPS[0](1, r, place)
+    SUM_STEPS[7](0, r, place)
+    for step in SUM_STEPS[1:5]:
+        step(1, r, place)
+    SUM_STEPS[8](0, r, place)
+    for step in SUM_STEPS[5:]:
+        step(1, r, place)
+
+    vec_drain(r)
+    for g in range(2):
+        sum_drain(g, r, place)
     wait_sent(r.grp_in, r.gsems.at[0], place.self_kv, 32)
 
     @pl.loop(0, 2)
@@ -596,17 +886,25 @@
         kernel,
         out_shape=[jax.ShapeDtypeStruct(shape, kind) for shape, kind in OUTPUTS.values()],
         in_specs=[vmem] * len(INPUTS),
-        out_specs=[vmem] * len(OUTPUTS),
+        out_specs=[
+            pl.BlockSpec(memory_space=pl.ANY) if n.startswith("sums") else vmem for n in OUTPUTS
+        ],
         scratch_shapes=[pltpu.VMEM(shape, kind) for shape, kind in SCRATCH.values()]
-        + [pltpu.SemaphoreType.DMA((12, 2)), pltpu.SemaphoreType.DMA((2,))],
+        + [pltpu.SemaphoreType.DMA(shape) for shape in SEMS.values()],
         compiler_params=pltpu.CompilerParams(
             collective_id=0, has_side_effects=True, vmem_limit_bytes=60 * 2**20
         ),
         name="visits",
     )(inputs, groups, cotangent, *params[:6], *vectors)
-    sums = lax.psum(tuple(out[2:]), ("section", "dp"))
-    vec = sums[6]
-    return (*out[:2], *sums[:6], vec[0], vec[1], vec[2], vec[3])
+    early, late = out[2].reshape(36, 512, 128), out[3].reshape(12, 512, 128)
+
+    def whole(tiles):
+        return tiles.transpose(1, 0, 2).reshape(tiles.shape[1], -1).astype(F32)
+
+    down = early[16:32].reshape(4, FF, 128)
+    grads = [whole(x) for x in (late[:4], late[4:8], late[8:], early[32:], early[:16], down)]
+    vec = out[4]
+    return (*out[:2], *grads, vec[0], vec[1], vec[2], vec[3])
 
 
 def solution(mesh):

time: 478 us -> 343 us (0.72)
  waiting for transfers between devices: 106 us -> 0 us
  blocking collectives: 77.3 us -> 0 us
  Pallas kernels: 266 us -> 320 us
  between operations: 14.1 us -> 0.7 us
    psum x1 -> x0, waiting for transfers between devices: 106 us -> none  [on_device(): sums = lax.psum(tuple(out[2:]), ('section', 'dp'))]
    psum x1 -> x0, blocking collectives: 77.3 us -> none  [on_device(): sums = lax.psum(tuple(out[2:]), ('section', 'dp'))]
    pallas_call x1, Pallas kernels: 266 us -> 320 us  [on_device(): pl.pallas_call(kernel, out_shape=[jax.ShapeDtypeStruct(shape, kind) for s...]
    convert_element_type x0 -> x3, local copies, waits for them, and re-layouts: none -> 13 us  [whole(): return tiles.transpose(1, 0, 2).reshape(tiles.shape[1], -1).astype(F32)]
    unnamed x22 -> x11, local copies, waits for them, and re-layouts: 14.3 us -> 3.78 us
  transfers between devices with their start and end apart: 1 -> 0, of which waited for: 1 -> 0; matrix products, arithmetic and copies ran while one was open for 0% -> 0% of each run, Pallas kernels for 0% -> 0%
where the time goes in v2:
time: 343 us
  Pallas kernels  320 us (93%)
  local copies, waits for them, and re-layouts  18.3 us (5%)
  other arithmetic  4.16 us (1%)
    pallas_call x1, Pallas kernels, on_device(): pl.pallas_call(kernel, out_shape=[jax.ShapeDtypeStruct(shape, kind) for s...  320 us
    convert_element_type x3, local copies, waits for them, and re-layouts, whole(): return tiles.transpose(1, 0, 2).reshape(tiles.shape[1], -1).astype(F32)  13 us

profile of v2, /device:TPU:1, one launch (start us, length us, event | category | flops | bytes accessed | tf_op | source)
XLA Modules:
  0.0 342.8 jit_solution(11159924947519354974)
XLA Ops:
  0.6 319.7 %visits.1 = (bf16[1,128,512]{2,1,0:T(8,128)(2,1)}, bf16[1,128,512]{2,1,0:T(8,128)(2,1)}, bf16[2,3,3072,128]{3,2,1,0:T(8,128)(2,1)}, bf16[2,3,1024,128]{3,2,1,0:T(8,128)(2,1)}, f32[8,512]{1,0:T(8,128)}) custom-call(bf16[2,128,512]{2,1,0:T(8,128)(2,1)} %refs_0_.1, s32[2,128]{1,0:T(2,128)} %refs_1_.1, bf16[2,128,512]{2,1,0:T(8,128)(2,1)} %refs_2_.1, ...), custom_call_target="tpu_custom_call" | custom-call | tf_op jit(solution)/shard_map/visits/pallas_call | solution.py:885
  320.3 1.5 fusion.1
  321.8 0.0 slice-start
  321.8 0.0 slice-start.1
  321.8 1.8 convert_bitcast_fusion.2
  323.6 1.6 copy_bitcast_fusion.3
  325.2 0.0 slice-done
  325.2 0.0 slice-done.1
  325.2 1.6 copy_bitcast_fusion.2
  326.8 0.5 fusion
  327.3 0.3 bitcast_convert_fusion
  327.6 8.9 %copy.30 = f32[4,2048,128]{2,0,1:T(4,128)S(1)} copy(f32[4,2048,128]{2,1,0:T(8,128)S(1)} %bitcast_convert_fusion) | data formatting | bytes 8388608 | tf_op jit(solution)/shard_map/convert_element_type | solution.py:902
  336.5 2.5 copy.43
  338.9 0.0 copy-start.1
  338.9 0.0 copy-start
  338.9 2.6 copy.44
  341.5 0.0 copy-done.1
  341.5 0.7 copy.47
  342.2 0.0 copy-done
  342.2 0.7 copy.48
  (1 shorter events, 0.0 us)
Async XLA Ops:
  321.8 3.4 slice-start
  321.8 3.4 slice-start.1
  338.9 2.6 copy-start.1
  338.9 3.2 copy-start

commit v3 on v2

--- a/solution.py
+++ b/solution.py
@@ -11,7 +11,7 @@
 BIG = 1e30
 ROWS, D, FF, HEADS = 128, 512, 2048, 8
 MESH = pl.DeviceIdType.MESH
-FWD_C, BWD_C = 8, 4
+BWD_C = 4
 
 
 def nt(a, b):
@@ -47,7 +47,7 @@
 
 
 def tile_of(r, t):
-    return 8 * (r // 2) + jnp.where(r % 2 == 0, t, 7 - t)
+    return 4 * r + (r + t) % 4
 
 
 def mean(x):
@@ -84,13 +84,12 @@
         self.s = lax.axis_index("section")
         me = self.me
         self.coords = (me % 4, me // 16, (me // 4) % 4)
-        self.t = me % 4
-        self.head = (me // 4) % 8
-        self.micro = me // 32
-        w = (me // 2) % 8
-        low = w < 4
-        self.own_t = jnp.where(low, w, 7 - w)
-        self.own_slot = 4 * (me // 16) + jnp.where(low, 0, 2) + me % 2
+        x, y, z = self.coords
+        self.t = (x + y + z) % 4
+        self.head = 4 * (y % 2) + x
+        self.micro = y // 2
+        self.own_t = ((me // 2) % 4 - me // 8 + 32) % 4
+        self.own_slot = 2 * (me // 8) + me % 2
         mine = self.micro == self.s
         self.self_kv = mine & (me % 2 == self.s)
         self.self_q = mine & (self.own_t == self.t)
@@ -100,7 +99,8 @@
         return self.me + ((c + d) % 4 - c) * (1, 16, 4)[axis]
 
     def chip(self, h, t):
-        return (self.s * 8 + h) * 4 + t
+        x, y = h % 4, 2 * self.s + h // 4
+        return 16 * y + 4 * ((t - x - y + 8) % 4) + x
 
     def send(self, src, dst, send_sem, recv_sem, section, dp):
         to_self = (section == self.s) & (dp == self.me)
@@ -178,7 +178,7 @@
                 place.me % 2,
                 place.chip(h, (place.me // 2 + b) % 4),
             )
-        h = (place.own_slot // 2 + a) % 8
+        h = (place.me // 4 + a) % 8
         for b in range(2):
             place.send(
                 r.q_out.at[v, h],
@@ -225,7 +225,9 @@
         g = column_of(r.grp_in[n][0:1, :]).astype(jnp.int32)
         inside = (ln >= 64) & (ln < 68)
         aug = jnp.where(inside, jnp.where(ln - 64 == g, 0.0, -BIG), 0.0)
-        r.key_aug[n] = jnp.where((ln >= 68) & (ln < 71), 1.0, aug).astype(BF)
+        aug = jnp.where((ln >= 68) & (ln < 71), 1.0, aug).astype(BF)
+        for v in range(2):
+            r.ka[v, ds(n * 128, 128), :] = aug
 
 
 def make_kv(v, r):
@@ -237,48 +239,49 @@
     def _(n):
         rows = ds(n * 128, 128)
         kv = r.kv_in[v, n].astype(F32)
-        r.ka[v, rows, :] = jnp.where(low, kv, r.key_aug[n].astype(F32)).astype(BF)
+        r.ka[v, rows, :] = jnp.where(low, kv, r.ka[v, rows, :].astype(F32)).astype(BF)
         r.va[v, rows, :] = jnp.where(low, ones, kv).astype(BF)
 
 
-def fwd_tile(v, i, r, place):
-    width = FWD_C * 128
-    u = tile_of(i, place.t)
-    q = jnp.concatenate([r.q_in[v, 2 * i], r.q_in[v, 2 * i + 1]], axis=0)
+def fwd_pair(v, j, r, place):
+    width = 1024
+    tiles = [tile_of(2 * j + k, place.t) for k in range(2)]
+    q = jnp.concatenate([r.q_in[v, 4 * j + k] for k in range(4)], axis=0)
 
     def step(c, carry, masked):
         top, acc = carry
         rows = ds(c * width, width)
         sc = nt(q, r.ka[v, rows, :])
         if masked:
-            col, row = lanes((256, width)), subs((256, width))
-            at = 256 * (col // 128) + col % 128 + (256 * FWD_C * c + 128 * place.s - 256 * u)
-            sc = jnp.where(at <= row, sc, -BIG)
+            col, row = lanes((512, width)), subs((512, width))
+            at = 256 * (col // 128) + col % 128 + (2048 * c + 128 * place.s)
+            limit = row % 256 + 256 * jnp.where(row < 256, tiles[0], tiles[1])
+            sc = jnp.where(at <= limit, sc, -BIG)
         new = jnp.maximum(top, jnp.max(sc, axis=1, keepdims=True))
         p = jnp.exp(sc - new).astype(BF)
         return new, acc * jnp.exp(top - new) + nn(p, r.va[v, rows, :])
 
-    start = (jnp.full((256, 1), -2 * BIG, F32), jnp.zeros((256, 128), F32))
-    full = u // FWD_C
-    carry = lax.fori_loop(0, full, lambda c, x: step(c, x, False), start)
-    top, acc = step(full, carry, True)
+    start = (jnp.full((512, 1), -2 * BIG, F32), jnp.zeros((512, 128), F32))
+    carry = lax.fori_loop(0, j, lambda c, x: step(c, x, False), start)
+    top, acc = step(j, carry, True)
     total = acc[:, 0:1]
     a, b, c = split3(top + jnp.log(total))
-    ln = lanes((256, 128))
+    ln = lanes((512, 128))
     aux = jnp.where(ln == 0, a, jnp.where(ln == 1, b, jnp.where(ln == 2, c, 0.0)))
     out = jnp.where(ln >= 64, acc / total, aux).astype(BF)
-    r.o_out[v, 2 * i] = out[:128]
-    r.o_out[v, 2 * i + 1] = out[128:]
-    for turn in range(2):
-        half = (turn + place.s) % 2
-        place.send(
-            r.o_out.at[v, 2 * i + half],
-            r.o_in.at[v, 2 * place.head + place.s],
-            r.sems.at[4, v],
-            r.sems.at[5, v],
-            place.micro,
-            2 * u + half,
-        )
+    for k in range(4):
+        r.o_out[v, 4 * j + k] = out[128 * k : 128 * k + 128]
+    for k in range(2):
+        for turn in range(2):
+            half = (turn + place.s) % 2
+            place.send(
+                r.o_out.at[v, 4 * j + 2 * k + half],
+                r.o_in.at[v, 2 * place.head + place.s],
+                r.sems.at[4, v],
+                r.sems.at[5, v],
+                place.micro,
+                2 * tiles[k] + half,
+            )
 
 
 def after_attention(v, r):
@@ -366,7 +369,7 @@
 def send_do(v, r, place):
     @pl.loop(0, HEADS)
     def _(a):
-        h = (place.own_slot // 2 + a) % 8
+        h = (place.me // 4 + a) % 8
         for b in range(2):
             place.send(
                 r.do_out.at[v, h],
@@ -437,12 +440,16 @@
             def _():
                 SUM_STEPS[step](0, r, place)
 
+    @pl.when(v == 0)
+    def _():
+        wait_sent(r.dkv_in.at[1], r.sems.at[10, 1], place.self_kv, 32)
+
     @pl.loop(0, 32)
     def _(k):
         n = (k + 4 * place.head + place.t) % 32
-        r.dkv_out[v, n] = r.dkv_acc[ds(n * 128, 128), :].astype(BF)
+        r.dkv_out[n] = r.dkv_acc[ds(n * 128, 128), :].astype(BF)
         place.send(
-            r.dkv_out.at[v, n],
+            r.dkv_out.at[n],
             r.dkv_in.at[v, 4 * place.head + place.t],
             r.sems.at[10, v],
             r.sems.at[11, v],
@@ -749,7 +756,6 @@
     "kv_in": ((2, 32, ROWS, 128), BF),
     "grp_out": ((1, 8, 128), jnp.int32),
     "grp_in": ((32, 8, 128), jnp.int32),
-    "key_aug": ((32, ROWS, 128), BF),
     "ka": ((2, 4096, 128), BF),
     "va": ((2, 4096, 128), BF),
     "kat": ((64, 4096), BF),
@@ -774,7 +780,7 @@
     "dq_out": ((2, 16, ROWS, 128), BF),
     "dq_in": ((2, 16, ROWS, 128), BF),
     "dkv_acc": ((4096, 128), F32),
-    "dkv_out": ((2, 32, ROWS, 128), BF),
+    "dkv_out": ((32, ROWS, 128), BF),
     "dkv_in": ((2, 32, ROWS, 128), BF),
     "dq": ((2, ROWS, D), BF),
     "dk": ((2, ROWS, D), BF),
@@ -821,9 +827,9 @@
         make_kv(v, r)
         wait_all(r.q_in.at[v], r.sems.at[3, v])
 
-        @pl.loop(0, 8)
-        def _(i):
-            fwd_tile(v, (i + place.head) % 8, r, place)
+        @pl.loop(0, 4)
+        def _(j):
+            fwd_pair(v, (j + place.head) % 4, r, place)
 
         wait_all(r.o_in.at[v], r.sems.at[5, v])
         after_attention(v, r)
@@ -876,7 +882,64 @@
         wait_sent(r.o_in.at[v], r.sems.at[4, v], place.self_q, 16)
         wait_sent(r.do_in.at[v], r.sems.at[6, v], place.self_q, 16)
         wait_sent(r.dq_in.at[v], r.sems.at[8, v], place.self_q, 16)
-        wait_sent(r.dkv_in.at[v], r.sems.at[10, v], place.self_kv, 32)
+
+    wait_sent(r.dkv_in.at[0], r.sems.at[10, 0], place.self_kv, 32)
+
+
+def unpack(early, late):
+    def body(early, late, query, key, value, out, up, down, got, small, up_f, down_f, sin, sout):
+        loads = []
+        for j in range(12):
+            src = late.at[pl.ds(4 * j, 4)] if j < 3 else early.at[pl.ds(4 * (j - 3), 4)]
+            loads.append(pltpu.make_async_copy(src, got.at[pl.ds(4 * j, 4)], sin.at[j]))
+        order = [0, 1, 2, 11, 3, 4, 5, 6, 7, 8, 9, 10]
+        for j in order:
+            loads[j].start()
+        stores = []
+
+        def store(j, src, dst):
+            stores.append(pltpu.make_async_copy(src, dst, sout.at[j]))
+            stores[-1].start()
+
+        for j in order:
+            loads[j].wait()
+            tiles = [got[4 * j + k].astype(F32) for k in range(4)]
+            cols = [slice(128 * k, 128 * k + 128) for k in range(4)]
+            if j < 3 or j == 11:
+                i = min(j, 3)
+                for k in range(4):
+                    small[i, :, cols[k]] = tiles[k]
+                store(j, small.at[i], (query, key, value, out)[i])
+            elif j < 7:
+                at = 512 * (j - 3)
+                for k in range(4):
+                    up_f[:, at + 128 * k : at + 128 * k + 128] = tiles[k]
+                store(j, up_f.at[:, pl.ds(at, 512)], up.at[:, pl.ds(at, 512)])
+            else:
+                for k in range(4):
+                    down_f[512 * k : 512 * k + 512, cols[j - 7]] = tiles[k]
+        store(7, down_f, down)
+        for copy in stores:
+            copy.wait()
+
+    square, hbm = jax.ShapeDtypeStruct((D, D), F32), pl.BlockSpec(memory_space=pl.ANY)
+    shapes = [square] * 4 + [jax.ShapeDtypeStruct((D, FF), F32), jax.ShapeDtypeStruct((FF, D), F32)]
+    return pl.pallas_call(
+        body,
+        out_shape=shapes,
+        in_specs=[hbm] * 2,
+        out_specs=[hbm] * 6,
+        scratch_shapes=[
+            pltpu.VMEM((48, 512, 128), BF),
+            pltpu.VMEM((4, D, D), F32),
+            pltpu.VMEM((D, FF), F32),
+            pltpu.VMEM((FF, D), F32),
+            pltpu.SemaphoreType.DMA((12,)),
+            pltpu.SemaphoreType.DMA((12,)),
+        ],
+        compiler_params=pltpu.CompilerParams(vmem_limit_bytes=40 * 2**20),
+        name="unpack",
+    )(early, late)
 
 
 def on_device(inputs, groups, cotangent, *params):
@@ -892,17 +955,11 @@
         scratch_shapes=[pltpu.VMEM(shape, kind) for shape, kind in SCRATCH.values()]
         + [pltpu.SemaphoreType.DMA(shape) for shape in SEMS.values()],
         compiler_params=pltpu.CompilerParams(
-            collective_id=0, has_side_effects=True, vmem_limit_bytes=60 * 2**20
+            collective_id=0, has_side_effects=True, vmem_limit_bytes=62 * 2**20
         ),
         name="visits",
     )(inputs, groups, cotangent, *params[:6], *vectors)
-    early, late = out[2].reshape(36, 512, 128), out[3].reshape(12, 512, 128)
-
-    def whole(tiles):
-        return tiles.transpose(1, 0, 2).reshape(tiles.shape[1], -1).astype(F32)
-
-    down = early[16:32].reshape(4, FF, 128)
-    grads = [whole(x) for x in (late[:4], late[4:8], late[8:], early[32:], early[:16], down)]
+    grads = unpack(out[2].reshape(36, 512, 128), out[3].reshape(12, 512, 128))
     vec = out[4]
     return (*out[:2], *grads, vec[0], vec[1], vec[2], vec[3])
 

time: 343 us -> 272 us (0.79)
  Pallas kernels: 320 us -> 264 us
  local copies, waits for them, and re-layouts: 18.3 us -> 6.53 us
  other arithmetic: 4.16 us -> 0 us
    pallas_call x1, Pallas kernels: 320 us -> 259 us  [on_device(): pl.pallas_call(kernel, out_shape=[jax.ShapeDtypeStruct(shape, kind) for s...]
    convert_element_type x3 -> x0, local copies, waits for them, and re-layouts: 13 us -> none  [whole(): return tiles.transpose(1, 0, 2).reshape(tiles.shape[1], -1).astype(F32)]
    pallas_call x0 -> x1, Pallas kernels: none -> 5.43 us  [unpack(): pl.pallas_call(body, out_shape=shapes, in_specs=[hbm] * 2, out_specs=[hbm...]
where the time goes in v3:
time: 272 us; the launch traced here: 271 us
  Pallas kernels  264 us (97%)
  local copies, waits for them, and re-layouts  6.53 us (2%)
    pallas_call x1, Pallas kernels, on_device(): pl.pallas_call(kernel, out_shape=[jax.ShapeDtypeStruct(shape, kind) for s...  259 us

profile of v3, /device:TPU:1, one launch (start us, length us, event | category | flops | bytes accessed | tf_op | source)
XLA Modules:
  0.0 271.4 jit_solution(6673996877336588978)
XLA Ops:
  0.6 258.8 %visits.1 = (bf16[1,128,512]{2,1,0:T(8,128)(2,1)}, bf16[1,128,512]{2,1,0:T(8,128)(2,1)}, bf16[2,3,3072,128]{3,2,1,0:T(8,128)(2,1)}, bf16[2,3,1024,128]{3,2,1,0:T(8,128)(2,1)}, f32[8,512]{1,0:T(8,128)}) custom-call(bf16[2,128,512]{2,1,0:T(8,128)(2,1)} %refs_0_.1, s32[2,128]{1,0:T(2,128)} %refs_1_.1, bf16[2,128,512]{2,1,0:T(8,128)(2,1)} %refs_2_.1, ...), custom_call_target="tpu_custom_call" | custom-call | tf_op jit(solution)/shard_map/visits/pallas_call | solution.py:948
  259.5 1.5 fusion
  260.9 0.0 copy-start
  260.9 2.3 copy-done
  263.3 0.0 copy-start.1
  263.3 1.4 copy-done.1
  264.7 0.0 copy-start.3
  264.7 0.0 copy-start.2
  264.7 5.4 %unpack.1 = (f32[512,512]{1,0:T(8,128)}, f32[512,512]{1,0:T(8,128)}, f32[512,512]{1,0:T(8,128)}, f32[512,512]{1,0:T(8,128)}, f32[512,2048]{1,0:T(8,128)}, /*index=5*/f32[2048,512]{1,0:T(8,128)}) custom-call(bf16[36,512,128]{2,1,0:T(8,128)(2,1)S(1)} %bitcast.10, bf16[12,512,128]{2,1,0:T(8,128)(2,1)S(1)} %bitcast.11), custom_call_target="tpu_custom_call" | custom-call | tf_op jit(solution)/shard_map/unpack/pallas_call | solution.py:927
  270.1 0.0 copy-done.3
  270.1 0.7 copy.27
  270.8 0.0 copy-done.2
  270.8 0.7 copy.28
Async XLA Ops:
  260.9 2.3 copy-start
  263.3 1.4 copy-start.1
  264.7 5.4 %copy-start.3 = (bf16[1,128,512]{2,1,0:T(8,128)(2,1)S(1)}, bf16[1,128,512]{2,1,0:T(8,128)(2,1)}, u32[]{:S(2)}) copy-start(bf16[1,128,512]{2,1,0:T(8,128)(2,1)} %get-tuple-element.50) | copy-start | bytes 393220
  264.7 6.1 %copy-start.2 = (bf16[1,128,512]{2,1,0:T(8,128)(2,1)S(1)}, bf16[1,128,512]{2,1,0:T(8,128)(2,1)}, u32[]{:S(2)}) copy-start(bf16[1,128,512]{2,1,0:T(8,128)(2,1)} %get-tuple-element.51) | copy-start | bytes 393220

commit v4 on v3

--- a/solution.py
+++ b/solution.py
@@ -11,7 +11,6 @@
 BIG = 1e30
 ROWS, D, FF, HEADS = 128, 512, 2048, 8
 MESH = pl.DeviceIdType.MESH
-BWD_C = 4
 
 
 def nt(a, b):
@@ -135,7 +134,7 @@
         wait_all(ref.at[pl.ds(0, count)], sem)
 
 
-def barrier(place):
+def greet(place):
     sem = pltpu.get_barrier_semaphore()
 
     @pl.loop(1, 128)
@@ -143,134 +142,182 @@
         other = (place.s * 64 + place.me + k) % 128
         pl.semaphore_signal(sem, inc=1, device_id=(other // 64, other % 64), device_id_type=MESH)
 
-    pl.semaphore_wait(sem, 127)
-
-
-def project(v, r):
+
+def all_here():
+    pl.semaphore_wait(pltpu.get_barrier_semaphore(), 127)
+
+
+LOADED = ["hid", "w_query", "w_key", "w_value", "w_out", "w_up", "w_down", "cot"]
+
+
+def load(name, r, place):
+    if name == "hid":
+        return pltpu.make_async_copy(r.inputs.at[place.s], r.hid.at[0], r.load_sems.at[0])
+    if name == "cot":
+        return pltpu.make_async_copy(r.cotangent.at[place.s], r.cot, r.load_sems.at[7])
+    return pltpu.make_async_copy(
+        getattr(r, name + "_hbm"), getattr(r, name), r.load_sems.at[LOADED.index(name)]
+    )
+
+
+def pack(tile, odd):
+    low = lanes((64, 128)) < 64
+    if odd:
+        return jnp.where(low, pltpu.roll(tile[:64], 64, 1), tile[64:])
+    return jnp.where(low, tile[:64], pltpu.roll(tile[64:], 64, 1))
+
+
+def spread(packed, odd):
+    turned = pltpu.roll(packed, 64, 1)
+    return jnp.concatenate([turned, packed] if odd else [packed, turned], axis=0)
+
+
+def parts_in_rows(rows):
+    at = subs((16, 128))
+    out = jnp.zeros((16, 128), F32)
+    for i, part in enumerate(rows):
+        out = jnp.where(at == i, part, out)
+    return out.astype(BF)
+
+
+def project_queries(v, r):
+    q = nn(r.hid[v], r.w_query[...]).astype(BF).astype(F32) * 0.125
+    for h in range(HEADS):
+        tile = q[:, 128 * (h // 2) : 128 * (h // 2) + 128]
+        r.q_out[v, h] = pack(tile, h % 2 == 1).astype(BF)
+
+
+def project_keys_values(v, r):
     hid = r.hid[v]
-    q = nn(hid, r.w_query[...]).astype(BF).astype(F32) * 0.125
     k = nn(hid, r.w_key[...]).astype(BF).astype(F32)
     w = nn(hid, r.w_value[...]).astype(BF).astype(F32)
-    ln = lanes((ROWS, 128))
-    low = ln < 64
-    aug = r.own_aug[...]
+    low = lanes((ROWS, 128)) < 64
     for h in range(HEADS):
         cols = slice(128 * (h // 2), 128 * (h // 2) + 128)
-        qt, kt, vt = q[:, cols], k[:, cols], w[:, cols]
+        kt, vt = k[:, cols], w[:, cols]
         if h % 2 == 0:
             vt = pltpu.roll(vt, 64, 1)
         else:
-            qt, kt = pltpu.roll(qt, 64, 1), pltpu.roll(kt, 64, 1)
-        r.q_out[v, h] = jnp.where(low, qt, aug).astype(BF)
+            kt = pltpu.roll(kt, 64, 1)
         r.kv_out[v, h] = jnp.where(low, kt, vt).astype(BF)
 
 
-def send_qkv(v, r, place):
+def to_queries(src, dst, send_sem, recv_sem, place):
     @pl.loop(0, HEADS)
     def _(a):
-        h = (place.me // 8 + a) % 8
-        for b in range(4):
-            place.send(
-                r.kv_out.at[v, h],
-                r.kv_in.at[v, place.me // 2],
-                r.sems.at[0, v],
-                r.sems.at[1, v],
-                place.me % 2,
-                place.chip(h, (place.me // 2 + b) % 4),
-            )
         h = (place.me // 4 + a) % 8
         for b in range(2):
-            place.send(
-                r.q_out.at[v, h],
-                r.q_in.at[v, place.own_slot],
-                r.sems.at[2, v],
-                r.sems.at[3, v],
-                (place.me + b) % 2,
-                place.chip(h, place.own_t),
-            )
+            core, chip = (place.me + b) % 2, place.chip(h, place.own_t)
+            place.send(src(h), dst.at[place.own_slot], send_sem, recv_sem, core, chip)
+
+
+def to_keys(src, dst, send_sem, recv_sem, place):
+    n = place.me // 2
+
+    @pl.loop(0, HEADS)
+    def _(a):
+        h = 2 * ((n // 8 + a // 2) % 4) + (n // 4 + a) % 2
+        for b in range(4):
+            chip = place.chip(h, (n + b) % 4)
+            place.send(src(h), dst.at[n], send_sem, recv_sem, place.me % 2, chip)
+
+
+def send_queries(v, r, place):
+    to_queries(
+        lambda h: r.q_out.at[v, h], r.q_in.at[v], r.sems.at[2, v], r.sems.at[3, v], place
+    )
+
+
+def send_keys_values(v, r, place):
+    to_keys(
+        lambda h: r.kv_out.at[v, h],
+        r.kv_in.at[v],
+        r.sems.at[0, v],
+        r.kv_sems.at[v, place.me // 16],
+        place,
+    )
 
 
 def send_groups(r, place):
     r.grp_out[0] = jnp.broadcast_to(r.groups[pl.ds(place.s, 1), :], (8, 128))
-
-    @pl.loop(0, HEADS)
-    def _(a):
-        h = (place.me // 8 + a) % 8
-        for b in range(4):
-            place.send(
-                r.grp_out.at[0],
-                r.grp_in.at[place.me // 2],
-                r.gsems.at[0],
-                r.gsems.at[1],
-                place.me % 2,
-                place.chip(h, (place.me // 2 + b) % 4),
-            )
+    to_queries(lambda h: r.grp_out.at[0], r.grp_q, r.gsems.at[2], r.gsems.at[3], place)
+    to_keys(lambda h: r.grp_out.at[0], r.grp_in, r.gsems.at[0], r.gsems.at[1], place)
 
 
 def column_of(row):
     return jnp.transpose(jnp.broadcast_to(row.astype(F32), (128, 128)))
 
 
-def make_own_aug(r, place):
+def make_aug(r):
     ln = lanes((ROWS, 128))
-    g = column_of(r.groups[pl.ds(place.s, 1), :]).astype(jnp.int32)
-    r.own_aug[...] = jnp.where(ln - 64 == g, 1.0, 0.0)
-
-
-def make_key_aug(r):
-    ln = lanes((ROWS, 128))
+    inside = (ln >= 64) & (ln < 68)
 
     @pl.loop(0, 32)
     def _(n):
         g = column_of(r.grp_in[n][0:1, :]).astype(jnp.int32)
-        inside = (ln >= 64) & (ln < 68)
-        aug = jnp.where(inside, jnp.where(ln - 64 == g, 0.0, -BIG), 0.0)
-        aug = jnp.where((ln >= 68) & (ln < 71), 1.0, aug).astype(BF)
+        aug = jnp.where(inside & (ln - 64 != g), -BIG, 0.0).astype(BF)
         for v in range(2):
             r.ka[v, ds(n * 128, 128), :] = aug
 
-
-def make_kv(v, r):
+    @pl.loop(0, 16)
+    def _(n):
+        g = column_of(r.grp_q[n][0:1, :]).astype(jnp.int32)
+        aug = jnp.where(ln - 64 == g, 1.0, 0.0).astype(BF)
+        for v in range(2):
+            r.lq[v, ds(n * 128, 128), :] = aug
+
+
+def make_queries(v, r):
+    low = lanes((ROWS, 128)) < 64
+
+    @pl.loop(0, 16)
+    def _(n):
+        rows = ds(n * 128, 128)
+        q = spread(r.q_in[v, n].astype(F32), False)
+        r.lq[v, rows, :] = jnp.where(low, q, r.lq[v, rows, :].astype(F32)).astype(BF)
+
+
+def make_kv(v, c, r):
     ln = lanes((ROWS, 128))
     low = ln < 64
-    ones = jnp.where(ln < 3, 1.0, 0.0)
-
-    @pl.loop(0, 32)
-    def _(n):
+    ones = jnp.where(ln < 1, 1.0, 0.0)
+
+    @pl.loop(0, 8)
+    def _(k):
+        n = 8 * c + k
         rows = ds(n * 128, 128)
         kv = r.kv_in[v, n].astype(F32)
         r.ka[v, rows, :] = jnp.where(low, kv, r.ka[v, rows, :].astype(F32)).astype(BF)
         r.va[v, rows, :] = jnp.where(low, ones, kv).astype(BF)
 
 
-def fwd_pair(v, j, r, place):
+def fwd_body(v, c, j, masked, r, place):
     width = 1024
-    tiles = [tile_of(2 * j + k, place.t) for k in range(2)]
-    q = jnp.concatenate([r.q_in[v, 4 * j + k] for k in range(4)], axis=0)
-
-    def step(c, carry, masked):
-        top, acc = carry
-        rows = ds(c * width, width)
-        sc = nt(q, r.ka[v, rows, :])
-        if masked:
-            col, row = lanes((512, width)), subs((512, width))
-            at = 256 * (col // 128) + col % 128 + (2048 * c + 128 * place.s)
-            limit = row % 256 + 256 * jnp.where(row < 256, tiles[0], tiles[1])
-            sc = jnp.where(at <= limit, sc, -BIG)
-        new = jnp.maximum(top, jnp.max(sc, axis=1, keepdims=True))
-        p = jnp.exp(sc - new).astype(BF)
-        return new, acc * jnp.exp(top - new) + nn(p, r.va[v, rows, :])
-
-    start = (jnp.full((512, 1), -2 * BIG, F32), jnp.zeros((512, 128), F32))
-    carry = lax.fori_loop(0, j, lambda c, x: step(c, x, False), start)
-    top, acc = step(j, carry, True)
+    rows = ds(c * width, width)
+    sc = nt(r.lq[v, ds(512 * j, 512), :], r.ka[v, rows, :])
+    if masked:
+        col, row = lanes((512, width)), subs((512, width))
+        tiles = [tile_of(2 * j + k, place.t) for k in range(2)]
+        at = 256 * (col // 128) + col % 128 + (2048 * c + 128 * place.s)
+        limit = row % 256 + 256 * jnp.where(row < 256, tiles[0], tiles[1])
+        sc = jnp.where(at <= limit, sc, -BIG)
+    top = r.f_top[j][:, 0:1]
+    new = jnp.maximum(top, jnp.max(sc, axis=1, keepdims=True))
+    p = jnp.exp(sc - new).astype(BF)
+    r.f_acc[j] = r.f_acc[j] * jnp.exp(top - new) + nn(p, r.va[v, rows, :])
+    r.f_top[j] = jnp.broadcast_to(new, (512, 128))
+
+
+def fwd_finish(v, j, r, place):
+    acc = r.f_acc[j]
     total = acc[:, 0:1]
-    a, b, c = split3(top + jnp.log(total))
-    ln = lanes((512, 128))
-    aux = jnp.where(ln == 0, a, jnp.where(ln == 1, b, jnp.where(ln == 2, c, 0.0)))
-    out = jnp.where(ln >= 64, acc / total, aux).astype(BF)
+    out = acc / total
+    logs = jnp.broadcast_to(r.f_top[j][:, 0:1] + jnp.log(total), (512, 128))
     for k in range(4):
-        r.o_out[v, 4 * j + k] = out[128 * k : 128 * k + 128]
+        rows = slice(128 * k, 128 * k + 128)
+        r.o_out[v, 4 * j + k, 0:64] = pack(out[rows], True).astype(BF)
+        row = jnp.transpose(logs[rows])[0:1]
+        r.o_out[v, 4 * j + k, 64:80] = parts_in_rows(split3(row))
     for k in range(2):
         for turn in range(2):
             half = (turn + place.s) % 2
@@ -280,26 +327,61 @@
                 r.sems.at[4, v],
                 r.sems.at[5, v],
                 place.micro,
-                2 * tiles[k] + half,
+                2 * tile_of(2 * j + k, place.t) + half,
             )
 
 
+def attention(v, r, place):
+    r.f_acc[...] = jnp.zeros_like(r.f_acc)
+    r.f_top[...] = jnp.full_like(r.f_top, -2 * BIG)
+
+    @pl.loop(0, 4)
+    def _(a):
+        c = (place.head // 2 + 4 - a) % 4
+
+        @pl.loop(0, jnp.where(a == 3, c, 0))
+        def _(j):
+            fwd_finish(v, j, r, place)
+
+        wait_all(r.kv_in.at[v, ds(8 * c, 8)], r.kv_sems.at[v, c])
+        make_kv(v, c, r)
+        fwd_body(v, c, c, True, r, place)
+
+        @pl.when(a == 3)
+        def _():
+            fwd_finish(v, c, r, place)
+
+        @pl.loop(c + 1, 4)
+        def _(j):
+            fwd_body(v, c, j, False, r, place)
+
+            @pl.when(a == 3)
+            def _():
+                fwd_finish(v, j, r, place)
+
+
 def after_attention(v, r):
-    ln = lanes((ROWS, 128))
-    low = ln < 64
-    att = []
+    low = lanes((ROWS, 128)) < 64
+    weights = [[], []]
     for h in range(HEADS):
-        parts = [r.o_in[v, 2 * h + core].astype(F32) for core in range(2)]
-        logs = [x[:, 0:1] + x[:, 1:2] + x[:, 2:3] for x in parts]
+        logs = []
+        for core in range(2):
+            x = r.o_in[v, 2 * h + core, 64:80].astype(F32)
+            logs.append(x[0:1] + x[1:2] + x[2:3])
         top = jnp.maximum(logs[0], logs[1])
-        weights = [jnp.exp(x - top) for x in logs]
-        total = weights[0] + weights[1]
-        whole = (parts[0] * weights[0] + parts[1] * weights[1]) / total
-        log_total = top + jnp.log(total)
-        r.att[v, h] = jnp.where(low, jnp.where(ln == 0, log_total, 0.0), whole)
-        att.append(whole)
+        w = [jnp.exp(x - top) for x in logs]
+        total = w[0] + w[1]
+        r.log_total[v, h : h + 1] = top + jnp.log(total)
+        for core in range(2):
+            weights[core].append(w[core] / total)
+    cols = jnp.transpose(jnp.concatenate(weights[0] + weights[1] + [jnp.zeros((112, 128), F32)], axis=0))
     for i in range(HEADS // 2):
-        pair = jnp.where(low, pltpu.roll(att[2 * i], 64, 1), att[2 * i + 1])
+        whole = []
+        for h in (2 * i, 2 * i + 1):
+            got = [spread(r.o_in[v, 2 * h + k, 0:64].astype(F32), h % 2 == 1) for k in range(2)]
+            whole.append(got[0] * cols[:, h : h + 1] + got[1] * cols[:, 8 + h : 9 + h])
+        pair = jnp.where(low, whole[0], whole[1])
+        r.att[v, :, 128 * i : 128 * i + 128] = pair
         r.att_low[v, :, 128 * i : 128 * i + 128] = pair.astype(BF)
     mixed = r.hid[v].astype(F32) + nn(r.att_low[v], r.w_out[...])
     n_one, f_one = norm(mixed)
@@ -353,64 +435,76 @@
     grad_att = nt(out_low, r.w_out[...]).astype(BF).astype(F32)
     ln = lanes((ROWS, 128))
     low = ln < 64
+    deltas = jnp.zeros((ROWS, 128), F32)
+    for h in range(HEADS):
+        cols = slice(128 * (h // 2), 128 * (h // 2) + 128)
+        product = grad_att[:, cols] * r.att[v, :, cols]
+        mine = jnp.where(low, product, 0.0) if h % 2 == 0 else jnp.where(low, 0.0, product)
+        deltas = jnp.where(ln == h, jnp.sum(mine, axis=1, keepdims=True), deltas)
+    deltas = jnp.transpose(deltas)
     for h in range(HEADS):
         tile = grad_att[:, 128 * (h // 2) : 128 * (h // 2) + 128]
-        if h % 2 == 0:
-            tile = pltpu.roll(tile, 64, 1)
-        att = r.att[v, h]
-        delta = jnp.sum(jnp.where(low, 0.0, tile * att), axis=1, keepdims=True)
-        parts = split3(-delta) + split3(-att[:, 0:1])
-        aux = jnp.zeros((ROWS, 128), F32)
-        for i, part in enumerate(parts):
-            aux = jnp.where(ln == i, part, aux)
-        r.do_out[v, h] = jnp.where(low, aux, tile).astype(BF)
+        r.do_out[v, h, 0:64] = pack(tile, h % 2 == 1).astype(BF)
+        rows = split3(-deltas[h : h + 1]) + split3(-r.log_total[v, h : h + 1])
+        r.do_out[v, h, 64:80] = parts_in_rows(rows)
 
 
 def send_do(v, r, place):
-    @pl.loop(0, HEADS)
-    def _(a):
-        h = (place.me // 4 + a) % 8
-        for b in range(2):
-            place.send(
-                r.do_out.at[v, h],
-                r.do_in.at[v, place.own_slot],
-                r.sems.at[6, v],
-                r.sems.at[7, v],
-                (place.me + b) % 2,
-                place.chip(h, place.own_t),
-            )
-
-
-def bwd_tile(v, i, r, place):
-    width = BWD_C * 128
-    u = tile_of(i, place.t)
-    q = jnp.concatenate([r.q_in[v, 2 * i], r.q_in[v, 2 * i + 1]], axis=0).astype(F32)
-    do = jnp.concatenate([r.do_in[v, 2 * i], r.do_in[v, 2 * i + 1]], axis=0).astype(F32)
-    ln = lanes((256, 128))
-    lq = jnp.where((ln >= 68) & (ln < 71), pltpu.roll(do, 65, 1), q).astype(BF)
-    ld = jnp.where((ln >= 3) & (ln < 64), 0.0, do).astype(BF)
-    qz = jnp.where(ln < 64, q, 0.0).astype(BF)
-    dz = jnp.where(ln >= 64, do, 0.0).astype(BF)
-
-    def step(c, dqt, masked):
-        rows = ds(c * width, width)
-        x = nt(r.ka[v, rows, :], lq)
+    to_queries(
+        lambda h: r.do_out.at[v, h], r.do_in.at[v], r.sems.at[6, v], r.sems.at[7, v], place
+    )
+
+
+def prepare_back(v, r):
+    low = lanes((ROWS, 128)) < 64
+
+    @pl.loop(0, 16)
+    def _(n):
+        rows = ds(n * 128, 128)
+        do = spread(r.do_in[v, n, 0:64].astype(F32), True)
+        r.ld[rows, :] = jnp.where(low, 0.0, do).astype(BF)
+        r.qz[rows, :] = jnp.where(low, r.lq[v, rows, :].astype(F32), 0.0).astype(BF)
+        x = r.do_in[v, n, 64:80].astype(F32)
+        r.neg_delta[n] = jnp.broadcast_to(x[0:1] + x[1:2] + x[2:3], (8, 128))
+        r.neg_log[n] = jnp.broadcast_to(x[3:4] + x[4:5] + x[5:6], (8, 128))
+
+    @pl.loop(0, 8)
+    def _(i):
+        rows = ds(i * 512, 512)
+        r.kat[:, rows] = jnp.transpose(r.ka[v, rows, :].astype(F32))[:64].astype(BF)
+
+    r.dqt[...] = jnp.zeros_like(r.dqt)
+
+
+def bwd_body(v, c, tiles, masked, r, place):
+    rows = ds(c * 512, 512)
+    probs, grads = [], []
+    for i in tiles:
+        mine = ds(i * 256, 256)
+        x = nt(r.ka[v, rows, :], r.lq[v, mine, :])
+        x = x + jnp.concatenate([r.neg_log[2 * i][0:1], r.neg_log[2 * i + 1][0:1]], axis=1)
         if masked:
-            row, col = subs((width, 256)), lanes((width, 256))
-            at = 256 * (row // 128) + row % 128 + (256 * BWD_C * c + 128 * place.s - 256 * u)
-            x = jnp.where(at <= col, x, -BIG)
+            row, col = subs((512, 256)), lanes((512, 256))
+            shift = 1024 * c + 128 * place.s - 256 * tile_of(i, place.t)
+            x = jnp.where(256 * (row // 128) + row % 128 + shift <= col, x, -BIG)
         p = jnp.exp(x)
-        dp = nt(r.va[v, rows, :], ld)
-        dsc = (p * dp).astype(BF)
-        r.dkv_acc[rows, :] += nn(dsc, qz) + nn(p.astype(BF), dz)
-        return dqt + nn(r.kat[:, rows], dsc)
-
-    full = u // BWD_C
-    dqt = lax.fori_loop(0, full, lambda c, x: step(c, x, False), jnp.zeros((64, 256), F32))
-    dqt = step(full, dqt, True)
-    dq = jnp.transpose(jnp.concatenate([dqt, jnp.zeros((64, 256), F32)], axis=0)).astype(BF)
-    r.dq_out[v, 2 * i] = dq[:128]
-    r.dq_out[v, 2 * i + 1] = dq[128:]
+        dp = nt(r.va[v, rows, :], r.ld[mine, :])
+        dp = dp + jnp.concatenate([r.neg_delta[2 * i][0:1], r.neg_delta[2 * i + 1][0:1]], axis=1)
+        probs.append(p.astype(BF))
+        grads.append((p * dp).astype(BF))
+    size = 256 * len(tiles)
+    queries = pl.ds(pl.multiple_of(tiles[0] * 256, 256), size)
+    r.dkv_acc[...] += nn(jnp.concatenate(grads, axis=1), r.qz[queries, :]) + nn(
+        jnp.concatenate(probs, axis=1), r.ld[queries, :]
+    )
+    for i, dsc in zip(tiles, grads):
+        r.dqt[i] += nn(r.kat[:, rows], dsc)
+
+
+def bwd_finish(v, i, r, place):
+    dq = jnp.transpose(jnp.concatenate([r.dqt[i], jnp.zeros((64, 256), F32)], axis=0))
+    for k in range(2):
+        r.dq_out[v, 2 * i + k] = pack(dq[128 * k : 128 * k + 128], False).astype(BF)
     for turn in range(2):
         half = (turn + place.s) % 2
         place.send(
@@ -419,43 +513,56 @@
             r.sems.at[8, v],
             r.sems.at[9, v],
             place.micro,
-            2 * u + half,
+            2 * tile_of(i, place.t) + half,
         )
 
 
 def attention_back(v, r, place):
-    r.dkv_acc[...] = jnp.zeros_like(r.dkv_acc)
-
-    @pl.loop(0, 8)
-    def _(i):
-        rows = ds(i * 512, 512)
-        r.kat[:, rows] = jnp.transpose(r.ka[v, rows, :].astype(F32))[:64].astype(BF)
-
-    @pl.loop(0, 8)
-    def _(i):
-        bwd_tile(v, (i + place.head) % 8, r, place)
-        for after, step in SUM_DURING_BACK:
-
-            @pl.when((v == 0) & (i == after))
-            def _():
-                SUM_STEPS[step](0, r, place)
+    prepare_back(v, r)
 
     @pl.when(v == 0)
     def _():
         wait_sent(r.dkv_in.at[1], r.sems.at[10, 1], place.self_kv, 32)
 
-    @pl.loop(0, 32)
+    @pl.loop(0, 8)
+    def _(a):
+        first = (a // 2 + place.head) % 4
+        c = jnp.where(a % 2 == 0, first, 7 - first)
+        r.dkv_acc[...] = jnp.zeros_like(r.dkv_acc)
+
+        @pl.when(c % 2 == 0)
+        def _():
+            bwd_body(v, c, [c, c + 1], True, r, place)
+
+        @pl.when(c % 2 == 1)
+        def _():
+            bwd_body(v, c, [c], True, r, place)
+
+        @pl.loop(c // 2 + 1, 4)
+        def _(m):
+            bwd_body(v, c, [2 * m, 2 * m + 1], False, r, place)
+
+        for b in range(4):
+            k = (b + place.t) % 4
+            n = 4 * c + k
+            r.dkv_out[n] = r.dkv_acc[ds(k * 128, 128), :].astype(BF)
+            place.send(
+                r.dkv_out.at[n],
+                r.dkv_in.at[v, 4 * place.head + place.t],
+                r.sems.at[10, v],
+                r.sems.at[11, v],
+                place.micro,
+                2 * n + place.s,
+            )
+        for after, step in SUM_DURING_BACK:
+
+            @pl.when((v == 0) & (a == after))
+            def _():
+                SUM_STEPS[step](0, r, place)
+
+    @pl.loop(0, 8)
     def _(k):
-        n = (k + 4 * place.head + place.t) % 32
-        r.dkv_out[n] = r.dkv_acc[ds(n * 128, 128), :].astype(BF)
-        place.send(
-            r.dkv_out.at[n],
-            r.dkv_in.at[v, 4 * place.head + place.t],
-            r.sems.at[10, v],
-            r.sems.at[11, v],
-            place.micro,
-            2 * n + place.s,
-        )
+        bwd_finish(v, (k + place.head) % 8, r, place)
 
 
 def after_attention_back(v, r):
@@ -466,10 +573,10 @@
         dq, dkv = [], []
         for h in (2 * i, 2 * i + 1):
             both = r.dq_in[v, 2 * h].astype(F32) + r.dq_in[v, 2 * h + 1].astype(F32)
-            dq.append(both * 0.125)
+            dq.append(spread(both * 0.125, h % 2 == 1))
             four = [r.dkv_in[v, 4 * h + t].astype(F32) for t in range(4)]
             dkv.append((four[0] + four[1]) + (four[2] + four[3]))
-        r.dq[v, :, cols] = jnp.where(low, dq[0], pltpu.roll(dq[1], 64, 1)).astype(BF)
+        r.dq[v, :, cols] = jnp.where(low, dq[0], dq[1]).astype(BF)
         r.dk[v, :, cols] = jnp.where(low, dkv[0], pltpu.roll(dkv[1], 64, 1)).astype(BF)
         r.dv[v, :, cols] = jnp.where(low, pltpu.roll(dkv[0], 64, 1), dkv[1]).astype(BF)
     r.work[...] += (
@@ -735,10 +842,11 @@
     gather_last,
     sum_out,
 )
-SUM_DURING_BACK = ((1, 1), (4, 2), (5, 3), (6, 4), (7, 5))
-
-
-INPUTS = ["inputs", "groups", "cotangent", "w_query", "w_key", "w_value", "w_out", "w_up", "w_down"]
+SUM_DURING_BACK = ((3, 2), (4, 3), (5, 4), (6, 5))
+
+
+WEIGHTS = ["w_query", "w_key", "w_value", "w_out", "w_up", "w_down"]
+INPUTS = ["inputs", "groups", "cotangent"] + [name + "_hbm" for name in WEIGHTS]
 INPUTS += ["gain_one", "shift_one", "gain_two", "shift_two"]
 OUTPUTS = {
     "output": ((1, ROWS, D), BF),
@@ -748,20 +856,41 @@
     "vec": ((8, D), F32),
 }
 SCRATCH = {
+    "w_query": ((D, D), BF),
+    "w_key": ((D, D), BF),
+    "w_value": ((D, D), BF),
+    "w_out": ((D, D), BF),
+    "w_up": ((D, FF), BF),
+    "w_down": ((FF, D), BF),
+    "cot": ((ROWS, D), BF),
     "hid": ((3, ROWS, D), BF),
-    "own_aug": ((ROWS, 128), F32),
-    "q_out": ((2, 8, ROWS, 128), BF),
+    "q_out": ((2, 8, 64, 128), BF),
+    "q_in": ((2, 16, 64, 128), BF),
+    "o_out": ((2, 16, 80, 128), BF),
+    "o_in": ((2, 16, 80, 128), BF),
+    "do_out": ((2, 8, 80, 128), BF),
+    "do_in": ((2, 16, 80, 128), BF),
+    "dq_out": ((2, 16, 64, 128), BF),
+    "dq_in": ((2, 16, 64, 128), BF),
+    "dkv_acc": ((512, 128), F32),
+    "dqt": ((8, 64, 256), F32),
+    "lq": ((2, 2048, 128), BF),
+    "qz": ((2048, 128), BF),
+    "ld": ((2048, 128), BF),
+    "neg_log": ((16, 8, 128), F32),
+    "neg_delta": ((16, 8, 128), F32),
+    "f_acc": ((4, 512, 128), F32),
+    "f_top": ((4, 512, 128), F32),
+    "att": ((2, ROWS, D), F32),
+    "log_total": ((2, 8, 128), F32),
+    "grp_q": ((16, 8, 128), jnp.int32),
     "kv_out": ((2, 8, ROWS, 128), BF),
-    "q_in": ((2, 16, ROWS, 128), BF),
     "kv_in": ((2, 32, ROWS, 128), BF),
     "grp_out": ((1, 8, 128), jnp.int32),
     "grp_in": ((32, 8, 128), jnp.int32),
     "ka": ((2, 4096, 128), BF),
     "va": ((2, 4096, 128), BF),
     "kat": ((64, 4096), BF),
-    "o_out": ((2, 16, ROWS, 128), BF),
-    "o_in": ((2, 16, ROWS, 128), BF),
-    "att": ((2, 8, ROWS, 128), F32),
     "att_low": ((2, ROWS, D), BF),
     "n_one": ((2, ROWS, D), F32),
     "f_one": ((2, ROWS, 128), F32),
@@ -775,11 +904,6 @@
     "down_low": ((2, ROWS, D), BF),
     "up_low": ((2, ROWS, FF), BF),
     "out_low": ((2, ROWS, D), BF),
-    "do_out": ((2, 8, ROWS, 128), BF),
-    "do_in": ((2, 16, ROWS, 128), BF),
-    "dq_out": ((2, 16, ROWS, 128), BF),
-    "dq_in": ((2, 16, ROWS, 128), BF),
-    "dkv_acc": ((4096, 128), F32),
     "dkv_out": ((32, ROWS, 128), BF),
     "dkv_in": ((2, 32, ROWS, 128), BF),
     "dq": ((2, ROWS, D), BF),
@@ -800,42 +924,57 @@
         f"sum_s1{g}": ((3, rows // 16, 128), BF),
         f"sum_t{g}": ((2, 3, rows, 128), BF),
     }
-SEMS = {"sems": (12, 2), "gsems": (2,), "sum_sems0": (2, 10, 3), "sum_sems1": (2, 10, 3), "vsems": (3, 4)}
+SEMS = {"sems": (12, 2), "gsems": (4,), "load_sems": (8,), "kv_sems": (2, 4), "sum_sems0": (2, 10, 3), "sum_sems1": (2, 10, 3), "vsems": (3, 4)}
 
 
 def kernel(*refs):
     names = INPUTS + list(OUTPUTS) + list(SCRATCH) + list(SEMS)
     r = SimpleNamespace(**dict(zip(names, refs)))
     place = Place()
-    barrier(place)
-    send_groups(r, place)
-    make_own_aug(r, place)
+    for name in LOADED:
+        load(name, r, place).start()
+    greet(place)
     r.vec_own[...] = jnp.zeros_like(r.vec_own)
-    r.hid[0] = r.inputs[place.s]
 
     @pl.loop(0, 2)
     def _(v):
-        project(v, r)
-        send_qkv(v, r, place)
+        @pl.when(v == 0)
+        def _():
+            for name in LOADED[:4]:
+                load(name, r, place).wait()
+
+        project_queries(v, r)
+        project_keys_values(v, r)
+
+        @pl.when(v == 0)
+        def _():
+            all_here()
+            send_groups(r, place)
+
+        send_queries(v, r, place)
+        send_keys_values(v, r, place)
 
         @pl.when(v == 0)
         def _():
             wait_all(r.grp_in, r.gsems.at[1])
-            make_key_aug(r)
-
-        wait_all(r.kv_in.at[v], r.sems.at[1, v])
-        make_kv(v, r)
+            wait_all(r.grp_q, r.gsems.at[3])
+            make_aug(r)
+
         wait_all(r.q_in.at[v], r.sems.at[3, v])
-
-        @pl.loop(0, 4)
-        def _(j):
-            fwd_pair(v, (j + place.head) % 4, r, place)
+        make_queries(v, r)
+        attention(v, r, place)
+
+        @pl.when(v == 0)
+        def _():
+            for name in LOADED[4:7]:
+                load(name, r, place).wait()
 
         wait_all(r.o_in.at[v], r.sems.at[5, v])
         after_attention(v, r)
 
     r.output[0] = r.hid[2]
-    r.dy[...] = r.cotangent[place.s].astype(F32)
+    load("cot", r, place).wait()
+    r.dy[...] = r.cot[...].astype(F32)
 
     @pl.loop(0, 2)
     def _(step):
@@ -849,6 +988,11 @@
             SUM_STEPS[0](0, r, place)
 
         wait_all(r.do_in.at[v], r.sems.at[7, v])
+
+        @pl.when(v == 0)
+        def _():
+            SUM_STEPS[1](0, r, place)
+
         attention_back(v, r, place)
 
         @pl.when(v == 0)
@@ -874,6 +1018,7 @@
     for g in range(2):
         sum_drain(g, r, place)
     wait_sent(r.grp_in, r.gsems.at[0], place.self_kv, 32)
+    wait_sent(r.grp_q, r.gsems.at[2], place.self_q, 16)
 
     @pl.loop(0, 2)
     def _(v):
@@ -886,8 +1031,11 @@
     wait_sent(r.dkv_in.at[0], r.sems.at[10, 0], place.self_kv, 32)
 
 
-def unpack(early, late):
-    def body(early, late, query, key, value, out, up, down, got, small, up_f, down_f, sin, sout):
+def unpack(output, input_grad, early, late, vec):
+    def body(*refs):
+        output, input_grad, early, late, vec, output_to, input_grad_to = refs[:7]
+        query, key, value, out, up, down = refs[7:13]
+        got, small, up_f, down_f, sin, sout = refs[17:]
         loads = []
         for j in range(12):
             src = late.at[pl.ds(4 * j, 4)] if j < 3 else early.at[pl.ds(4 * (j - 3), 4)]
@@ -895,7 +1043,14 @@
         order = [0, 1, 2, 11, 3, 4, 5, 6, 7, 8, 9, 10]
         for j in order:
             loads[j].start()
-        stores = []
+        for i in range(4):
+            refs[13 + i][...] = vec[i]
+        stores = [
+            pltpu.make_async_copy(output, output_to, sout.at[12]),
+            pltpu.make_async_copy(input_grad, input_grad_to, sout.at[13]),
+        ]
+        for copy in stores:
+            copy.start()
 
         def store(j, src, dst):
             stores.append(pltpu.make_async_copy(src, dst, sout.at[j]))
@@ -923,23 +1078,26 @@
             copy.wait()
 
     square, hbm = jax.ShapeDtypeStruct((D, D), F32), pl.BlockSpec(memory_space=pl.ANY)
-    shapes = [square] * 4 + [jax.ShapeDtypeStruct((D, FF), F32), jax.ShapeDtypeStruct((FF, D), F32)]
+    vmem = pl.BlockSpec(memory_space=pltpu.VMEM)
+    rows = jax.ShapeDtypeStruct((1, ROWS, D), BF)
+    shapes = [rows] * 2 + [square] * 4
+    shapes += [jax.ShapeDtypeStruct((D, FF), F32), jax.ShapeDtypeStruct((FF, D), F32)]
     return pl.pallas_call(
         body,
-        out_shape=shapes,
-        in_specs=[hbm] * 2,
-        out_specs=[hbm] * 6,
+        out_shape=shapes + [jax.ShapeDtypeStruct((D,), F32)] * 4,
+        in_specs=[hbm] * 4 + [vmem],
+        out_specs=[hbm] * 8 + [vmem] * 4,
         scratch_shapes=[
             pltpu.VMEM((48, 512, 128), BF),
             pltpu.VMEM((4, D, D), F32),
             pltpu.VMEM((D, FF), F32),
             pltpu.VMEM((FF, D), F32),
             pltpu.SemaphoreType.DMA((12,)),
-            pltpu.SemaphoreType.DMA((12,)),
+            pltpu.SemaphoreType.DMA((14,)),
         ],
-        compiler_params=pltpu.CompilerParams(vmem_limit_bytes=40 * 2**20),
+        compiler_params=pltpu.CompilerParams(vmem_limit_bytes=60 * 2**20),
         name="unpack",
-    )(early, late)
+    )(output, input_grad, early, late, vec)
 
 
 def on_device(inputs, groups, cotangent, *params):
@@ -948,7 +1106,10 @@
     out = pl.pallas_call(
         kernel,
         out_shape=[jax.ShapeDtypeStruct(shape, kind) for shape, kind in OUTPUTS.values()],
-        in_specs=[vmem] * len(INPUTS),
+        in_specs=[
+            pl.BlockSpec(memory_space=pl.ANY) if n.endswith("_hbm") or n in ("inputs", "cotangent") else vmem
+            for n in INPUTS
+        ],
         out_specs=[
             pl.BlockSpec(memory_space=pl.ANY) if n.startswith("sums") else vmem for n in OUTPUTS
         ],
@@ -959,9 +1120,7 @@
         ),
         name="visits",
     )(inputs, groups, cotangent, *params[:6], *vectors)
-    grads = unpack(out[2].reshape(36, 512, 128), out[3].reshape(12, 512, 128))
-    vec = out[4]
-    return (*out[:2], *grads, vec[0], vec[1], vec[2], vec[3])
+    return unpack(*out[:2], out[2].reshape(36, 512, 128), out[3].reshape(12, 512, 128), out[4])
 
 
 def solution(mesh):

time: 272 us -> 241 us (0.89)
  Pallas kernels: 264 us -> 240 us
  local copies, waits for them, and re-layouts: 6.53 us -> 0 us
    pallas_call x1, Pallas kernels: 259 us -> 230 us  [on_device(): pl.pallas_call(kernel, out_shape=[jax.ShapeDtypeStruct(shape, kind) for s...]
    pallas_call x1, Pallas kernels: 5.43 us -> 10.6 us  [unpack(): pl.pallas_call(body, out_shape=shapes + [jax.ShapeDtypeStruct((D,), F32)]...]
    unnamed x10 -> x0, local copies, waits for them, and re-layouts: 5.06 us -> none
where the time goes in v4:
time: 241 us
  Pallas kernels  240 us (100%)
    pallas_call x1, Pallas kernels, on_device(): pl.pallas_call(kernel, out_shape=[jax.ShapeDtypeStruct(shape, kind) for s...  230 us
    pallas_call x1, Pallas kernels, unpack(): pl.pallas_call(body, out_shape=shapes + [jax.ShapeDtypeStruct((D,), F32)]...  10.6 us

profile of v4, /device:TPU:1, one launch (start us, length us, event | category | flops | bytes accessed | tf_op | source)
XLA Modules:
  0.0 241.0 jit_solution(5603475597370258864)
XLA Ops:
  0.6 229.8 %visits.1 = (bf16[1,128,512]{2,1,0:T(8,128)(2,1)}, bf16[1,128,512]{2,1,0:T(8,128)(2,1)}, bf16[2,3,3072,128]{3,2,1,0:T(8,128)(2,1)}, bf16[2,3,1024,128]{3,2,1,0:T(8,128)(2,1)}, f32[8,512]{1,0:T(8,128)}) custom-call(bf16[2,128,512]{2,1,0:T(8,128)(2,1)} %refs_0_.1, s32[2,128]{1,0:T(2,128)} %refs_1_.1, bf16[2,128,512]{2,1,0:T(8,128)(2,1)} %refs_2_.1, ...), custom_call_target="tpu_custom_call" | custom-call | tf_op jit(solution)/shard_map/visits/pallas_call | solution.py:1106
  230.4 10.6 %unpack.1 = (bf16[1,128,512]{2,1,0:T(8,128)(2,1)}, bf16[1,128,512]{2,1,0:T(8,128)(2,1)}, f32[512,512]{1,0:T(8,128)}, f32[512,512]{1,0:T(8,128)}, f32[512,512]{1,...) custom-call(bf16[1,128,512]{2,1,0:T(8,128)(2,1)} %get-tuple-element., ...), custom_call_target="tpu_custom_call" | custom-call | tf_op jit(solution)/shard_map/unpack/pallas_call | solution.py:1085

commit v5 on v4

--- a/solution.py
+++ b/solution.py
@@ -97,6 +97,9 @@
         c = self.coords[axis]
         return self.me + ((c + d) % 4 - c) * (1, 16, 4)[axis]
 
+    def chip_in_plane(self, h):
+        return 16 * (2 * self.s + h // 4) + 4 * self.coords[2] + h % 4
+
     def chip(self, h, t):
         x, y = h % 4, 2 * self.s + h // 4
         return 16 * y + 4 * ((t - x - y + 8) % 4) + x
@@ -118,6 +121,17 @@
         @pl.when(to_self)
         def _():
             pltpu.make_async_copy(src, dst, recv_sem).start()
+
+
+def remote(src, dst, send_sem, recv_sem, section, dp):
+    pltpu.make_async_remote_copy(
+        src_ref=src,
+        dst_ref=dst,
+        send_sem=send_sem,
+        recv_sem=recv_sem,
+        device_id=(section, dp),
+        device_id_type=MESH,
+    ).start()
 
 
 def wait_all(ref, sem):
@@ -229,13 +243,33 @@
 
 
 def send_keys_values(v, r, place):
-    to_keys(
-        lambda h: r.kv_out.at[v, h],
-        r.kv_in.at[v],
-        r.sems.at[0, v],
-        r.kv_sems.at[v, place.me // 16],
-        place,
-    )
+    x, y, _ = place.coords
+    n = place.me // 2
+
+    @pl.loop(0, HEADS)
+    def _(a):
+        h = 2 * ((n // 8 + a // 2) % 4) + (n // 4 + a) % 2
+        place.send(
+            r.kv_out.at[v, h],
+            r.kv_in.at[v, n],
+            r.sems.at[0, v],
+            r.plane_sems.at[v, 2 * y + x // 2],
+            x % 2,
+            place.chip_in_plane(h),
+        )
+
+
+def pass_on(v, r, place):
+    z = place.coords[2]
+
+    @pl.loop(0, 4)
+    def _(y):
+        for b in range(2):
+            block = r.kv_in.at[v, 8 * y + 2 * z + b]
+            wait_all(block, r.plane_sems.at[v, 2 * y + b])
+            for d in (2, 1, 3):
+                to = place.along(2, d)
+                remote(block, block, r.sems.at[1, v], r.kv_sems.at[v, y], place.s, to)
 
 
 def send_groups(r, place):
@@ -336,28 +370,15 @@
     r.f_top[...] = jnp.full_like(r.f_top, -2 * BIG)
 
     @pl.loop(0, 4)
-    def _(a):
-        c = (place.head // 2 + 4 - a) % 4
-
-        @pl.loop(0, jnp.where(a == 3, c, 0))
-        def _(j):
-            fwd_finish(v, j, r, place)
-
-        wait_all(r.kv_in.at[v, ds(8 * c, 8)], r.kv_sems.at[v, c])
+    def _(c):
+        wait_all(r.kv_in.at[v, pl.ds(0, 6)], r.kv_sems.at[v, c])
         make_kv(v, c, r)
         fwd_body(v, c, c, True, r, place)
-
-        @pl.when(a == 3)
-        def _():
-            fwd_finish(v, c, r, place)
+        fwd_finish(v, c, r, place)
 
         @pl.loop(c + 1, 4)
         def _(j):
             fwd_body(v, c, j, False, r, place)
-
-            @pl.when(a == 3)
-            def _():
-                fwd_finish(v, j, r, place)
 
 
 def after_attention(v, r):
@@ -461,12 +482,7 @@
     @pl.loop(0, 16)
     def _(n):
         rows = ds(n * 128, 128)
-        do = spread(r.do_in[v, n, 0:64].astype(F32), True)
-        r.ld[rows, :] = jnp.where(low, 0.0, do).astype(BF)
         r.qz[rows, :] = jnp.where(low, r.lq[v, rows, :].astype(F32), 0.0).astype(BF)
-        x = r.do_in[v, n, 64:80].astype(F32)
-        r.neg_delta[n] = jnp.broadcast_to(x[0:1] + x[1:2] + x[2:3], (8, 128))
-        r.neg_log[n] = jnp.broadcast_to(x[3:4] + x[4:5] + x[5:6], (8, 128))
 
     @pl.loop(0, 8)
     def _(i):
@@ -474,6 +490,18 @@
         r.kat[:, rows] = jnp.transpose(r.ka[v, rows, :].astype(F32))[:64].astype(BF)
 
     r.dqt[...] = jnp.zeros_like(r.dqt)
+
+
+def take_do(v, r):
+    low = lanes((ROWS, 128)) < 64
+
+    @pl.loop(0, 16)
+    def _(n):
+        do = spread(r.do_in[v, n, 0:64].astype(F32), True)
+        r.ld[ds(n * 128, 128), :] = jnp.where(low, 0.0, do).astype(BF)
+        x = r.do_in[v, n, 64:80].astype(F32)
+        r.neg_delta[n] = jnp.broadcast_to(x[0:1] + x[1:2] + x[2:3], (8, 128))
+        r.neg_log[n] = jnp.broadcast_to(x[3:4] + x[4:5] + x[5:6], (8, 128))
 
 
 def bwd_body(v, c, tiles, masked, r, place):
@@ -517,8 +545,13 @@
         )
 
 
+def chunk_at(a, place):
+    first = (a // 2 + place.head) % 4
+    return jnp.where(a % 2 == 0, first, 7 - first)
+
+
 def attention_back(v, r, place):
-    prepare_back(v, r)
+    take_do(v, r)
 
     @pl.when(v == 0)
     def _():
@@ -528,6 +561,11 @@
     def _(a):
         first = (a // 2 + place.head) % 4
         c = jnp.where(a % 2 == 0, first, 7 - first)
+
+        @pl.loop(0, jnp.where(a == 7, c, 0))
+        def _(i):
+            bwd_finish(v, i, r, place)
+
         r.dkv_acc[...] = jnp.zeros_like(r.dkv_acc)
 
         @pl.when(c % 2 == 0)
@@ -560,14 +598,13 @@
             def _():
                 SUM_STEPS[step](0, r, place)
 
-    @pl.loop(0, 8)
-    def _(k):
-        bwd_finish(v, (k + place.head) % 8, r, place)
-
-
-def after_attention_back(v, r):
-    ln = lanes((ROWS, 128))
-    low = ln < 64
+    @pl.loop(7 - (3 + place.head) % 4, 8)
+    def _(i):
+        bwd_finish(v, i, r, place)
+
+
+def take_gradients(v, r):
+    low = lanes((ROWS, 128)) < 64
     for i in range(HEADS // 2):
         cols = slice(128 * i, 128 * i + 128)
         dq, dkv = [], []
@@ -579,9 +616,15 @@
         r.dq[v, :, cols] = jnp.where(low, dq[0], dq[1]).astype(BF)
         r.dk[v, :, cols] = jnp.where(low, dkv[0], pltpu.roll(dkv[1], 64, 1)).astype(BF)
         r.dv[v, :, cols] = jnp.where(low, pltpu.roll(dkv[0], 64, 1), dkv[1]).astype(BF)
-    r.work[...] += (
-        nt(r.dq[v], r.w_query[...]) + nt(r.dk[v], r.w_key[...]) + nt(r.dv[v], r.w_value[...])
-    )
+
+
+def input_gradient(v, r):
+    return (
+        r.work[...]
+        + nt(r.dq[v], r.w_query[...])
+        + nt(r.dk[v], r.w_key[...])
+        + nt(r.dv[v], r.w_value[...])
+    ).astype(BF)
 
 
 def both(ref):
@@ -620,30 +663,18 @@
 
 SUM_ROWS = (3072, 1024)
 ORDERS = ((0, 1, 2), (1, 2, 0), (2, 0, 1))
+PLANE = [(d, e) for d in range(4) for e in range(4) if (d, e) != (0, 0)]
 
 
 def sum_refs(g, r):
-    names = ("in", "x", "r0", "r1", "r2", "s0", "s1", "t", "sems")
+    names = ("in", "x", "r0", "r1", "s0", "t", "sems")
     return SimpleNamespace(**{n: getattr(r, "sum_" + n + str(g)) for n in names})
 
 
-def remote(src, dst, send_sem, recv_sem, section, dp):
-    pltpu.make_async_remote_copy(
-        src_ref=src,
-        dst_ref=dst,
-        send_sem=send_sem,
-        recv_sem=recv_sem,
-        device_id=(section, dp),
-        device_id_type=MESH,
-    ).start()
-
-
 def offsets(p, rows, place):
-    out, at = [], 0
-    for k in range(3):
-        at = at + place.coords[ORDERS[p][k]] * (rows // 4 ** (k + 1))
-        out.append(at)
-    return out
+    first, second, third = [place.coords[axis] for axis in ORDERS[p]]
+    at = first * (rows // 4)
+    return at, at + (4 * second + third) * (rows // 64)
 
 
 def exchange_start(g, r, place):
@@ -659,19 +690,33 @@
         )
 
 
-def scatter_send(g, p, k, src, base, q, place):
-    size = SUM_ROWS[g] // 4 ** (k + 1)
-    dst = (q.r0, q.r1, q.r2)[k]
-    axis = ORDERS[p][k]
+def axis_send(p, base, q, g, src, place):
+    size = SUM_ROWS[g] // 4
+    axis = ORDERS[p][0]
     for d in (2, 1, 3):
         c = (place.coords[axis] + d) % 4
         remote(
             src.at[ds(base + c * size, size)],
-            dst.at[p, d - 1],
-            q.sems.at[0, 1 + k, p],
-            q.sems.at[1, 1 + k, p],
+            q.r0.at[p, d - 1],
+            q.sems.at[0, 1, p],
+            q.sems.at[1, 1, p],
             place.s,
             place.along(axis, d),
+        )
+
+
+def plane_send(p, q, g, place):
+    size = SUM_ROWS[g] // 64
+    second, third = ORDERS[p][1:]
+    for d, e in PLANE:
+        block = 4 * ((place.coords[second] + d) % 4) + (place.coords[third] + e) % 4
+        remote(
+            q.s0.at[p, ds(block * size, size)],
+            q.r1.at[p, 4 * d + e - 1],
+            q.sems.at[0, 2, p],
+            q.sems.at[1, 2, p],
+            place.s,
+            place.along(second, d) + place.along(third, e) - place.me,
         )
 
 
@@ -688,42 +733,36 @@
             other = q.x[ds(p * rows + k * 512, 512), :]
             src[at, :] = (src[at, :].astype(F32) + other.astype(F32)).astype(BF)
 
-        scatter_send(g, p, 0, src, base, q, place)
-
-
-def scatter_done(k, g, r, place):
+        axis_send(p, base, q, g, src, place)
+
+
+def axis_done(g, r, place):
     q, rows = sum_refs(g, r), SUM_ROWS[g]
-    size = rows // 4 ** (k + 1)
-    got = (q.r0, q.r1, q.r2)[k]
+    size = rows // 4
     for p in range(3):
-        wait_all(got.at[p], q.sems.at[1, 1 + k, p])
-        c = place.coords[ORDERS[p][k]]
-        if k == 0:
-            own = q.__dict__["in"][ds(place.s * 3 * rows + p * rows + c * size, size), :]
-        else:
-            own = (q.s0, q.s1)[k - 1][p, ds(c * size, size), :]
-        total = own.astype(F32)
+        wait_all(q.r0.at[p], q.sems.at[1, 1, p])
+        at = place.s * 3 * rows + p * rows + place.coords[ORDERS[p][0]] * size
+        total = q.__dict__["in"][ds(at, size), :].astype(F32)
         for d in range(3):
-            total = total + got[p, d].astype(F32)
-        if k < 2:
-            dst = (q.s0, q.s1)[k]
-            dst[p] = total.astype(BF)
-            scatter_send(g, p, k + 1, dst.at[p], 0, q, place)
-        else:
-            q.t[place.s, p, ds(offsets(p, rows, place)[2], size), :] = total.astype(BF)
-            gather_send(g, p, 2, q, place)
-
-
-def gather_send(g, p, k, q, place):
-    rows = SUM_ROWS[g]
-    size = rows // 4 ** (k + 1)
-    block = q.t.at[place.s, p, ds(offsets(p, rows, place)[k], size)]
-    axis = ORDERS[p][k]
-    for d in (2, 1, 3):
-        sem = 4 + k if k else 6 + d
-        remote(
-            block, block, q.sems.at[0, sem, p], q.sems.at[1, sem, p], place.s, place.along(axis, d)
-        )
+            total = total + q.r0[p, d].astype(F32)
+        q.s0[p] = total.astype(BF)
+        plane_send(p, q, g, place)
+
+
+def plane_done(g, r, place):
+    q, rows = sum_refs(g, r), SUM_ROWS[g]
+    size = rows // 64
+    for p in range(3):
+        wait_all(q.r1.at[p], q.sems.at[1, 2, p])
+        second, third = [place.coords[axis] for axis in ORDERS[p][1:]]
+        total = q.s0[p, ds((4 * second + third) * size, size), :].astype(F32)
+        for d in range(15):
+            total = total + q.r1[p, d].astype(F32)
+        block = q.t.at[place.s, p, ds(offsets(p, rows, place)[1], size)]
+        block[...] = total.astype(BF)
+        for d, e in PLANE:
+            to = place.along(ORDERS[p][1], d) + place.along(ORDERS[p][2], e) - place.me
+            remote(block, block, q.sems.at[0, 3, p], q.sems.at[1, 3, p], place.s, to)
 
 
 def cross_send(p, start, size, q, place):
@@ -731,16 +770,16 @@
     remote(block, block, q.sems.at[0, 4, p], q.sems.at[1, 4, p], 1 - place.s, place.me)
 
 
-def gather_done(k, g, r, place):
+def plane_back(g, r, place):
     q, rows = sum_refs(g, r), SUM_ROWS[g]
     for p in range(3):
-        wait_all(
-            q.t.at[0, p, pl.ds(0, 3 * rows // 4 ** (k + 1))],
-            q.sems.at[1, 4 + k, p],
-        )
-        gather_send(g, p, k - 1, q, place)
-        if k == 1:
-            cross_send(p, offsets(p, rows, place)[0], rows // 4, q, place)
+        wait_all(q.t.at[0, p, pl.ds(0, 15 * rows // 64)], q.sems.at[1, 3, p])
+        at, axis = offsets(p, rows, place)[0], ORDERS[p][0]
+        block = q.t.at[place.s, p, ds(at, rows // 4)]
+        for d in (2, 1, 3):
+            send_sem, recv_sem = q.sems.at[0, 4 + d, p], q.sems.at[1, 4 + d, p]
+            remote(block, block, send_sem, recv_sem, place.s, place.along(axis, d))
+        cross_send(p, at, rows // 4, q, place)
 
 
 def gather_last(g, r, place):
@@ -748,7 +787,7 @@
     size = rows // 4
     for d in (1, 3, 2):
         for p in range(3):
-            wait_all(q.t.at[0, p, pl.ds(0, size)], q.sems.at[1, 6 + d, p])
+            wait_all(q.t.at[0, p, pl.ds(0, size)], q.sems.at[1, 4 + d, p])
             c = (place.coords[ORDERS[p][0]] - d + 4) % 4
             cross_send(p, c * size, size, q, place)
 
@@ -764,12 +803,11 @@
     q, rows = sum_refs(g, r), SUM_ROWS[g]
     for p in range(3):
         wait_all(q.x.at[pl.ds(0, rows)], q.sems.at[0, 0, p])
-        for k in range(3):
-            wait_all(q.t.at[0, p, pl.ds(0, 3 * rows // 4 ** (k + 1))], q.sems.at[0, 1 + k, p])
-        for k in (1, 2):
-            wait_all(q.t.at[0, p, pl.ds(0, 3 * rows // 4 ** (k + 1))], q.sems.at[0, 4 + k, p])
+        wait_all(q.r0.at[p], q.sems.at[0, 1, p])
+        for k in (2, 3):
+            wait_all(q.r1.at[p], q.sems.at[0, k, p])
         for d in range(1, 4):
-            wait_all(q.t.at[0, p, pl.ds(0, rows // 4)], q.sems.at[0, 6 + d, p])
+            wait_all(q.t.at[0, p, pl.ds(0, rows // 4)], q.sems.at[0, 4 + d, p])
         wait_all(q.t.at[0, p], q.sems.at[0, 4, p])
     pltpu.make_async_copy(q.t, (r.sums0, r.sums1)[g], r.vsems.at[2, g]).wait()
 
@@ -825,24 +863,36 @@
         vec_step(0, r, place)
 
 
-def step_between(k, g, r, place):
-    scatter_done(k, g, r, place)
+def step_axis(g, r, place):
+    axis_done(g, r, place)
     if g == 0:
-        vec_step(k + 1, r, place)
+        vec_step(1, r, place)
+
+
+def step_plane(g, r, place):
+    plane_done(g, r, place)
+    if g == 0:
+        vec_step(2, r, place)
+
+
+def step_back(g, r, place):
+    plane_back(g, r, place)
+    if g == 0:
+        vec_step(3, r, place)
 
 
 SUM_STEPS = (
     step_exchange,
     step_scatter,
-    lambda *a: step_between(0, *a),
-    lambda *a: step_between(1, *a),
-    lambda *a: step_between(2, *a),
-    lambda *a: gather_done(2, *a),
-    lambda *a: gather_done(1, *a),
+    step_axis,
+    step_plane,
+    step_back,
     gather_last,
     sum_out,
 )
-SUM_DURING_BACK = ((3, 2), (4, 3), (5, 4), (6, 5))
+SUM_DURING_BACK = ((7, 2),)
+SUM_AFTER_BACK = (3,)
+SUM_TAIL = ((0, 4), (1, 1), (1, 2), (0, 5), (1, 3), (0, 6), (1, 4), (1, 5), (1, 6))
 
 
 WEIGHTS = ["w_query", "w_key", "w_value", "w_out", "w_up", "w_down"]
@@ -918,13 +968,11 @@
         f"sum_in{g}": ((6 * rows, 128), BF),
         f"sum_x{g}": ((3 * rows, 128), BF),
         f"sum_r0{g}": ((3, 3, rows // 4, 128), BF),
-        f"sum_r1{g}": ((3, 3, rows // 16, 128), BF),
-        f"sum_r2{g}": ((3, 3, rows // 64, 128), BF),
+        f"sum_r1{g}": ((3, 15, rows // 64, 128), BF),
         f"sum_s0{g}": ((3, rows // 4, 128), BF),
-        f"sum_s1{g}": ((3, rows // 16, 128), BF),
         f"sum_t{g}": ((2, 3, rows, 128), BF),
     }
-SEMS = {"sems": (12, 2), "gsems": (4,), "load_sems": (8,), "kv_sems": (2, 4), "sum_sems0": (2, 10, 3), "sum_sems1": (2, 10, 3), "vsems": (3, 4)}
+SEMS = {"sems": (12, 2), "gsems": (4,), "load_sems": (8,), "kv_sems": (2, 4), "plane_sems": (2, 8), "sum_sems0": (2, 8, 3), "sum_sems1": (2, 8, 3), "vsems": (3, 4)}
 
 
 def kernel(*refs):
@@ -953,6 +1001,7 @@
 
         send_queries(v, r, place)
         send_keys_values(v, r, place)
+        pass_on(v, r, place)
 
         @pl.when(v == 0)
         def _():
@@ -987,6 +1036,7 @@
             weight_grads_early(r)
             SUM_STEPS[0](0, r, place)
 
+        prepare_back(v, r)
         wait_all(r.do_in.at[v], r.sems.at[7, v])
 
         @pl.when(v == 0)
@@ -997,22 +1047,22 @@
 
         @pl.when(v == 0)
         def _():
-            SUM_STEPS[6](0, r, place)
+            for step in SUM_AFTER_BACK:
+                SUM_STEPS[step](0, r, place)
 
         wait_all(r.dq_in.at[v], r.sems.at[9, v])
         wait_all(r.dkv_in.at[v], r.sems.at[11, v])
-        after_attention_back(v, r)
-        r.dy[...] = r.work[...].astype(BF).astype(F32)
-
-    r.input_grad[0] = r.dy[...].astype(BF)
+        take_gradients(v, r)
+
+        @pl.when(v == 1)
+        def _():
+            r.dy[...] = input_gradient(v, r).astype(F32)
+
     weight_grads_late(r)
     SUM_STEPS[0](1, r, place)
-    SUM_STEPS[7](0, r, place)
-    for step in SUM_STEPS[1:5]:
-        step(1, r, place)
-    SUM_STEPS[8](0, r, place)
-    for step in SUM_STEPS[5:]:
-        step(1, r, place)
+    r.input_grad[0] = input_gradient(0, r)
+    for g, step in SUM_TAIL:
+        SUM_STEPS[step](g, r, place)
 
     vec_drain(r)
     for g in range(2):
@@ -1022,7 +1072,8 @@
 
     @pl.loop(0, 2)
     def _(v):
-        wait_sent(r.kv_in.at[v], r.sems.at[0, v], place.self_kv, 32)
+        wait_sent(r.kv_in.at[v], r.sems.at[0, v], place.self_kv, 8)
+        wait_all(r.kv_in.at[v, pl.ds(0, 24)], r.sems.at[1, v])
         wait_sent(r.q_in.at[v], r.sems.at[2, v], place.self_q, 16)
         wait_sent(r.o_in.at[v], r.sems.at[4, v], place.self_q, 16)
         wait_sent(r.do_in.at[v], r.sems.at[6, v], place.self_q, 16)
@@ -1035,16 +1086,16 @@
     def body(*refs):
         output, input_grad, early, late, vec, output_to, input_grad_to = refs[:7]
         query, key, value, out, up, down = refs[7:13]
-        got, small, up_f, down_f, sin, sout = refs[17:]
+        got, small, up_f, down_f, vec_in, vec_out, sin, sout = refs[17:]
         loads = []
         for j in range(12):
             src = late.at[pl.ds(4 * j, 4)] if j < 3 else early.at[pl.ds(4 * (j - 3), 4)]
             loads.append(pltpu.make_async_copy(src, got.at[pl.ds(4 * j, 4)], sin.at[j]))
-        order = [0, 1, 2, 11, 3, 4, 5, 6, 7, 8, 9, 10]
+        order = [7, 8, 9, 10, 3, 4, 5, 6, 0, 1, 2, 11]
         for j in order:
             loads[j].start()
-        for i in range(4):
-            refs[13 + i][...] = vec[i]
+        get_vec = pltpu.make_async_copy(vec, vec_in, sin.at[12])
+        get_vec.start()
         stores = [
             pltpu.make_async_copy(output, output_to, sout.at[12]),
             pltpu.make_async_copy(input_grad, input_grad_to, sout.at[13]),
@@ -1073,27 +1124,35 @@
             else:
                 for k in range(4):
                     down_f[512 * k : 512 * k + 512, cols[j - 7]] = tiles[k]
-        store(7, down_f, down)
+                if j == 10:
+                    store(7, down_f, down)
+        get_vec.wait()
+        for i in range(4):
+            vec_out[i, 0] = vec_in[i]
+            copy = pltpu.make_async_copy(vec_out.at[i, 0], refs[13 + i], sout.at[14 + i])
+            copy.start()
+            stores.append(copy)
         for copy in stores:
             copy.wait()
 
     square, hbm = jax.ShapeDtypeStruct((D, D), F32), pl.BlockSpec(memory_space=pl.ANY)
-    vmem = pl.BlockSpec(memory_space=pltpu.VMEM)
     rows = jax.ShapeDtypeStruct((1, ROWS, D), BF)
     shapes = [rows] * 2 + [square] * 4
     shapes += [jax.ShapeDtypeStruct((D, FF), F32), jax.ShapeDtypeStruct((FF, D), F32)]
     return pl.pallas_call(
         body,
         out_shape=shapes + [jax.ShapeDtypeStruct((D,), F32)] * 4,
-        in_specs=[hbm] * 4 + [vmem],
-        out_specs=[hbm] * 8 + [vmem] * 4,
+        in_specs=[hbm] * 5,
+        out_specs=[hbm] * 12,
         scratch_shapes=[
             pltpu.VMEM((48, 512, 128), BF),
             pltpu.VMEM((4, D, D), F32),
             pltpu.VMEM((D, FF), F32),
             pltpu.VMEM((FF, D), F32),
-            pltpu.SemaphoreType.DMA((12,)),
-            pltpu.SemaphoreType.DMA((14,)),
+            pltpu.VMEM((8, D), F32),
+            pltpu.VMEM((4, 1, D), F32),
+            pltpu.SemaphoreType.DMA((13,)),
+            pltpu.SemaphoreType.DMA((18,)),
         ],
         compiler_params=pltpu.CompilerParams(vmem_limit_bytes=60 * 2**20),
         name="unpack",

time: 241 us -> 223 us (0.925)
  Pallas kernels: 240 us -> 222 us
    pallas_call x1, Pallas kernels: 230 us -> 213 us  [on_device(): pl.pallas_call(kernel, out_shape=[jax.ShapeDtypeStruct(shape, kind) for s...]
where the time goes in v5:
time: 223 us
  Pallas kernels  222 us (100%)
    pallas_call x1, Pallas kernels, on_device(): pl.pallas_call(kernel, out_shape=[jax.ShapeDtypeStruct(shape, kind) for s...  213 us
    pallas_call x1, Pallas kernels, unpack(): pl.pallas_call(body, out_shape=shapes + [jax.ShapeDtypeStruct((D,), F32)]...  9.36 us

profile of v5, /device:TPU:1, one launch (start us, length us, event | category | flops | bytes accessed | tf_op | source)
XLA Modules:
  0.0 222.6 jit_solution(10386119947147638337)
XLA Ops:
  0.6 212.6 %visits.1 = (bf16[1,128,512]{2,1,0:T(8,128)(2,1)}, bf16[1,128,512]{2,1,0:T(8,128)(2,1)}, bf16[2,3,3072,128]{3,2,1,0:T(8,128)(2,1)}, bf16[2,3,1024,128]{3,2,1,0:T(8,128)(2,1)}, f32[8,512]{1,0:T(8,128)}) custom-call(bf16[2,128,512]{2,1,0:T(8,128)(2,1)} %refs_0_.1, s32[2,128]{1,0:T(2,128)} %refs_1_.1, bf16[2,128,512]{2,1,0:T(8,128)(2,1)} %refs_2_.1, ...), custom_call_target="tpu_custom_call" | custom-call | tf_op jit(solution)/shard_map/visits/pallas_call | solution.py:1165
  213.2 9.4 %unpack.1 = (bf16[1,128,512]{2,1,0:T(8,128)(2,1)}, bf16[1,128,512]{2,1,0:T(8,128)(2,1)}, f32[512,512]{1,0:T(8,128)}, f32[512,512]{1,0:T(8,128)}, f32[512,512]{1,...) custom-call(bf16[1,128,512]{2,1,0:T(8,128)(2,1)} %get-tuple-element., ...), custom_call_target="tpu_custom_call" | custom-call | tf_op jit(solution)/shard_map/unpack/pallas_call | solution.py:1142

commit v6 on v5

--- a/solution.py
+++ b/solution.py
@@ -161,17 +161,17 @@
     pl.semaphore_wait(pltpu.get_barrier_semaphore(), 127)
 
 
-LOADED = ["hid", "w_query", "w_key", "w_value", "w_out", "w_up", "w_down", "cot"]
+LOADED = ["hid", "w_query", "w_key", "w_value", "groups", "w_out", "w_up", "w_down", "gain_one"]
+LOADED += ["shift_one", "gain_two", "shift_two", "cot"]
 
 
 def load(name, r, place):
+    sem = r.load_sems.at[LOADED.index(name)]
     if name == "hid":
-        return pltpu.make_async_copy(r.inputs.at[place.s], r.hid.at[0], r.load_sems.at[0])
+        return pltpu.make_async_copy(r.inputs.at[place.s], r.hid.at[0], sem)
     if name == "cot":
-        return pltpu.make_async_copy(r.cotangent.at[place.s], r.cot, r.load_sems.at[7])
-    return pltpu.make_async_copy(
-        getattr(r, name + "_hbm"), getattr(r, name), r.load_sems.at[LOADED.index(name)]
-    )
+        return pltpu.make_async_copy(r.cotangent.at[place.s], r.cot, sem)
+    return pltpu.make_async_copy(getattr(r, name + "_hbm"), getattr(r, name), sem)
 
 
 def pack(tile, odd):
@@ -550,6 +550,11 @@
     return jnp.where(a % 2 == 0, first, 7 - first)
 
 
+def chunk_at(a, place):
+    first = (a // 2 + place.coords[0] + place.t) % 4
+    return jnp.where((a + place.coords[1]) % 2 == 0, first, 7 - first)
+
+
 def attention_back(v, r, place):
     take_do(v, r)
 
@@ -559,8 +564,7 @@
 
     @pl.loop(0, 8)
     def _(a):
-        first = (a // 2 + place.head) % 4
-        c = jnp.where(a % 2 == 0, first, 7 - first)
+        c = chunk_at(a, place)
 
         @pl.loop(0, jnp.where(a == 7, c, 0))
         def _(i):
@@ -598,7 +602,7 @@
             def _():
                 SUM_STEPS[step](0, r, place)
 
-    @pl.loop(7 - (3 + place.head) % 4, 8)
+    @pl.loop(chunk_at(7, place), 8)
     def _(i):
         bwd_finish(v, i, r, place)
 
@@ -792,11 +796,17 @@
             cross_send(p, c * size, size, q, place)
 
 
+def half_out(half, sem, g, r):
+    q = sum_refs(g, r)
+    return pltpu.make_async_copy(q.t.at[half], (r.sums0, r.sums1)[g].at[half], r.vsems.at[2, sem])
+
+
 def sum_out(g, r, place):
     q = sum_refs(g, r)
     for p in range(3):
         wait_all(q.t.at[0, p], q.sems.at[1, 4, p])
-    pltpu.make_async_copy(q.t, (r.sums0, r.sums1)[g], r.vsems.at[2, g]).start()
+    half_out(1 - place.s, g, g, r).start()
+    half_out(place.s, 2 + g, g, r).start()
 
 
 def sum_drain(g, r, place):
@@ -809,7 +819,8 @@
         for d in range(1, 4):
             wait_all(q.t.at[0, p, pl.ds(0, rows // 4)], q.sems.at[0, 4 + d, p])
         wait_all(q.t.at[0, p], q.sems.at[0, 4, p])
-    pltpu.make_async_copy(q.t, (r.sums0, r.sums1)[g], r.vsems.at[2, g]).wait()
+    half_out(1 - place.s, g, g, r).wait()
+    half_out(place.s, 2 + g, g, r).wait()
 
 
 def vec_exchange(r, place):
@@ -892,18 +903,18 @@
 )
 SUM_DURING_BACK = ((7, 2),)
 SUM_AFTER_BACK = (3,)
-SUM_TAIL = ((0, 4), (1, 1), (1, 2), (0, 5), (1, 3), (0, 6), (1, 4), (1, 5), (1, 6))
+SUM_TAIL = ((1, 1), (0, 4), (1, 2), (1, 3), (0, 5), (1, 4), (0, 6), (1, 5), (1, 6))
 
 
 WEIGHTS = ["w_query", "w_key", "w_value", "w_out", "w_up", "w_down"]
-INPUTS = ["inputs", "groups", "cotangent"] + [name + "_hbm" for name in WEIGHTS]
-INPUTS += ["gain_one", "shift_one", "gain_two", "shift_two"]
+INPUTS = ["inputs", "groups_hbm", "cotangent"] + [name + "_hbm" for name in WEIGHTS]
+INPUTS += [name + "_hbm" for name in ("gain_one", "shift_one", "gain_two", "shift_two")]
 OUTPUTS = {
     "output": ((1, ROWS, D), BF),
     "input_grad": ((1, ROWS, D), BF),
     "sums0": ((2, 3, 3072, 128), BF),
     "sums1": ((2, 3, 1024, 128), BF),
-    "vec": ((8, D), F32),
+    "vec_hbm": ((8, D), F32),
 }
 SCRATCH = {
     "w_query": ((D, D), BF),
@@ -913,6 +924,13 @@
     "w_up": ((D, FF), BF),
     "w_down": ((FF, D), BF),
     "cot": ((ROWS, D), BF),
+    "groups": ((2, ROWS), jnp.int32),
+    "gain_one": ((1, D), F32),
+    "shift_one": ((1, D), F32),
+    "gain_two": ((1, D), F32),
+    "shift_two": ((1, D), F32),
+    "last_grad": ((ROWS, D), BF),
+    "vec": ((8, D), F32),
     "hid": ((3, ROWS, D), BF),
     "q_out": ((2, 8, 64, 128), BF),
     "q_in": ((2, 16, 64, 128), BF),
@@ -972,23 +990,25 @@
         f"sum_s0{g}": ((3, rows // 4, 128), BF),
         f"sum_t{g}": ((2, 3, rows, 128), BF),
     }
-SEMS = {"sems": (12, 2), "gsems": (4,), "load_sems": (8,), "kv_sems": (2, 4), "plane_sems": (2, 8), "sum_sems0": (2, 8, 3), "sum_sems1": (2, 8, 3), "vsems": (3, 4)}
+SEMS = {"sems": (12, 2), "gsems": (4,), "load_sems": (13,), "out_sems": (3,), "kv_sems": (2, 4), "plane_sems": (2, 8), "sum_sems0": (2, 8, 3), "sum_sems1": (2, 8, 3), "vsems": (3, 4)}
 
 
 def kernel(*refs):
     names = INPUTS + list(OUTPUTS) + list(SCRATCH) + list(SEMS)
     r = SimpleNamespace(**dict(zip(names, refs)))
     place = Place()
-    for name in LOADED:
+    for name in LOADED[:5]:
         load(name, r, place).start()
     greet(place)
+    for name in LOADED[5:]:
+        load(name, r, place).start()
     r.vec_own[...] = jnp.zeros_like(r.vec_own)
 
     @pl.loop(0, 2)
     def _(v):
         @pl.when(v == 0)
         def _():
-            for name in LOADED[:4]:
+            for name in LOADED[:5]:
                 load(name, r, place).wait()
 
         project_queries(v, r)
@@ -1015,13 +1035,18 @@
 
         @pl.when(v == 0)
         def _():
-            for name in LOADED[4:7]:
+            for name in LOADED[5:12]:
                 load(name, r, place).wait()
 
         wait_all(r.o_in.at[v], r.sems.at[5, v])
         after_attention(v, r)
 
-    r.output[0] = r.hid[2]
+    finals = [
+        pltpu.make_async_copy(r.hid.at[2], r.output.at[0], r.out_sems.at[0]),
+        pltpu.make_async_copy(r.last_grad, r.input_grad.at[0], r.out_sems.at[1]),
+        pltpu.make_async_copy(r.vec, r.vec_hbm, r.out_sems.at[2]),
+    ]
+    finals[0].start()
     load("cot", r, place).wait()
     r.dy[...] = r.cot[...].astype(F32)
 
@@ -1060,10 +1085,14 @@
 
     weight_grads_late(r)
     SUM_STEPS[0](1, r, place)
-    r.input_grad[0] = input_gradient(0, r)
+    r.last_grad[...] = input_gradient(0, r)
+    finals[1].start()
     for g, step in SUM_TAIL:
         SUM_STEPS[step](g, r, place)
 
+    finals[2].start()
+    for copy in finals:
+        copy.wait()
     vec_drain(r)
     for g in range(2):
         sum_drain(g, r, place)
@@ -1125,7 +1154,9 @@
                 for k in range(4):
                     down_f[512 * k : 512 * k + 512, cols[j - 7]] = tiles[k]
                 if j == 10:
-                    store(7, down_f, down)
+                    for k in range(4):
+                        rows = pl.ds(512 * k, 512)
+                        store(7 + k, down_f.at[rows], down.at[rows])
         get_vec.wait()
         for i in range(4):
             vec_out[i, 0] = vec_in[i]
@@ -1161,17 +1192,12 @@
 
 def on_device(inputs, groups, cotangent, *params):
     vectors = [x.reshape(1, D) for x in params[6:]]
-    vmem = pl.BlockSpec(memory_space=pltpu.VMEM)
+    hbm = pl.BlockSpec(memory_space=pl.ANY)
     out = pl.pallas_call(
         kernel,
         out_shape=[jax.ShapeDtypeStruct(shape, kind) for shape, kind in OUTPUTS.values()],
-        in_specs=[
-            pl.BlockSpec(memory_space=pl.ANY) if n.endswith("_hbm") or n in ("inputs", "cotangent") else vmem
-            for n in INPUTS
-        ],
-        out_specs=[
-            pl.BlockSpec(memory_space=pl.ANY) if n.startswith("sums") else vmem for n in OUTPUTS
-        ],
+        in_specs=[hbm] * len(INPUTS),
+        out_specs=[hbm] * len(OUTPUTS),
         scratch_shapes=[pltpu.VMEM(shape, kind) for shape, kind in SCRATCH.values()]
         + [pltpu.SemaphoreType.DMA(shape) for shape in SEMS.values()],
         compiler_params=pltpu.CompilerParams(

time: 223 us -> 217 us (0.973)
  Pallas kernels: 222 us -> 217 us
    pallas_call x1, Pallas kernels: 213 us -> 207 us  [on_device(): pl.pallas_call(kernel, out_shape=[jax.ShapeDtypeStruct(shape, kind) for s...]
where the time goes in v6:
time: 217 us
  Pallas kernels  217 us (100%)
    pallas_call x1, Pallas kernels, on_device(): pl.pallas_call(kernel, out_shape=[jax.ShapeDtypeStruct(shape, kind) for s...  207 us
    pallas_call x1, Pallas kernels, unpack(): pl.pallas_call(body, out_shape=shapes + [jax.ShapeDtypeStruct((D,), F32)]...  9.37 us

profile of v6, /device:TPU:1, one launch (start us, length us, event | category | flops | bytes accessed | tf_op | source)
XLA Modules:
  0.0 217.4 jit_solution(11581247514849688829)
XLA Ops:
  0.6 207.2 %visits.1 = (bf16[1,128,512]{2,1,0:T(8,128)(2,1)}, bf16[1,128,512]{2,1,0:T(8,128)(2,1)}, bf16[2,3,3072,128]{3,2,1,0:T(8,128)(2,1)}, bf16[2,3,1024,128]{3,2,1,0:T(8,128)(2,1)}, f32[8,512]{1,0:T(8,128)}) custom-call(bf16[2,128,512]{2,1,0:T(8,128)(2,1)} %refs_0_.1, s32[2,128]{1,0:T(2,128)} %refs_1_.1, bf16[2,128,512]{2,1,0:T(8,128)(2,1)} %refs_2_.1, ...), custom_call_target="tpu_custom_call" | custom-call | tf_op jit(solution)/shard_map/visits/pallas_call | solution.py:1196
  207.9 9.4 %unpack.1 = (bf16[1,128,512]{2,1,0:T(8,128)(2,1)}, bf16[1,128,512]{2,1,0:T(8,128)(2,1)}, f32[512,512]{1,0:T(8,128)}, f32[512,512]{1,0:T(8,128)}, f32[512,512]{1,...) custom-call(bf16[1,128,512]{2,1,0:T(8,128)(2,1)} %get-tuple-element., ...), custom_call_target="tpu_custom_call" | custom-call | tf_op jit(solution)/shard_map/unpack/pallas_call | solution.py:1173

commit v7 on v6

--- a/solution.py
+++ b/solution.py
@@ -903,7 +903,7 @@
 )
 SUM_DURING_BACK = ((7, 2),)
 SUM_AFTER_BACK = (3,)
-SUM_TAIL = ((1, 1), (0, 4), (1, 2), (1, 3), (0, 5), (1, 4), (0, 6), (1, 5), (1, 6))
+SUM_TAIL = ((1, 1), (1, 2), (0, 4), (1, 3), (1, 4), (0, 5), (1, 5), (0, 6), (1, 6))
 
 
 WEIGHTS = ["w_query", "w_key", "w_value", "w_out", "w_up", "w_down"]
@@ -1062,11 +1062,12 @@
             SUM_STEPS[0](0, r, place)
 
         prepare_back(v, r)
-        wait_all(r.do_in.at[v], r.sems.at[7, v])
 
         @pl.when(v == 0)
         def _():
             SUM_STEPS[1](0, r, place)
+
+        wait_all(r.do_in.at[v], r.sems.at[7, v])
 
         attention_back(v, r, place)
 

time: 217 us -> 212 us (0.977)
  Pallas kernels: 217 us -> 211 us
    pallas_call x1, Pallas kernels: 207 us -> 201 us  [on_device(): pl.pallas_call(kernel, out_shape=[jax.ShapeDtypeStruct(shape, kind) for s...]
where the time goes in v7:
time: 212 us
  Pallas kernels  211 us (100%)
    pallas_call x1, Pallas kernels, on_device(): pl.pallas_call(kernel, out_shape=[jax.ShapeDtypeStruct(shape, kind) for s...  201 us
    pallas_call x1, Pallas kernels, unpack(): pl.pallas_call(body, out_shape=shapes + [jax.ShapeDtypeStruct((D,), F32)]...  9.37 us

profile of v7, /device:TPU:1, one launch (start us, length us, event | category | flops | bytes accessed | tf_op | source)
XLA Modules:
  0.0 211.7 jit_solution(15826613348719240790)
XLA Ops:
  0.6 201.5 %visits.1 = (bf16[1,128,512]{2,1,0:T(8,128)(2,1)}, bf16[1,128,512]{2,1,0:T(8,128)(2,1)}, bf16[2,3,3072,128]{3,2,1,0:T(8,128)(2,1)}, bf16[2,3,1024,128]{3,2,1,0:T(8,128)(2,1)}, f32[8,512]{1,0:T(8,128)}) custom-call(bf16[2,128,512]{2,1,0:T(8,128)(2,1)} %refs_0_.1, s32[2,128]{1,0:T(2,128)} %refs_1_.1, bf16[2,128,512]{2,1,0:T(8,128)(2,1)} %refs_2_.1, ...), custom_call_target="tpu_custom_call" | custom-call | tf_op jit(solution)/shard_map/visits/pallas_call | solution.py:1197
  202.1 9.4 %unpack.1 = (bf16[1,128,512]{2,1,0:T(8,128)(2,1)}, bf16[1,128,512]{2,1,0:T(8,128)(2,1)}, f32[512,512]{1,0:T(8,128)}, f32[512,512]{1,0:T(8,128)}, f32[512,512]{1,...) custom-call(bf16[1,128,512]{2,1,0:T(8,128)(2,1)} %get-tuple-element., ...), custom_call_target="tpu_custom_call" | custom-call | tf_op jit(solution)/shard_map/unpack/pallas_call | solution.py:1174

commit v8 on v7

--- a/solution.py
+++ b/solution.py
@@ -1012,14 +1012,19 @@
                 load(name, r, place).wait()
 
         project_queries(v, r)
-        project_keys_values(v, r)
 
         @pl.when(v == 0)
         def _():
+            project_keys_values(v, r)
             all_here()
             send_groups(r, place)
 
         send_queries(v, r, place)
+
+        @pl.when(v == 1)
+        def _():
+            project_keys_values(v, r)
+
         send_keys_values(v, r, place)
         pass_on(v, r, place)
 

time: 212 us -> 214 us (level)
    pallas_call x1, Pallas kernels: 201 us -> 204 us  [on_device(): pl.pallas_call(kernel, out_shape=[jax.ShapeDtypeStruct(shape, kind) for s...]
where the time goes in v8:
time: 214 us
  Pallas kernels  213 us (100%)
    pallas_call x1, Pallas kernels, on_device(): pl.pallas_call(kernel, out_shape=[jax.ShapeDtypeStruct(shape, kind) for s...  204 us
    pallas_call x1, Pallas kernels, unpack(): pl.pallas_call(body, out_shape=shapes + [jax.ShapeDtypeStruct((D,), F32)]...  9.37 us

profile of v8, /device:TPU:1, one launch (start us, length us, event | category | flops | bytes accessed | tf_op | source)
XLA Modules:
  0.0 213.8 jit_solution(9533664212479395570)
XLA Ops:
  0.6 203.6 %visits.1 = (bf16[1,128,512]{2,1,0:T(8,128)(2,1)}, bf16[1,128,512]{2,1,0:T(8,128)(2,1)}, bf16[2,3,3072,128]{3,2,1,0:T(8,128)(2,1)}, bf16[2,3,1024,128]{3,2,1,0:T(8,128)(2,1)}, f32[8,512]{1,0:T(8,128)}) custom-call(bf16[2,128,512]{2,1,0:T(8,128)(2,1)} %refs_0_.1, s32[2,128]{1,0:T(2,128)} %refs_1_.1, bf16[2,128,512]{2,1,0:T(8,128)(2,1)} %refs_2_.1, ...), custom_call_target="tpu_custom_call" | custom-call | tf_op jit(solution)/shard_map/visits/pallas_call | solution.py:1202
  204.3 9.4 %unpack.1 = (bf16[1,128,512]{2,1,0:T(8,128)(2,1)}, bf16[1,128,512]{2,1,0:T(8,128)(2,1)}, f32[512,512]{1,0:T(8,128)}, f32[512,512]{1,0:T(8,128)}, f32[512,512]{1,...) custom-call(bf16[1,128,512]{2,1,0:T(8,128)(2,1)} %get-tuple-element., ...), custom_call_target="tpu_custom_call" | custom-call | tf_op jit(solution)/shard_map/unpack/pallas_call | solution.py:1179
